TPU v7x, 512 devices: a whole 4x4x16 slice. The times are simulated.
512 devices in a mesh: dp: 128 (over y, z, core), hg: 4 (over x).
Axes of the slice: x: 4, y: 4, z: 16, core: 2. Of those that a mesh axis runs over, the one named last changes fastest.
Arguments:
- queries: bfloat16 [128, 128, 576], P('dp', 'hg'), may hold values from -40 to 40
- latent_cache: bfloat16 [128, 512, 576], P('dp', 'hg'), may hold values from -8 to 8
- lengths: int32 [128], P('dp'), may hold values from 64 to 512, as said below
- residual: bfloat16 [2048, 3584], P('dp'), may hold values from -6 to 6
- partials: bfloat16 [4, 2048, 3584], P('hg', 'dp'), may hold values from -50 to 50
- norm_gain: float32 [3584], replicated, may hold values from 0.1 to 1.9
- router: bfloat16 [3584, 128], P(None, 'hg'), may hold values from -0.09375 to 0.09375
- expert_ids: int32 [2048, 8], P('dp'), may hold values from 0 to 127, all different within a row; in each aligned block of 16 rows (0 to 15, 16 to 31, ...) at most 2 rows name the same one
- up_proj: bfloat16 [128, 3584, 1024], P('dp', None, 'hg'), may hold values from -0.09375 to 0.09375
- down_proj: bfloat16 [128, 1024, 3584], P('dp', 'hg'), may hold values from -0.1875 to 0.1875
Outputs:
- attended: bfloat16 [128, 128, 512], P('dp', 'hg')
- layer_out: bfloat16 [2048, 3584], P('dp', 'hg')
Inputs may be any that keep to these rules, and one draw needn't show every extreme that they name: `expert_ids`: each row names 8 different experts. Among the 16 rows of one dp index no expert is named more than 2 times, a bound that some block reaches. `lengths`: positions at or past a row's length are not attended. Some row has length 512 and some row has length 64.
All inputs are finite; a program needn't handle non-finite values.
Results may differ from a plain program's by a relative error of at most 0.015.
Values may be sent and summed in bfloat16 or wider, within the bound.
No kernel may reach another device: no remote copies, remote signals or barrier semaphores. Data moves between devices by JAX's collectives and lax.ppermute only.
A program may use at most 64 MiB of HBM per device.

v0:
```python
import jax
import jax.numpy as jnp
from jax import lax
from jax.sharding import PartitionSpec as P

LATENT = 512


SOFTMAX_SCALE = 192.0 ** (-0.5)
ROUTE_SCALE = 2.5
NORM_EPS = 1e-06


def attention(queries, latent_cache, lengths):
    whole_cache = lax.all_gather(latent_cache, "hg", axis=1, tiled=True)
    positions = jnp.arange(whole_cache.shape[1], dtype=jnp.int32)
    scores = (
        jnp.einsum("rhc,rpc->rhp", queries, whole_cache, preferred_element_type=jnp.float32)
        * SOFTMAX_SCALE
    )
    in_range = positions[None, :] < lengths[:, None]
    scores = jnp.where(in_range[:, None, :], scores, -jnp.inf)
    largest = jnp.max(scores, axis=2, keepdims=True)
    weights = jnp.exp(scores - largest)
    probabilities = (weights / jnp.sum(weights, axis=2, keepdims=True)).astype(jnp.bfloat16)
    combined = jnp.einsum(
        "rhp,rpc->rhc",
        probabilities,
        whole_cache[:, :, :LATENT],
        preferred_element_type=jnp.float32,
    )
    attended = combined.astype(jnp.bfloat16)
    return attended


def on_device(
    queries,
    latent_cache,
    lengths,
    residual,
    partials,
    norm_gain,
    router,
    expert_ids,
    up_proj,
    down_proj,
):
    attended = attention(queries, latent_cache, lengths)
    row_count = residual.shape[0]
    feature_width = residual.shape[1]
    top_count = expert_ids.shape[1]
    experts = lax.axis_size("dp") * up_proj.shape[0]
    capacity = min(row_count, max(2, 2 * row_count * top_count // experts))
    slice_width = feature_width // lax.axis_size("hg")
    summed = lax.psum(partials[0].astype(jnp.float32).astype(jnp.bfloat16), "hg").astype(
        jnp.float32
    )
    hidden = residual.astype(jnp.float32) + summed
    mean_square = jnp.mean(hidden * hidden, axis=1, keepdims=True)
    normed = (hidden * lax.rsqrt(mean_square + NORM_EPS) * norm_gain).astype(jnp.bfloat16)
    local_logits = jnp.dot(normed, router, preferred_element_type=jnp.float32)
    logits = lax.all_gather(local_logits, "hg", axis=1, tiled=True)
    numbers = jnp.arange(experts, dtype=jnp.int32)
    picker = expert_ids[:, :, None] == numbers[None, None, :]
    chosen = jnp.sum(jnp.where(picker, logits[:, None, :], 0.0), axis=2)
    affinity = jax.nn.sigmoid(chosen)
    gate_values = (ROUTE_SCALE * affinity / jnp.sum(affinity, axis=1, keepdims=True)).astype(
        jnp.bfloat16
    )
    flat_ids = expert_ids.reshape(-1)
    onehot = (flat_ids[:, None] == numbers[None, :]).astype(jnp.int32)
    slot_index = jnp.sum((jnp.cumsum(onehot, axis=0) - onehot) * onehot, axis=1).reshape(
        row_count, top_count
    )
    target = slot_index * experts + expert_ids
    slot_lanes = jnp.arange(experts * capacity, dtype=jnp.int32)
    slot_hits = target[:, :, None] == slot_lanes[None, None, :]
    route_matrix = jnp.any(slot_hits, axis=1).astype(jnp.bfloat16)
    gate_matrix = jnp.sum(
        jnp.where(slot_hits, gate_values[:, :, None].astype(jnp.float32), 0.0), axis=1
    ).astype(jnp.bfloat16)
    outgoing = jnp.einsum("te,td->ed", route_matrix, normed, preferred_element_type=jnp.float32)
    outgoing = outgoing.astype(jnp.bfloat16).reshape(capacity, experts, feature_width)
    arrived = lax.all_to_all(outgoing, "dp", split_axis=1, concat_axis=1, tiled=True)
    flat_rows = arrived.reshape(arrived.shape[0] * arrived.shape[1], feature_width)
    up_values = jnp.dot(flat_rows, up_proj[0], preferred_element_type=jnp.float32)
    arrived_shape = arrived.shape
    activated = jax.nn.silu(up_values).astype(jnp.bfloat16)
    expert_part = jnp.dot(activated, down_proj[0], preferred_element_type=jnp.float32).astype(
        jnp.bfloat16
    )
    expert_out = expert_part.reshape(arrived_shape[0], arrived_shape[1], feature_width)
    reduced = lax.psum_scatter(
        expert_out.astype(jnp.float32).astype(jnp.bfloat16), "hg", scatter_dimension=2, tiled=True
    ).astype(jnp.float32)
    returned = lax.all_to_all(
        reduced.astype(jnp.bfloat16), "dp", split_axis=1, concat_axis=1, tiled=True
    ).astype(reduced.dtype)
    routed_sum = jnp.dot(
        gate_matrix.astype(jnp.float32),
        returned.reshape(experts * capacity, slice_width),
        precision=lax.Precision.HIGHEST,
    )
    hidden_slice = lax.dynamic_slice_in_dim(
        hidden, lax.axis_index("hg") * slice_width, slice_width, 1
    )
    layer_out = (hidden_slice + routed_sum).astype(jnp.bfloat16)
    return (attended, layer_out)


def solution(mesh):
    return jax.shard_map(
        on_device,
        mesh=mesh,
        in_specs=(
            P("dp", "hg", None),
            P("dp", "hg", None),
            P("dp"),
            P("dp", None),
            P("hg", "dp", None),
            P(),
            P(None, "hg"),
            P("dp", None),
            P("dp", None, "hg"),
            P("dp", "hg", None),
        ),
        out_specs=(P("dp", "hg", None), P("dp", "hg")),
        check_vma=False,
    )
```

profile of v0, /device:TPU:1, one launch (start us, length us, event | category | flops | bytes accessed | tf_op | source)
XLA Modules:
  0.0 282.3 jit_solution(14561414655814285275)
XLA Ops:
  7.2 0.7 all-reduce.2.cloned.1.call-update
  8.0 0.8 copy.42
  8.9 0.2 reduce_window_sum.11
  9.5 60.2 %all-reduce.2.cloned.1.call-done = bf16[16,3584]{1,0:T(8,128)(2,1)} async-done(((bf16[16,3584]{1,0:T(8,128)(2,1)}), bf16[16,3584]{1,0:T(8,128)(2,1)}) %all-reduce.2.cloned.1.call-update) | async-done | bytes 114704 | tf_op jit(solution)/shard_map/psum | solution.py:55
  69.7 1.1 convert_add_fusion
  70.8 1.7 convolution_convert_fusion.1
  72.5 1.9 copy.48
  74.4 106.3 %all_to_all.10 = bf16[2,128,3584]{2,0,1:T(2,128)(2,1)S(1)} all-to-all(bf16[2,128,3584]{2,0,1:T(2,128)(2,1)S(1)} %copy.48), channel_id=1, replica_groups=mesh['dp'=128,'hg'=4] {'dp'}, dimensions={1} | all-to-all | bytes 3670016 | tf_op jit(solution)/shard_map/all_to_all | solution.py:84
  180.7 1.4 copy.49
  182.1 5.4 %convolution_convert_fusion = bf16[256,3584]{1,0:T(8,128)(2,1)} fusion(bf16[1,256,3584]{2,1,0:T(8,128)(2,1)S(1)} %copy-done, bf16[256,3584]{1,0:T(8,128)(2,1)} %bitcast.50, bf16[1,3584,256]{2,1,0:T(8,128)(2,1)} %param.18), kind=kOutput, calls=%fused_computation | convolution fusion | flops 940769280 | bytes 7340032 | tf_op jit(solution)/shard_map/dot_general | solution.py:89
  187.5 5.5 %copy.52 = bf16[2,128,3584]{1,0,2:T(2,128)(2,1)} copy(bf16[2,128,3584]{2,1,0:T(8,128)(2,1)} %bitcast.51) | data formatting | bytes 3670016
  193.0 3.0 %copy.57 = bf16[448,8,2,128]{3,1,2,0:T(8,128)(2,1)} copy(bf16[448,8,2,128]{3,2,1,0:T(2,128)(2,1)} %bitcast.54) | data formatting | bytes 3670016
  196.1 27.9 %reduce-scatter.4.cloned.1.call-done = bf16[896,256]{1,0:T(8,128)(2,1)} async-done(((bf16[3584,256]{1,0:T(8,128)(2,1)}), bf16[896,256]{1,0:T(8,128)(2,1)}) %reduce-scatter.4.cloned.1.call-update) | async-done | bytes 458768
  224.0 1.1 reshape.109
  225.1 2.3 copy.50
  227.4 16.8 %all-to-all-start.1 = ((bf16[2,128,896]{2,0,1:T(2,128)(2,1)}), bf16[2,128,896]{2,0,1:T(2,128)(2,1)S(1)}, u32[]{:S(2)}, u32[]{:S(2)}) async-start(bf16[2,128,896]{2,0,1:T(2,128)(2,1)} %copy.50), calls=%async_computation.1 | async-start | bytes 917504 | tf_op jit(solution)/shard_map/all_to_all | solution.py:96
  244.8 12.6 %all_gather.6 = bf16[1,512,576]{1,2,0:T(8,128)(2,1)S(1)} all-gather(bf16[1,128,576]{1,2,0:T(8,128)(2,1)S(1)} %copy-done.4), channel_id=1, replica_groups=mesh['dp'=128,'hg'=4] {'hg'}, dimensions={1}, use_global_device_ids=true | all-gather | bytes 737280 | tf_op jit(solution)/shard_map/all_gather | solution.py:15
  257.5 0.3 fusion.22
  257.8 0.2 fusion.14
  258.0 0.9 fusion.5
  258.9 0.2 convolution_bitcast_fusion
  259.1 9.8 %all-gather = f32[4,32,16]{1,2,0:T(8,128)S(1)} all-gather(f32[1,32,16]{1,2,0:T(8,128)S(1)} %convolution_bitcast_fusion), channel_id=1, replica_groups=mesh['dp'=128,'hg'=4] {'hg'}, dimensions={0}, use_global_device_ids=true | all-gather | bytes 10240 | tf_op jit(solution)/shard_map/all_gather | solution.py:62
  269.5 5.1 %all-to-all-done.1 = bf16[2,128,896]{2,0,1:T(2,128)(2,1)S(1)} async-done(((bf16[2,128,896]{2,0,1:T(2,128)(2,1)}), bf16[2,128,896]{2,0,1:T(2,128)(2,1)S(1)}, u32[]{:S(2)}, u32[]{:S(2)}) %all-to-all-start.1) | async-done | bytes 458784 | tf_op jit(solution)/shard_map/all_to_all | solution.py:96
  274.7 0.8 fusion.4
  (35 shorter events, 1.3 us)
Async XLA Ops:
  7.2 174.9 %copy-start = (bf16[1,256,3584]{2,1,0:T(8,128)(2,1)S(1)}, bf16[1,256,3584]{2,1,0:T(8,128)(2,1)}, u32[]{:S(2)}) copy-start(bf16[1,256,3584]{2,1,0:T(8,128)(2,1)} %param.19) | copy-start | bytes 5505028
  7.2 62.5 %all-reduce.2.cloned.1.call-start = ((), (), s32[]{:S(2)}) async-start(), calls=%async_computation.3 | async-start | bytes 229376 | tf_op jit(solution)/shard_map/psum | solution.py:55
  7.9 216.1 %reduce-scatter.4.cloned.1.call-start = ((), (), s32[]{:S(2)}) async-start(), calls=%async_computation.4 | async-start | bytes 2293760
  196.0 48.8 %copy-start.4 = (bf16[1,128,576]{1,2,0:T(8,128)(2,1)S(1)}, bf16[1,128,576]{1,2,0:T(8,128)(2,1)}, u32[]{:S(2)}) copy-start(bf16[1,128,576]{1,2,0:T(8,128)(2,1)} %param.11) | copy-start | bytes 442372
  196.0 61.4 %copy-start.6 = (bf16[1,32,576]{2,1,0:T(8,128)(2,1)S(1)}, bf16[1,32,576]{2,1,0:T(8,128)(2,1)}, u32[]{:S(2)}) copy-start(bf16[1,32,576]{2,1,0:T(8,128)(2,1)} %param.10) | copy-start | bytes 110596
  227.4 31.5 %copy-start.1 = (bf16[16,3584]{1,0:T(8,128)(2,1)S(1)}, bf16[16,3584]{1,0:T(8,128)(2,1)}, u32[]{:S(2)}) copy-start(bf16[16,3584]{1,0:T(8,128)(2,1)} %param.13) | copy-start | bytes 344068
  227.4 31.5 %copy-start.2 = (bf16[16,3584]{1,0:T(8,128)(2,1)S(1)}, bf16[16,3584]{1,0:T(8,128)(2,1)}, u32[]{:S(2)}) copy-start(bf16[16,3584]{1,0:T(8,128)(2,1)} %all-reduce.2.cloned.1.call-done) | copy-start | bytes 344068
  227.4 31.5 %copy-start.3 = (bf16[3584,32]{0,1:T(8,128)(2,1)S(1)}, bf16[3584,32]{0,1:T(8,128)(2,1)}, u32[]{:S(2)}) copy-start(bf16[3584,32]{0,1:T(8,128)(2,1)} %param.16) | copy-start | bytes 688132
  227.4 31.5 %copy-start.5 = (f32[3584]{0:T(1024)S(1)}, f32[3584]{0:T(1024)}, u32[]{:S(2)}) copy-start(f32[3584]{0:T(1024)} %param.15) | copy-start | bytes 43012
  227.4 47.2 %all-to-all-start.1 = ((bf16[2,128,896]{2,0,1:T(2,128)(2,1)}), bf16[2,128,896]{2,0,1:T(2,128)(2,1)S(1)}, u32[]{:S(2)}, u32[]{:S(2)}) async-start(bf16[2,128,896]{2,0,1:T(2,128)(2,1)} %copy.50), calls=%async_computation.1 | async-start | bytes 917504 | tf_op jit(solution)/shard_map/all_to_all | solution.py:96
Sparse Core Ops, SparseCore 0:
  10.3 59.3 all-reduce.1
  196.2 27.7 reduce-scatter.3
where the time goes:
time: 283 us; the launch traced here: 282 us
  blocking collectives  129 us (46%)
  waiting for transfers between devices  93.9 us (33%)
  starting transfers between devices  16.8 us (6%)
  local copies, waits for them, and re-layouts  16.5 us (6%)
  between operations  14.8 us (5%)
  matrix products  9.34 us (3%)
    all_to_all x1, blocking collectives, on_device(): lax.all_to_all(outgoing, 'dp', split_axis=1, concat_axis=1, tiled=True)  106 us
    psum x1, waiting for transfers between devices, on_device(): lax.psum(partials[0].astype(jnp.float32).astype(jnp.bfloat16), 'hg')  60.2 us
    unnamed x3, waiting for transfers between devices  28.6 us
    all_to_all x1, starting transfers between devices, on_device(): lax.all_to_all(reduced.astype(jnp.bfloat16), 'dp', split_axis=1, concat_a...  16.8 us
    all_gather x1, blocking collectives, attention(): whole_cache = lax.all_gather(latent_cache, 'hg', axis=1, tiled=True)  12.6 us
    unnamed x19, local copies, waits for them, and re-layouts  10.5 us
    all_gather x1, blocking collectives, on_device(): logits = lax.all_gather(local_logits, 'hg', axis=1, tiled=True)  9.78 us
  transfers between devices with their start and end apart: 3, of which 3 were waited for; matrix products, arithmetic and copies ran while one was open for 1% of the time, Pallas kernels for 0%

commit v1 on v0

v1 whole, which is shorter than its diff:
```python
import jax
import jax.numpy as jnp
from jax import lax
from jax.experimental import pallas as pl
from jax.experimental.pallas import tpu as pltpu
from jax.sharding import PartitionSpec as P

LATENT = 512
SOFTMAX_SCALE = 192.0 ** (-0.5)
ROUTE_SCALE = 2.5
NORM_EPS = 1e-06


def shift(value, distance, size):
    return lax.ppermute(value, "hg", [(i, (i + distance) % size) for i in range(size)])


def spread(value, size):
    return lax.all_to_all(jnp.broadcast_to(value[None], (size,) + value.shape), "hg", 0, 0, tiled=True)


def spread_ready(value):
    return lax.all_to_all(value, "hg", 0, 0, tiled=True)


def attention(queries, latent_cache, lengths):
    size = lax.axis_size("hg")
    me = lax.axis_index("hg")
    width = latent_cache.shape[1]
    blocks = [latent_cache] + [shift(latent_cache, d, size) for d in range(1, size)]
    whole_cache = jnp.concatenate(blocks, axis=1)
    places = jnp.arange(size * width, dtype=jnp.int32)
    owner = (me - places // width + size) % size
    positions = owner * width + places % width
    scores = (
        jnp.einsum("rhc,rpc->rhp", queries, whole_cache, preferred_element_type=jnp.float32)
        * SOFTMAX_SCALE
    )
    in_range = positions[None, :] < lengths[:, None]
    scores = jnp.where(in_range[:, None, :], scores, -jnp.inf)
    largest = jnp.max(scores, axis=2, keepdims=True)
    weights = jnp.exp(scores - largest)
    probabilities = (weights / jnp.sum(weights, axis=2, keepdims=True)).astype(jnp.bfloat16)
    combined = jnp.einsum(
        "rhp,rpc->rhc",
        probabilities,
        whole_cache[:, :, :LATENT],
        preferred_element_type=jnp.float32,
    )
    return combined.astype(jnp.bfloat16)


def column_blocks(weights, size):
    depth, width = weights.shape
    part = width // size

    def kernel(weights_ref, *outs):
        me = lax.axis_index("hg")
        for d in range(size):
            start = pl.multiple_of(lax.rem(me + d, size) * part, 128)
            outs[d][...] = weights_ref[:, pl.ds(start, part)]

    return pl.pallas_call(
        kernel,
        out_shape=[jax.ShapeDtypeStruct((depth, part), weights.dtype)] * size,
        cost_estimate=pl.CostEstimate(flops=0, bytes_accessed=4 * depth * width, transcendentals=0),
        compiler_params=pltpu.CompilerParams(vmem_limit_bytes=20 << 20),
        name="column_blocks",
    )(weights)


def expert_up(all_rows, weights, extra):
    size, slots, part = all_rows.shape
    units = weights.shape[1]
    more = extra.shape[0]

    def kernel(rows_ref, weights_ref, extra_ref, out_ref):
        total = jnp.zeros((slots, units), jnp.float32)
        for x in range(size):
            total += jnp.dot(
                rows_ref[x], weights_ref[x * part:(x + 1) * part, :],
                preferred_element_type=jnp.float32,
            )
        active = (total / (1.0 + jnp.exp(-total))).astype(jnp.bfloat16)
        for x in range(size):
            out_ref[x, :slots, :] = active
            out_ref[x, slots:, :] = extra_ref[...]

    return pl.pallas_call(
        kernel,
        out_shape=jax.ShapeDtypeStruct((size, slots + more, units), jnp.bfloat16),
        cost_estimate=pl.CostEstimate(
            flops=2 * slots * size * part * units,
            bytes_accessed=2 * (slots * size * part + size * part * units + size * slots * units),
            transcendentals=slots * units,
        ),
        compiler_params=pltpu.CompilerParams(vmem_limit_bytes=40 << 20),
        name="expert_up",
    )(all_rows, weights, extra)


def expert_down(active, blocks, slots):
    size, _, units = active.shape
    part = blocks[0].shape[1]

    def kernel(active_ref, *rest):
        blocks_ref, out_ref = rest[:size], rest[size]
        me = lax.axis_index("hg")
        total = jnp.zeros((slots, part), jnp.float32)
        for d in range(size):
            owner = lax.rem(me + size - d, size)
            total += jnp.dot(
                active_ref[owner, :slots, :], blocks_ref[d][...],
                preferred_element_type=jnp.float32,
            )
        out_ref[...] = total.astype(jnp.bfloat16)

    return pl.pallas_call(
        kernel,
        out_shape=jax.ShapeDtypeStruct((slots, part), jnp.bfloat16),
        cost_estimate=pl.CostEstimate(
            flops=2 * slots * size * part * units,
            bytes_accessed=2 * (slots * size * units + size * part * units + slots * part),
            transcendentals=0,
        ),
        compiler_params=pltpu.CompilerParams(vmem_limit_bytes=40 << 20),
        name="expert_down",
    )(active, *blocks)


def on_device(
    queries,
    latent_cache,
    lengths,
    residual,
    partials,
    norm_gain,
    router,
    expert_ids,
    up_proj,
    down_proj,
):
    size = lax.axis_size("hg")
    me = lax.axis_index("hg")
    row_count, feature_width = residual.shape
    top_count = expert_ids.shape[1]
    experts = lax.axis_size("dp") * up_proj.shape[0]
    capacity = min(row_count, max(2, 2 * row_count * top_count // experts))
    slice_width = feature_width // size
    unit_count = up_proj.shape[2]

    attended = attention(queries, latent_cache, lengths)

    hidden = residual.astype(jnp.float32) + jnp.sum(
        spread(partials[0], size).astype(jnp.float32), axis=0
    )
    mean_square = jnp.mean(hidden * hidden, axis=1, keepdims=True)
    normed = (hidden * lax.rsqrt(mean_square + NORM_EPS) * norm_gain).astype(jnp.bfloat16)

    numbers = jnp.arange(experts, dtype=jnp.int32)
    flat_ids = expert_ids.reshape(-1)
    onehot = (flat_ids[:, None] == numbers[None, :]).astype(jnp.int32)
    slot_index = jnp.sum((jnp.cumsum(onehot, axis=0) - onehot) * onehot, axis=1).reshape(
        row_count, top_count
    )
    target = expert_ids * capacity + slot_index
    slot_lanes = jnp.arange(experts * capacity, dtype=jnp.int32)
    slot_hits = target[:, :, None] == slot_lanes[None, None, :]
    route_matrix = jnp.any(slot_hits, axis=1).astype(jnp.bfloat16)

    normed_slice = lax.dynamic_slice_in_dim(normed, me * slice_width, slice_width, 1)
    outgoing = jnp.einsum(
        "te,td->ed", route_matrix, normed_slice, preferred_element_type=jnp.float32
    ).astype(jnp.bfloat16)
    outgoing = outgoing.reshape(experts, capacity, slice_width)
    down_own, *down_sent = column_blocks(down_proj[0], size)
    outgoing, *down_sent = lax.optimization_barrier((outgoing, *down_sent))
    arrived = lax.all_to_all(outgoing, "dp", split_axis=0, concat_axis=0, tiled=True)
    down_got = [shift(block, d + 1, size) for d, block in enumerate(down_sent)]
    local_logits = jnp.dot(normed, router, preferred_element_type=jnp.float32)
    high = local_logits.astype(jnp.bfloat16)
    low = (local_logits - high.astype(jnp.float32)).astype(jnp.bfloat16)
    local = experts // size
    extra = jnp.pad(
        jnp.concatenate([high, low], axis=1), ((0, 0), (0, unit_count - 2 * local))
    )
    arrived, extra, *down_got = lax.optimization_barrier((arrived, extra, *down_got))
    slots = experts * capacity
    rows = arrived.reshape(slots, slice_width)

    active = spread_ready(expert_up(spread(rows, size), up_proj[0], extra))
    reduced = expert_down(active, [down_own, *down_got], slots)
    returned = lax.all_to_all(
        reduced.reshape(experts, capacity, slice_width),
        "dp", split_axis=0, concat_axis=0, tiled=True,
    ).reshape(slots, slice_width)

    logit_parts = active[:, slots:, :2 * local].astype(jnp.float32)
    logits = (logit_parts[:, :, :local] + logit_parts[:, :, local:]).transpose(1, 0, 2).reshape(
        row_count, experts
    )
    picker = expert_ids[:, :, None] == numbers[None, None, :]
    chosen = jnp.sum(jnp.where(picker, logits[:, None, :], 0.0), axis=2)
    affinity = jax.nn.sigmoid(chosen)
    gate_values = (ROUTE_SCALE * affinity / jnp.sum(affinity, axis=1, keepdims=True)).astype(
        jnp.bfloat16
    )
    gate_matrix = jnp.sum(
        jnp.where(slot_hits, gate_values[:, :, None].astype(jnp.float32), 0.0), axis=1
    ).astype(jnp.bfloat16)
    routed_sum = jnp.dot(gate_matrix, returned, preferred_element_type=jnp.float32)
    hidden_slice = lax.dynamic_slice_in_dim(hidden, me * slice_width, slice_width, 1)
    layer_out = (hidden_slice + routed_sum).astype(jnp.bfloat16)
    return (attended, layer_out)


def solution(mesh):
    return jax.shard_map(
        on_device,
        mesh=mesh,
        in_specs=(
            P("dp", "hg", None),
            P("dp", "hg", None),
            P("dp"),
            P("dp", None),
            P("hg", "dp", None),
            P(),
            P(None, "hg"),
            P("dp", None),
            P("dp", None, "hg"),
            P("dp", "hg", None),
        ),
        out_specs=(P("dp", "hg", None), P("dp", "hg")),
        check_vma=False,
    )
```

time: 283 us -> 165 us (0.58)
  blocking collectives: 129 us -> 24.5 us
  starting transfers between devices: 16.8 us -> 68.4 us
  waiting for transfers between devices: 93.9 us -> 50.3 us
  between operations: 14.8 us -> 1.6 us
  local copies, waits for them, and re-layouts: 16.5 us -> 11.2 us
  matrix products: 9.34 us -> 4.23 us
    all_to_all x1, blocking collectives: 106 us -> 24.5 us  [spread(): lax.all_to_all(jnp.broadcast_to(value[None], (size,) + value.shape), 'hg'...]
    psum x1 -> x0, waiting for transfers between devices: 60.2 us -> none  [on_device(): lax.psum(partials[0].astype(jnp.float32).astype(jnp.bfloat16), 'hg')]
    all_to_all x1 -> x4, starting transfers between devices: 16.8 us -> 49.3 us  [the longest x1 22.6 us: on_device(): lax.all_to_all(outgoing, 'dp', split_axis=0, concat_axis=0, tiled=True)]
    unnamed x3 -> x0, waiting for transfers between devices: 28.6 us -> none
    all_to_all x1 -> x4, waiting for transfers between devices: 5.08 us -> 33 us  [the longest x1 26.3 us: on_device(): lax.all_to_all(reduced.reshape(experts, capacity, slice_width), 'dp', spl...]
    all_gather x2 -> x0, blocking collectives: 22.4 us -> none  [the longest x1 12.6 us: attention(): whole_cache = lax.all_gather(latent_cache, 'hg', axis=1, tiled=True)]
    ppermute x0 -> x6, starting transfers between devices: none -> 19.1 us  [shift(): lax.ppermute(value, 'hg', [(i, (i + distance) % size) for i in range(size)])]
    ppermute x0 -> x6, waiting for transfers between devices: none -> 17.3 us  [shift(): lax.ppermute(value, 'hg', [(i, (i + distance) % size) for i in range(size)])]
  transfers between devices with their start and end apart: 3 -> 10, of which waited for: 3 -> 6; matrix products, arithmetic and copies ran while one was open for 1% -> 5% of each run, Pallas kernels for 0% -> 1%
where the time goes in v1:
time: 165 us; the launch traced here: 164 us
  starting transfers between devices  68.4 us (41%)
  waiting for transfers between devices  50.3 us (30%)
  blocking collectives  24.5 us (15%)
  local copies, waits for them, and re-layouts  11.2 us (7%)
  matrix products  4.23 us (3%)
  Pallas kernels  2.39 us (1%)
    all_to_all x1, waiting for transfers between devices, on_device(): lax.all_to_all(reduced.reshape(experts, capacity, slice_width), 'dp', spl...  26.3 us
    all_to_all x1, blocking collectives, spread(): lax.all_to_all(jnp.broadcast_to(value[None], (size,) + value.shape), 'hg'...  24.5 us
    all_to_all x1, starting transfers between devices, on_device(): lax.all_to_all(outgoing, 'dp', split_axis=0, concat_axis=0, tiled=True)  22.6 us
    ppermute x6, starting transfers between devices, shift(): lax.ppermute(value, 'hg', [(i, (i + distance) % size) for i in range(size)])  19.1 us
    all_to_all x1, starting transfers between devices, on_device(): lax.all_to_all(reduced.reshape(experts, capacity, slice_width), 'dp', spl...  18.2 us
    ppermute x6, waiting for transfers between devices, shift(): lax.ppermute(value, 'hg', [(i, (i + distance) % size) for i in range(size)])  17.3 us
    unnamed x24, local copies, waits for them, and re-layouts  5.58 us
    all_to_all x1, starting transfers between devices, spread(): lax.all_to_all(jnp.broadcast_to(value[None], (size,) + value.shape), 'hg'...  4.97 us
  transfers between devices with their start and end apart: 10, of which 6 were waited for; matrix products, arithmetic and copies ran while one was open for 5% of the time, Pallas kernels for 1%

profile of v1, /device:TPU:1, one launch (start us, length us, event | category | flops | bytes accessed | tf_op | source)
XLA Modules:
  0.0 164.2 jit_solution(10092661516745646322)
XLA Ops:
  0.6 1.7 %broadcast_in_dim.69 = bf16[4,16,3584]{2,1,0:T(8,128)(2,1)} broadcast(bf16[16,3584]{1,0:T(8,128)(2,1)} %bitcast.29), dimensions={1,2} | broadcast | bytes 573440 | tf_op jit(solution)/shard_map/broadcast_in_dim | solution.py:19
  2.4 5.0 %all-to-all-start = ((bf16[4,16,3584]{2,1,0:T(8,128)(2,1)}), bf16[4,16,3584]{2,1,0:T(8,128)(2,1)S(1)}, u32[]{:S(2)}, u32[]{:S(2)}) async-start(bf16[4,16,3584]{2,1,0:T(8,128)(2,1)} %broadcast_in_dim.69), calls=%async_computation | async-start | bytes 917504 | tf_op jit(solution)/shard_map/all_to_all | solution.py:19
  8.8 1.5 copy-done.1
  10.5 3.4 %all-to-all-done = bf16[4,16,3584]{2,1,0:T(8,128)(2,1)S(1)} async-done(((bf16[4,16,3584]{2,1,0:T(8,128)(2,1)}), bf16[4,16,3584]{2,1,0:T(8,128)(2,1)S(1)}, u32[]{:S(2)}, u32[]{:S(2)}) %all-to-all-start) | async-done | bytes 458784 | tf_op jit(solution)/shard_map/all_to_all | solution.py:19
  15.3 1.0 reshape.133
  16.3 22.6 %all-to-all-start.1 = ((bf16[128,2,896]{2,1,0:T(2,128)(2,1)}), bf16[128,2,896]{2,1,0:T(2,128)(2,1)}, u32[]{:S(2)}, u32[]{:S(2)}) async-start(bf16[128,2,896]{2,1,0:T(2,128)(2,1)} %reshape.133), calls=%async_computation.1 | async-start | bytes 917504 | tf_op jit(solution)/shard_map/all_to_all | solution.py:178
  38.9 2.2 %collective-permute-start.3 = (bf16[256,896]{1,0:T(8,128)(2,1)S(1)}, bf16[256,896]{1,0:T(8,128)(2,1)S(1)}, u32[]{:S(2)}, u32[]{:S(2)}) collective-permute-start(bf16[256,896]{1,0:T(8,128)(2,1)S(1)} %get-tuple-element.19), channel_id=1, source_target_pairs={{0,1},{1,2},{2,3},{3,0},{4,5},{5,6},{6,7},{7,4},{8,9},{9,10},{10,1... | collective-permute-start | bytes 1376264 | tf_op jit(solution)/shard_map/ppermute | solution.py:15
  41.1 3.7 %collective-permute-start.4 = (bf16[256,896]{1,0:T(8,128)(2,1)S(1)}, bf16[256,896]{1,0:T(8,128)(2,1)S(1)}, u32[]{:S(2)}, u32[]{:S(2)}) collective-permute-start(bf16[256,896]{1,0:T(8,128)(2,1)S(1)} %get-tuple-element.20), channel_id=1, source_target_pairs={{0,2},{1,3},{2,0},{3,1},{4,6},{5,7},{6,4},{7,5},{8,10},{9,11},{10,... | collective-permute-start | bytes 1376264 | tf_op jit(solution)/shard_map/ppermute | solution.py:15
  44.8 2.5 %collective-permute-start.5 = (bf16[256,896]{1,0:T(8,128)(2,1)S(1)}, bf16[256,896]{1,0:T(8,128)(2,1)S(1)}, u32[]{:S(2)}, u32[]{:S(2)}) collective-permute-start(bf16[256,896]{1,0:T(8,128)(2,1)S(1)} %get-tuple-element.21), channel_id=1, source_target_pairs={{0,3},{1,0},{2,1},{3,2},{4,7},{5,4},{6,5},{7,6},{8,11},{9,8},{10,9... | collective-permute-start | bytes 1376264 | tf_op jit(solution)/shard_map/ppermute | solution.py:15
  47.3 1.1 subtract_convert_fusion
  48.5 5.3 %collective-permute-done.3.rest_1_ = bf16[256,896]{1,0:T(8,128)(2,1)S(1)} collective-permute-done((bf16[256,896]{1,0:T(8,128)(2,1)S(1)}, bf16[256,896]{1,0:T(8,128)(2,1)S(1)}, u32[]{:S(2)}, u32[]{:S(2)}) %collective-permute-start.3) | collective-permute-done | bytes 458784 | tf_op jit(solution)/shard_map/ppermute | solution.py:15
  53.8 8.7 %collective-permute-done.4.rest_2_ = bf16[256,896]{1,0:T(8,128)(2,1)S(1)} collective-permute-done((bf16[256,896]{1,0:T(8,128)(2,1)S(1)}, bf16[256,896]{1,0:T(8,128)(2,1)S(1)}, u32[]{:S(2)}, u32[]{:S(2)}) %collective-permute-start.4) | collective-permute-done | bytes 458784 | tf_op jit(solution)/shard_map/ppermute | solution.py:15
  62.4 3.3 %collective-permute-done.5.rest_3_ = bf16[256,896]{1,0:T(8,128)(2,1)S(1)} collective-permute-done((bf16[256,896]{1,0:T(8,128)(2,1)S(1)}, bf16[256,896]{1,0:T(8,128)(2,1)S(1)}, u32[]{:S(2)}, u32[]{:S(2)}) %collective-permute-start.5) | collective-permute-done | bytes 458784 | tf_op jit(solution)/shard_map/ppermute | solution.py:15
  65.7 3.3 %all-to-all-done.1 = bf16[128,2,896]{2,1,0:T(2,128)(2,1)} async-done(((bf16[128,2,896]{2,1,0:T(2,128)(2,1)}), bf16[128,2,896]{2,1,0:T(2,128)(2,1)}, u32[]{:S(2)}, u32[]{:S(2)}) %all-to-all-start.1) | async-done | bytes 458784 | tf_op jit(solution)/shard_map/all_to_all | solution.py:178
  69.0 1.2 broadcast_in_dim.70
  70.4 24.5 %all_to_all.25.rows_ref = bf16[4,256,896]{2,1,0:T(8,128)(2,1)S(1)} all-to-all(bf16[4,256,896]{2,1,0:T(8,128)(2,1)S(1)} %broadcast_in_dim.71), channel_id=1, replica_groups=mesh['dp'=128,'hg'=4] {'hg'}, dimensions={0} | all-to-all | bytes 3670016 | tf_op jit(solution)/shard_map/all_to_all | solution.py:19
  94.9 1.5 expert_up.1
  96.4 3.5 %all-to-all-start.3 = ((bf16[4,272,256]{2,1,0:T(8,128)(2,1)}), bf16[4,272,256]{2,1,0:T(8,128)(2,1)S(1)}, u32[]{:S(2)}, u32[]{:S(2)}) async-start(bf16[4,272,256]{2,1,0:T(8,128)(2,1)} %expert_up.1), calls=%async_computation.3 | async-start | bytes 1114112 | tf_op jit(solution)/shard_map/all_to_all | solution.py:23
  99.9 3.3 %collective-permute-start = (bf16[1,128,576]{1,2,0:T(8,128)(2,1)S(1)}, bf16[1,128,576]{1,2,0:T(8,128)(2,1)}, u32[]{:S(2)}, u32[]{:S(2)}) collective-permute-start(bf16[1,128,576]{1,2,0:T(8,128)(2,1)S(1)} %copy-done.6), channel_id=1, source_target_pairs={{0,1},{1,2},{2,3},{3,0},{4,5},{5,6},{6,7},{7,4},{8,9},{9,10},{10,1... | collective-permute-start | bytes 442376 | tf_op jit(solution)/shard_map/ppermute | solution.py:15
  103.2 4.3 %collective-permute-start.1 = (bf16[1,128,576]{1,2,0:T(8,128)(2,1)S(1)}, bf16[1,128,576]{1,2,0:T(8,128)(2,1)}, u32[]{:S(2)}, u32[]{:S(2)}) collective-permute-start(bf16[1,128,576]{1,2,0:T(8,128)(2,1)S(1)} %copy-done.6), channel_id=1, source_target_pairs={{0,2},{1,3},{2,0},{3,1},{4,6},{5,7},{6,4},{7,5},{8,10},{9,11},{10,... | collective-permute-start | bytes 442376 | tf_op jit(solution)/shard_map/ppermute | solution.py:15
  107.5 3.1 %collective-permute-start.2 = (bf16[1,128,576]{1,2,0:T(8,128)(2,1)S(1)}, bf16[1,128,576]{1,2,0:T(8,128)(2,1)S(1)}, u32[]{:S(2)}, u32[]{:S(2)}) collective-permute-start(bf16[1,128,576]{1,2,0:T(8,128)(2,1)S(1)} %copy-done.6), channel_id=1, source_target_pairs={{0,3},{1,0},{2,1},{3,2},{4,7},{5,4},{6,5},{7,6},{8,11},{9,8},{10,9... | collective-permute-start | bytes 442376 | tf_op jit(solution)/shard_map/ppermute | solution.py:15
  113.7 18.2 %all-to-all-start.4 = ((bf16[128,2,896]{2,1,0:T(2,128)(2,1)}), bf16[128,2,896]{2,1,0:T(2,128)(2,1)S(1)}, u32[]{:S(2)}, u32[]{:S(2)}) async-start(bf16[128,2,896]{2,1,0:T(2,128)(2,1)} %reshape.134), calls=%async_computation.4 | async-start | bytes 917504 | tf_op jit(solution)/shard_map/all_to_all | solution.py:193
  136.1 26.3 %all-to-all-done.4 = bf16[128,2,896]{2,1,0:T(2,128)(2,1)S(1)} async-done(((bf16[128,2,896]{2,1,0:T(2,128)(2,1)}), bf16[128,2,896]{2,1,0:T(2,128)(2,1)S(1)}, u32[]{:S(2)}, u32[]{:S(2)}) %all-to-all-start.4) | async-done | bytes 458784 | tf_op jit(solution)/shard_map/all_to_all | solution.py:193
  162.6 1.6 fusion.1
  (60 shorter events, 9.8 us)
Async XLA Ops:
  0.6 46.7 %copy-start = (bf16[3584,32]{0,1:T(8,128)(2,1)S(1)}, bf16[3584,32]{0,1:T(8,128)(2,1)}, u32[]{:S(2)}) copy-start(bf16[3584,32]{0,1:T(8,128)(2,1)} %param.16) | copy-start | bytes 688132
  2.4 11.6 %copy-start.7 = (bf16[16,3584]{1,0:T(8,128)(2,1)S(1)}, bf16[16,3584]{1,0:T(8,128)(2,1)}, u32[]{:S(2)}) copy-start(bf16[16,3584]{1,0:T(8,128)(2,1)} %param.13) | copy-start | bytes 344068
  2.4 11.6 %all-to-all-start = ((bf16[4,16,3584]{2,1,0:T(8,128)(2,1)}), bf16[4,16,3584]{2,1,0:T(8,128)(2,1)S(1)}, u32[]{:S(2)}, u32[]{:S(2)}) async-start(bf16[4,16,3584]{2,1,0:T(8,128)(2,1)} %broadcast_in_dim.69), calls=%async_computation | async-start | bytes 917504 | tf_op jit(solution)/shard_map/all_to_all | solution.py:19
  7.4 7.5 %copy-start.9 = (f32[3584]{0:T(1024)S(1)}, f32[3584]{0:T(1024)}, u32[]{:S(2)}) copy-start(f32[3584]{0:T(1024)} %param.15) | copy-start | bytes 43012
  8.8 1.5 copy-start.1
  14.2 0.7 copy-start.3
  14.9 23.9 %copy-start.5 = (bf16[16,3584]{1,0:T(8,128)(2,1)}, bf16[16,3584]{1,0:T(8,128)(2,1)S(1)}, u32[]{:S(2)}) copy-start(bf16[16,3584]{1,0:T(8,128)(2,1)S(1)} %multiply_convert_fusion) | copy-start | bytes 344068
  16.3 52.8 %all-to-all-start.1 = ((bf16[128,2,896]{2,1,0:T(2,128)(2,1)}), bf16[128,2,896]{2,1,0:T(2,128)(2,1)}, u32[]{:S(2)}, u32[]{:S(2)}) async-start(bf16[128,2,896]{2,1,0:T(2,128)(2,1)} %reshape.133), calls=%async_computation.1 | async-start | bytes 917504 | tf_op jit(solution)/shard_map/all_to_all | solution.py:178
  38.9 14.9 %collective-permute-start.3 = (bf16[256,896]{1,0:T(8,128)(2,1)S(1)}, bf16[256,896]{1,0:T(8,128)(2,1)S(1)}, u32[]{:S(2)}, u32[]{:S(2)}) collective-permute-start(bf16[256,896]{1,0:T(8,128)(2,1)S(1)} %get-tuple-element.19), channel_id=1, source_target_pairs={{0,1},{1,2},{2,3},{3,0},{4,5},{5,6},{6,7},{7,4},{8,9},{9,10},{10,1... | collective-permute-start | bytes 1376264 | tf_op jit(solution)/shard_map/ppermute | solution.py:15
  41.1 21.3 %collective-permute-start.4 = (bf16[256,896]{1,0:T(8,128)(2,1)S(1)}, bf16[256,896]{1,0:T(8,128)(2,1)S(1)}, u32[]{:S(2)}, u32[]{:S(2)}) collective-permute-start(bf16[256,896]{1,0:T(8,128)(2,1)S(1)} %get-tuple-element.20), channel_id=1, source_target_pairs={{0,2},{1,3},{2,0},{3,1},{4,6},{5,7},{6,4},{7,5},{8,10},{9,11},{10,... | collective-permute-start | bytes 1376264 | tf_op jit(solution)/shard_map/ppermute | solution.py:15
  44.8 20.9 %collective-permute-start.5 = (bf16[256,896]{1,0:T(8,128)(2,1)S(1)}, bf16[256,896]{1,0:T(8,128)(2,1)S(1)}, u32[]{:S(2)}, u32[]{:S(2)}) collective-permute-start(bf16[256,896]{1,0:T(8,128)(2,1)S(1)} %get-tuple-element.21), channel_id=1, source_target_pairs={{0,3},{1,0},{2,1},{3,2},{4,7},{5,4},{6,5},{7,6},{8,11},{9,8},{10,9... | collective-permute-start | bytes 1376264 | tf_op jit(solution)/shard_map/ppermute | solution.py:15
  70.4 24.5 %copy-start.2 = (bf16[1,3584,256]{2,1,0:T(8,128)(2,1)S(1)}, bf16[1,3584,256]{2,1,0:T(8,128)(2,1)}, u32[]{:S(2)}) copy-start(bf16[1,3584,256]{2,1,0:T(8,128)(2,1)} %param.18) | copy-start | bytes 5505028
  94.9 5.0 %copy-start.6 = (bf16[1,128,576]{1,2,0:T(8,128)(2,1)S(1)}, bf16[1,128,576]{1,2,0:T(8,128)(2,1)}, u32[]{:S(2)}) copy-start(bf16[1,128,576]{1,2,0:T(8,128)(2,1)} %param.11) | copy-start | bytes 442372
  96.4 15.6 %all-to-all-start.3 = ((bf16[4,272,256]{2,1,0:T(8,128)(2,1)}), bf16[4,272,256]{2,1,0:T(8,128)(2,1)S(1)}, u32[]{:S(2)}, u32[]{:S(2)}) async-start(bf16[4,272,256]{2,1,0:T(8,128)(2,1)} %expert_up.1), calls=%async_computation.3 | async-start | bytes 1114112 | tf_op jit(solution)/shard_map/all_to_all | solution.py:23
  99.9 32.1 %collective-permute-start = (bf16[1,128,576]{1,2,0:T(8,128)(2,1)S(1)}, bf16[1,128,576]{1,2,0:T(8,128)(2,1)}, u32[]{:S(2)}, u32[]{:S(2)}) collective-permute-start(bf16[1,128,576]{1,2,0:T(8,128)(2,1)S(1)} %copy-done.6), channel_id=1, source_target_pairs={{0,1},{1,2},{2,3},{3,0},{4,5},{5,6},{6,7},{7,4},{8,9},{9,10},{10,1... | collective-permute-start | bytes 442376 | tf_op jit(solution)/shard_map/ppermute | solution.py:15
  103.2 29.7 %collective-permute-start.1 = (bf16[1,128,576]{1,2,0:T(8,128)(2,1)S(1)}, bf16[1,128,576]{1,2,0:T(8,128)(2,1)}, u32[]{:S(2)}, u32[]{:S(2)}) collective-permute-start(bf16[1,128,576]{1,2,0:T(8,128)(2,1)S(1)} %copy-done.6), channel_id=1, source_target_pairs={{0,2},{1,3},{2,0},{3,1},{4,6},{5,7},{6,4},{7,5},{8,10},{9,11},{10,... | collective-permute-start | bytes 442376 | tf_op jit(solution)/shard_map/ppermute | solution.py:15
  107.5 26.3 %collective-permute-start.2 = (bf16[1,128,576]{1,2,0:T(8,128)(2,1)S(1)}, bf16[1,128,576]{1,2,0:T(8,128)(2,1)S(1)}, u32[]{:S(2)}, u32[]{:S(2)}) collective-permute-start(bf16[1,128,576]{1,2,0:T(8,128)(2,1)S(1)} %copy-done.6), channel_id=1, source_target_pairs={{0,3},{1,0},{2,1},{3,2},{4,7},{5,4},{6,5},{7,6},{8,11},{9,8},{10,9... | collective-permute-start | bytes 442376 | tf_op jit(solution)/shard_map/ppermute | solution.py:15
  112.7 19.2 %copy-start.4 = (bf16[1,512,576]{1,2,0:T(8,128)(2,1)S(1)}, bf16[1,512,576]{1,2,0:T(8,128)(2,1)}, u32[]{:S(2)}) copy-start(bf16[1,512,576]{1,2,0:T(8,128)(2,1)} %constant_dynamic-update-slice_fusion.3) | copy-start | bytes 1769476
  112.7 21.2 %copy-start.8 = (bf16[1,32,576]{2,1,0:T(8,128)(2,1)S(1)}, bf16[1,32,576]{2,1,0:T(8,128)(2,1)}, u32[]{:S(2)}) copy-start(bf16[1,32,576]{2,1,0:T(8,128)(2,1)} %param.10) | copy-start | bytes 110596
  113.7 48.7 %all-to-all-start.4 = ((bf16[128,2,896]{2,1,0:T(2,128)(2,1)}), bf16[128,2,896]{2,1,0:T(2,128)(2,1)S(1)}, u32[]{:S(2)}, u32[]{:S(2)}) async-start(bf16[128,2,896]{2,1,0:T(2,128)(2,1)} %reshape.134), calls=%async_computation.4 | async-start | bytes 917504 | tf_op jit(solution)/shard_map/all_to_all | solution.py:193

commit v2 on v1

v2 whole, which is shorter than its diff:
```python
import jax
import jax.numpy as jnp
from jax import lax
from jax.experimental import pallas as pl
from jax.experimental.pallas import tpu as pltpu
from jax.sharding import PartitionSpec as P

LATENT = 512
SOFTMAX_SCALE = 192.0 ** (-0.5)
ROUTE_SCALE = 2.5
NORM_EPS = 1e-06
VMEM_LIMIT = 16 << 20
WHOLE_VMEM = 60 << 20


def shift(value, distance, size):
    return lax.ppermute(value, "hg", [(i, (i + distance) % size) for i in range(size)])


def spread(value, size):
    return lax.all_to_all(jnp.broadcast_to(value[None], (size,) + value.shape), "hg", 0, 0, tiled=True)


def exchange(value):
    return lax.all_to_all(value, "hg", 0, 0, tiled=True)


def attention(queries, latent_cache, lengths):
    size = lax.axis_size("hg")
    me = lax.axis_index("hg")
    width = latent_cache.shape[1]
    blocks = [latent_cache] + [shift(latent_cache, d, size) for d in range(1, size)]
    whole_cache = jnp.concatenate(blocks, axis=1)
    places = jnp.arange(size * width, dtype=jnp.int32)
    owner = (me - places // width + size) % size
    positions = owner * width + places % width
    scores = (
        jnp.einsum("rhc,rpc->rhp", queries, whole_cache, preferred_element_type=jnp.float32)
        * SOFTMAX_SCALE
    )
    in_range = positions[None, :] < lengths[:, None]
    scores = jnp.where(in_range[:, None, :], scores, -jnp.inf)
    largest = jnp.max(scores, axis=2, keepdims=True)
    weights = jnp.exp(scores - largest)
    probabilities = (weights / jnp.sum(weights, axis=2, keepdims=True)).astype(jnp.bfloat16)
    combined = jnp.einsum(
        "rhp,rpc->rhc",
        probabilities,
        whole_cache[:, :, :LATENT],
        preferred_element_type=jnp.float32,
    )
    return combined.astype(jnp.bfloat16)


HBM = pl.BlockSpec(memory_space=pltpu.HBM)
VMEM = pl.BlockSpec(memory_space=pltpu.VMEM)


def start_all(pairs, sems, first=0):
    copies = [
        pltpu.make_async_copy(source, target, sems.at[first + i])
        for i, (source, target) in enumerate(pairs)
    ]
    for copy in copies:
        copy.start()
    return copies


def wait_all(copies):
    for copy in copies:
        copy.wait()


def place(d, size, width):
    return pl.multiple_of(lax.rem(lax.axis_index("hg") + d, size) * width, 128)


def pack_weights(up_weights, down_weights, earlier, size):
    features, units = up_weights.shape
    part = features // size
    half = units // 2
    chunks = part // 128
    block = 2 * part
    assert units == 256 and size == 4 and part % 128 == 0 and block == chunks * units
    turns = (1, 3, 2)

    def kernel(up_hbm, down_hbm, earlier_ref, next_hbm, back_hbm, up_ref, down_ref, next_ref, back_ref, sems):
        ups = start_all(
            [(up_hbm.at[pl.ds(place(d, size, part), part), :], up_ref.at[i]) for i, d in enumerate(turns)], sems
        )
        downs = start_all(
            [(down_hbm.at[:, pl.ds(place(d, size, part), part)], down_ref.at[i]) for i, d in enumerate(turns)], sems, 3
        )
        outs = []
        for i, (to_ref, to_hbm) in enumerate(((next_ref, next_hbm), (back_ref, back_hbm))):
            ups[i].wait()
            to_ref[:part, :] = up_ref[i, :, :half]
            to_ref[part:block, :] = up_ref[i, :, half:]
            downs[i].wait()
            for k in range(chunks):
                to_ref[block + k * units:block + (k + 1) * units, :] = down_ref[i, :, k * 128:(k + 1) * 128]
            outs += start_all(
                [(to_ref.at[:2 * block, :], to_hbm.at[:2 * block, :])], sems, 6 + 2 * i
            )
        ups[2].wait()
        downs[2].wait()
        for i, (to_ref, to_hbm) in enumerate(((next_ref, next_hbm), (back_ref, back_hbm))):
            first = 2 * block
            to_ref[first:first + part, :] = up_ref[2, :, i * half:(i + 1) * half]
            first += part
            for k in range(chunks):
                to_ref[first + k * half:first + (k + 1) * half, :] = down_ref[
                    2, i * half:(i + 1) * half, k * 128:(k + 1) * 128
                ]
            outs += start_all(
                [(to_ref.at[2 * block:, :], to_hbm.at[2 * block:, :])], sems, 7 + 2 * i
            )
        wait_all(outs)

    sent = pltpu.HBM((3 * block, 128), up_weights.dtype)
    return pl.pallas_call(
        kernel,
        out_shape=[sent, sent],
        in_specs=[HBM, HBM, pl.BlockSpec(memory_space=pl.ANY)],
        out_specs=[HBM, HBM],
        scratch_shapes=[
            pltpu.VMEM((3, part, units), up_weights.dtype),
            pltpu.VMEM((3, units, part), up_weights.dtype),
            pltpu.VMEM((3 * block, 128), up_weights.dtype),
            pltpu.VMEM((3 * block, 128), up_weights.dtype),
            pltpu.SemaphoreType.DMA((10,)),
        ],
        cost_estimate=pl.CostEstimate(
            flops=0, bytes_accessed=8 * features * units, transcendentals=0
        ),
        compiler_params=pltpu.CompilerParams(vmem_limit_bytes=WHOLE_VMEM),
        name="pack_weights",
    )(up_weights, down_weights, earlier)


def own_blocks(up_weights, down_weights, earlier, size):
    features, units = up_weights.shape
    part = features // size

    def kernel(up_hbm, down_hbm, earlier_ref, own_up_hbm, own_down_hbm, up_ref, down_ref, sems):
        wait_all(start_all(
            [
                (up_hbm.at[pl.ds(place(0, size, part), part), :], up_ref),
                (down_hbm.at[:, pl.ds(place(0, size, part), part)], down_ref),
            ],
            sems,
        ))
        wait_all(start_all([(up_ref, own_up_hbm), (down_ref, own_down_hbm)], sems, 2))

    dtype = up_weights.dtype
    return pl.pallas_call(
        kernel,
        out_shape=[pltpu.HBM((part, units), dtype), pltpu.HBM((units, part), dtype)],
        in_specs=[HBM, HBM, pl.BlockSpec(memory_space=pl.ANY)],
        out_specs=[HBM, HBM],
        scratch_shapes=[
            pltpu.VMEM((part, units), dtype),
            pltpu.VMEM((units, part), dtype),
            pltpu.SemaphoreType.DMA((4,)),
        ],
        compiler_params=pltpu.CompilerParams(vmem_limit_bytes=WHOLE_VMEM),
        name="own_blocks",
    )(up_weights, down_weights, earlier)


def join_weights(own_up, own_down, after, before, far_low, far_high):
    part, units = own_up.shape
    half = units // 2
    chunks = part // 128
    block = 2 * part

    def kernel(own_up_ref, own_down_ref, after_ref, before_ref, low_ref, high_ref, up_ref, down_ref):
        up_ref[:, :units] = own_up_ref[...]
        up_ref[:, units:units + half] = after_ref[:part, :]
        up_ref[:, units + half:2 * units] = after_ref[part:block, :]
        up_ref[:, 2 * units:2 * units + half] = low_ref[:part, :]
        up_ref[:, 2 * units + half:3 * units] = high_ref[:part, :]
        up_ref[:, 3 * units:3 * units + half] = before_ref[:part, :]
        up_ref[:, 3 * units + half:] = before_ref[part:block, :]
        down_ref[:units, :] = own_down_ref[...]
        for k in range(chunks):
            lanes = slice(k * 128, (k + 1) * 128)
            whole = slice(block + k * units, block + (k + 1) * units)
            some = slice(part + k * half, part + (k + 1) * half)
            down_ref[units:2 * units, lanes] = after_ref[whole, :]
            down_ref[2 * units:2 * units + half, lanes] = low_ref[some, :]
            down_ref[2 * units + half:3 * units, lanes] = high_ref[some, :]
            down_ref[3 * units:, lanes] = before_ref[whole, :]

    return pl.pallas_call(
        kernel,
        out_shape=[
            jax.ShapeDtypeStruct((part, 4 * units), own_up.dtype),
            jax.ShapeDtypeStruct((4 * units, part), own_up.dtype),
        ],
        cost_estimate=pl.CostEstimate(
            flops=0, bytes_accessed=32 * part * units, transcendentals=0
        ),
        compiler_params=pltpu.CompilerParams(vmem_limit_bytes=VMEM_LIMIT),
        name="join_weights",
    )(own_up, own_down, after, before, far_low, far_high)


def norm_and_route(copies, residual, gain, choices, experts, capacity):
    size, rows, features = copies.shape
    part = features // size
    slots = experts * capacity
    top = choices.shape[0]

    def kernel(
        copies_ref, residual_hbm, gain_hbm, choices_hbm, normed_hbm, hidden_hbm, route_hbm, out_hbm,
        residual_ref, gain_ref, choices_ref, hidden_ref, normed_ref, route_ref, out_ref, sems,
    ):
        fetched = start_all(
            [(choices_hbm, choices_ref), (residual_hbm, residual_ref), (gain_hbm, gain_ref)], sems, 4
        )
        fetched[0].wait()
        expert = lax.div(lax.broadcasted_iota(jnp.int32, (slots, rows), 0), capacity)
        slot = lax.broadcasted_iota(jnp.int32, (slots, rows), 0) - expert * capacity
        hits = jnp.zeros((slots, rows), jnp.float32)
        for k in range(top):
            hits += jnp.where(choices_ref[k:k + 1, :] == expert, 1.0, 0.0)
        above = lax.broadcasted_iota(jnp.int32, (rows, rows), 0) < lax.broadcasted_iota(
            jnp.int32, (rows, rows), 1
        )
        earlier = jnp.dot(
            hits.astype(jnp.bfloat16), jnp.where(above, 1.0, 0.0).astype(jnp.bfloat16),
            preferred_element_type=jnp.float32,
        )
        route = jnp.where(earlier == slot.astype(jnp.float32), hits, 0.0).astype(jnp.bfloat16)
        route_ref[...] = route

        wait_all(fetched[1:])
        hidden = residual_ref[...].astype(jnp.float32)
        for x in range(size):
            hidden += copies_ref[x].astype(jnp.float32)
        hidden_ref[...] = hidden
        scale = lax.rsqrt(jnp.mean(hidden * hidden, axis=1, keepdims=True) + NORM_EPS)
        normed_ref[...] = (hidden * scale * gain_ref[...][None, :]).astype(jnp.bfloat16)
        mine = pl.ds(place(0, size, part), part)
        out_ref[...] = jnp.dot(
            route, normed_ref[:, mine], preferred_element_type=jnp.float32
        ).astype(jnp.bfloat16).reshape(experts, capacity, part)
        wait_all(start_all(
            [
                (out_ref, out_hbm),
                (normed_ref, normed_hbm),
                (hidden_ref.at[:, mine], hidden_hbm),
                (route_ref, route_hbm),
            ],
            sems,
        ))

    shapes = [
        ((rows, features), jnp.bfloat16),
        ((rows, part), jnp.float32),
        ((slots, rows), jnp.bfloat16),
        ((experts, capacity, part), jnp.bfloat16),
    ]
    return pl.pallas_call(
        kernel,
        out_shape=[pltpu.HBM(*shape) for shape in shapes],
        in_specs=[VMEM, HBM, HBM, HBM],
        out_specs=[HBM] * 4,
        scratch_shapes=[
            pltpu.VMEM(residual.shape, residual.dtype),
            pltpu.VMEM(gain.shape, gain.dtype),
            pltpu.VMEM(choices.shape, choices.dtype),
            pltpu.VMEM((rows, features), jnp.float32),
            pltpu.VMEM((rows, features), jnp.bfloat16),
            pltpu.VMEM((slots, rows), jnp.bfloat16),
            pltpu.VMEM((experts, capacity, part), jnp.bfloat16),
            pltpu.SemaphoreType.DMA((7,)),
        ],
        cost_estimate=pl.CostEstimate(
            flops=2 * slots * rows * part,
            bytes_accessed=2 * (size + 2) * rows * features + 2 * slots * part,
            transcendentals=0,
        ),
        compiler_params=pltpu.CompilerParams(vmem_limit_bytes=VMEM_LIMIT),
        name="norm_and_route",
    )(copies, residual, gain, choices)


def gates(logit_parts, route, experts, capacity):
    size, rows, lanes = logit_parts.shape
    slots = experts * capacity
    local = experts // size

    def kernel(parts_ref, route_ref, out_ref):
        expert = lax.div(lax.broadcasted_iota(jnp.int32, (slots, lanes), 0), capacity)
        lane = lax.broadcasted_iota(jnp.int32, (slots, lanes), 1)
        column = jnp.where(lane < local, lane, lane - local)
        logits = jnp.zeros((slots, rows), jnp.float32)
        for x in range(size):
            pick = (column + x * local == expert) & (lane < 2 * local)
            logits += lax.dot_general(
                jnp.where(pick, 1.0, 0.0).astype(jnp.bfloat16), parts_ref[x],
                (((1,), (1,)), ((), ())), preferred_element_type=jnp.float32,
            )
        affinity = route_ref[...].astype(jnp.float32) / (1.0 + jnp.exp(-logits))
        total = jnp.sum(affinity, axis=0, keepdims=True)
        out_ref[...] = (ROUTE_SCALE * affinity / total).astype(jnp.bfloat16)

    return pl.pallas_call(
        kernel,
        out_shape=jax.ShapeDtypeStruct((slots, rows), jnp.bfloat16),
        name="gates",
    )(logit_parts, route)


def combine(gate_matrix, returned, hidden):
    experts, capacity, part = returned.shape
    slots = experts * capacity

    def kernel(gates_hbm, returned_ref, hidden_hbm, out_ref, gates_ref, hidden_ref, sems):
        copies = start_all([(gates_hbm, gates_ref), (hidden_hbm, hidden_ref)], sems)
        wait_all(copies)
        routed = lax.dot_general(
            gates_ref[...], returned_ref[...].reshape(slots, part), (((0,), (0,)), ((), ())),
            preferred_element_type=jnp.float32,
        )
        out_ref[...] = (hidden_ref[...] + routed).astype(jnp.bfloat16)

    return pl.pallas_call(
        kernel,
        out_shape=jax.ShapeDtypeStruct(hidden.shape, jnp.bfloat16),
        in_specs=[HBM, VMEM, HBM],
        scratch_shapes=[
            pltpu.VMEM(gate_matrix.shape, gate_matrix.dtype),
            pltpu.VMEM(hidden.shape, hidden.dtype),
            pltpu.SemaphoreType.DMA((2,)),
        ],
        compiler_params=pltpu.CompilerParams(vmem_limit_bytes=VMEM_LIMIT),
        name="combine",
    )(gate_matrix, returned, hidden)


def expert_up(arrived, weights):
    size = lax.axis_size("hg")
    experts, capacity, part = arrived.shape
    slots = experts * capacity
    units = weights.shape[1] // size

    def kernel(rows_ref, weights_ref, out_ref):
        me = lax.axis_index("hg")
        rows = rows_ref[...].reshape(slots, part)
        for d in range(size):
            owner = lax.rem(me + size - d, size)
            out_ref[owner] = jnp.dot(
                rows, weights_ref[:, d * units:(d + 1) * units],
                preferred_element_type=jnp.float32,
            ).astype(jnp.bfloat16)

    return pl.pallas_call(
        kernel,
        out_shape=jax.ShapeDtypeStruct((size, slots, units), jnp.bfloat16),
        cost_estimate=pl.CostEstimate(
            flops=2 * slots * size * part * units,
            bytes_accessed=2 * (slots * part + size * part * units + size * slots * units),
            transcendentals=0,
        ),
        compiler_params=pltpu.CompilerParams(vmem_limit_bytes=VMEM_LIMIT),
        name="expert_up",
    )(arrived, weights)


def expert_silu(shares, extra):
    size, slots, units = shares.shape
    more = extra.shape[0]

    def kernel(shares_hbm, extra_hbm, out_hbm, shares_ref, active_ref, sems):
        copies = start_all(
            [(shares_hbm.at[x], shares_ref.at[x]) for x in range(size)]
            + [(extra_hbm, active_ref.at[slots:, :])],
            sems,
        )
        total = jnp.zeros((slots, units), jnp.float32)
        for x in range(size):
            copies[x].wait()
            total += shares_ref[x].astype(jnp.float32)
        active_ref[:slots, :] = (total / (1.0 + jnp.exp(-total))).astype(jnp.bfloat16)
        copies[size].wait()
        wait_all(start_all([(active_ref, out_hbm.at[x]) for x in range(size)], sems, size + 1))

    return pl.pallas_call(
        kernel,
        out_shape=pltpu.HBM((size, slots + more, units), jnp.bfloat16),
        in_specs=[pl.BlockSpec(memory_space=pl.ANY)] * 2,
        out_specs=HBM,
        scratch_shapes=[
            pltpu.VMEM((size, slots, units), jnp.bfloat16),
            pltpu.VMEM((slots + more, units), jnp.bfloat16),
            pltpu.SemaphoreType.DMA((2 * size + 1,)),
        ],
        cost_estimate=pl.CostEstimate(
            flops=8 * slots * units,
            bytes_accessed=4 * size * slots * units,
            transcendentals=slots * units,
        ),
        compiler_params=pltpu.CompilerParams(vmem_limit_bytes=VMEM_LIMIT),
        name="expert_silu",
    )(shares, extra)


def expert_down(active, weights, experts, capacity):
    size, _, units = active.shape
    part = weights.shape[1]
    slots = experts * capacity

    def kernel(active_ref, weights_ref, out_ref):
        me = lax.axis_index("hg")
        total = jnp.zeros((slots, part), jnp.float32)
        for d in range(size):
            owner = lax.rem(me + size - d, size)
            total += jnp.dot(
                active_ref[owner, :slots, :], weights_ref[d * units:(d + 1) * units, :],
                preferred_element_type=jnp.float32,
            )
        out_ref[...] = total.astype(jnp.bfloat16).reshape(experts, capacity, part)

    return pl.pallas_call(
        kernel,
        out_shape=jax.ShapeDtypeStruct((experts, capacity, part), jnp.bfloat16),
        cost_estimate=pl.CostEstimate(
            flops=2 * slots * size * part * units,
            bytes_accessed=2 * (slots * size * units + size * part * units + slots * part),
            transcendentals=0,
        ),
        compiler_params=pltpu.CompilerParams(vmem_limit_bytes=VMEM_LIMIT),
        name="expert_down",
    )(active, weights)


def on_device(
    queries,
    latent_cache,
    lengths,
    residual,
    partials,
    norm_gain,
    router,
    expert_ids,
    up_proj,
    down_proj,
):
    size = lax.axis_size("hg")
    row_count, feature_width = residual.shape
    top_count = expert_ids.shape[1]
    experts = lax.axis_size("dp") * up_proj.shape[0]
    capacity = min(row_count, max(2, 2 * row_count * top_count // experts))
    unit_count = up_proj.shape[2]
    slots = experts * capacity

    copies = jnp.broadcast_to(partials[0][None], (size,) + partials.shape[1:])
    to_next, to_back = pack_weights(up_proj[0], down_proj[0], copies, size)
    after, before = shift(to_next, 1, size), shift(to_back, size - 1, size)
    far = 4 * (feature_width // size)
    far_low, far_high = shift(after[far:], 1, size), shift(before[far:], size - 1, size)

    normed, hidden, route, outgoing = norm_and_route(
        exchange(copies), residual, norm_gain, expert_ids.T, experts, capacity
    )
    arrived = lax.all_to_all(outgoing, "dp", split_axis=0, concat_axis=0, tiled=True)

    local_logits = jnp.dot(normed, router, preferred_element_type=jnp.float32)
    high = local_logits.astype(jnp.bfloat16)
    low = (local_logits - high.astype(jnp.float32)).astype(jnp.bfloat16)
    extra = jnp.pad(
        jnp.concatenate([high, low], axis=1), ((0, 0), (0, unit_count - 2 * high.shape[1]))
    )
    own_up, own_down = own_blocks(up_proj[0], down_proj[0], normed, size)
    up_all, down_all = join_weights(own_up, own_down, after, before, far_low, far_high)
    arrived, extra, up_all, down_all = lax.optimization_barrier((arrived, extra, up_all, down_all))

    shares = exchange(expert_up(arrived, up_all))
    active = exchange(expert_silu(shares, extra))
    reduced = expert_down(active, down_all, experts, capacity)
    reduced, latent_cache = lax.optimization_barrier((reduced, latent_cache))
    returned = lax.all_to_all(reduced, "dp", split_axis=0, concat_axis=0, tiled=True)
    attended = attention(queries, latent_cache, lengths)
    gate_matrix = gates(active[:, slots:], route, experts, capacity)
    layer_out = combine(gate_matrix, returned, hidden)
    return (attended, layer_out)


def solution(mesh):
    return jax.shard_map(
        on_device,
        mesh=mesh,
        in_specs=(
            P("dp", "hg", None),
            P("dp", "hg", None),
            P("dp"),
            P("dp", None),
            P("hg", "dp", None),
            P(),
            P(None, "hg"),
            P("dp", None),
            P("dp", None, "hg"),
            P("dp", "hg", None),
        ),
        out_specs=(P("dp", "hg", None), P("dp", "hg")),
        check_vma=False,
    )
```

time: 165 us -> 152 us (0.921)
  waiting for transfers between devices: 50.3 us -> 30.7 us
  Pallas kernels: 2.39 us -> 15.6 us
  blocking collectives: 24.5 us -> 21.5 us
  matrix products: 4.23 us -> 1.38 us
    all_to_all x3 -> x2, waiting for transfers between devices: 29.8 us -> 14.7 us  [the longest x1 14.7 us: on_device(): lax.all_to_all(reduced, 'dp', split_axis=0, concat_axis=0, tiled=True)]
    pallas_call x3 -> x9, Pallas kernels: 2.39 us -> 15.6 us  [the longest x1 3.15 us: pack_weights(): pl.pallas_call(kernel, out_shape=[sent, sent], in_specs=[HBM, HBM, pl.Blo...]
    ppermute x6 -> x7, waiting for transfers between devices: 17.3 us -> 9.7 us  [shift(): lax.ppermute(value, 'hg', [(i, (i + distance) % size) for i in range(size)])]
    all_to_all x1, waiting for transfers between devices: 3.29 us -> 6.35 us  [on_device(): lax.all_to_all(outgoing, 'dp', split_axis=0, concat_axis=0, tiled=True)]
    all_to_all x1 -> x2, blocking collectives: 24.5 us -> 21.5 us  [exchange(): return lax.all_to_all(value, 'hg', 0, 0, tiled=True)]
    ppermute x6 -> x7, starting transfers between devices: 19.1 us -> 21.6 us  [shift(): lax.ppermute(value, 'hg', [(i, (i + distance) % size) for i in range(size)])]
    slice x0 -> x3, local copies, waits for them, and re-layouts: none -> 2.24 us  [the longest x1 0.82 us: on_device(): after[far:]]
    reshape x4 -> x0, local copies, waits for them, and re-layouts: 2.15 us -> none  [the longest x1 0.96 us: on_device(): outgoing = outgoing.reshape(experts, capacity, slice_width)]
  transfers between devices with their start and end apart: 10 -> 10, of which waited for: 6 -> 6; matrix products, arithmetic and copies ran while one was open for 5% -> 3% of each run, Pallas kernels for 1% -> 7%
where the time goes in v2:
time: 152 us; the launch traced here: 151 us
  starting transfers between devices  68.3 us (45%)
  waiting for transfers between devices  30.7 us (20%)
  blocking collectives  21.5 us (14%)
  Pallas kernels  15.6 us (10%)
  local copies, waits for them, and re-layouts  11.5 us (8%)
  between operations  1.55 us (1%)
    ppermute x7, starting transfers between devices, shift(): lax.ppermute(value, 'hg', [(i, (i + distance) % size) for i in range(size)])  21.6 us
    all_to_all x2, blocking collectives, exchange(): return lax.all_to_all(value, 'hg', 0, 0, tiled=True)  21.5 us
    all_to_all x1, starting transfers between devices, on_device(): lax.all_to_all(reduced, 'dp', split_axis=0, concat_axis=0, tiled=True)  21.3 us
    all_to_all x1, starting transfers between devices, on_device(): lax.all_to_all(outgoing, 'dp', split_axis=0, concat_axis=0, tiled=True)  20.6 us
    all_to_all x1, waiting for transfers between devices, on_device(): lax.all_to_all(reduced, 'dp', split_axis=0, concat_axis=0, tiled=True)  14.7 us
    ppermute x7, waiting for transfers between devices, shift(): lax.ppermute(value, 'hg', [(i, (i + distance) % size) for i in range(size)])  9.7 us
    unnamed x33, local copies, waits for them, and re-layouts  7.53 us
    all_to_all x1, waiting for transfers between devices, on_device(): lax.all_to_all(outgoing, 'dp', split_axis=0, concat_axis=0, tiled=True)  6.35 us
  transfers between devices with their start and end apart: 10, of which 6 were waited for; matrix products, arithmetic and copies ran while one was open for 3% of the time, Pallas kernels for 7%

profile of v2, /device:TPU:1, one launch (start us, length us, event | category | flops | bytes accessed | tf_op | source)
XLA Modules:
  0.0 150.9 jit_solution(8801013246605878889)
XLA Ops:
  0.6 1.7 %broadcast_in_dim.26.earlier_ref = bf16[4,16,3584]{2,1,0:T(8,128)(2,1)} broadcast(bf16[16,3584]{1,0:T(8,128)(2,1)} %bitcast.28), dimensions={1,2} | broadcast | bytes 573440 | tf_op jit(solution)/shard_map/broadcast_in_dim | solution.py:460
  2.4 4.8 %all-to-all-start = ((bf16[4,16,3584]{2,1,0:T(8,128)(2,1)}), bf16[4,16,3584]{2,1,0:T(8,128)(2,1)S(1)}, u32[]{:S(2)}, u32[]{:S(2)}) async-start(bf16[4,16,3584]{2,1,0:T(8,128)(2,1)} %broadcast_in_dim.26.earlier_ref), calls=%async_computation | async-start | bytes 917504 | tf_op jit(solution)/shard_map/all_to_all | solution.py:25
  7.2 3.1 %pack_weights.1 = (bf16[5376,128]{1,0:T(8,128)(2,1)}, bf16[5376,128]{1,0:T(8,128)(2,1)}) custom-call(bf16[3584,256]{1,0:T(8,128)(2,1)} %bitcast.24, bf16[256,3584]{1,0:T(8,128)(2,1)} %bitcast.26, bf16[4,16,3584]{2,1,0:T(8,128)(2,1)} %broadcast_in_dim.26.earlier_ref), custom_call_target="tpu_custom_call" | custom-call | bytes 7340032 | tf_op jit(solution)/shard_map/pack_weights/pallas_call | solution.py:121
  10.4 3.4 %collective-permute-start = (bf16[5376,128]{1,0:T(8,128)(2,1)}, bf16[5376,128]{1,0:T(8,128)(2,1)S(1)}, u32[]{:S(2)}, u32[]{:S(2)}) collective-permute-start(bf16[5376,128]{1,0:T(8,128)(2,1)} %get-tuple-element.22), channel_id=1, source_target_pairs={{0,1},{1,2},{2,3},{3,0},{4,5},{5,6},{6,7},{7,4},{8,9},{9,10},{10,1... | collective-permute-start | bytes 4128776 | tf_op jit(solution)/shard_map/ppermute | solution.py:17
  13.8 3.1 %collective-permute-start.1 = (bf16[5376,128]{1,0:T(8,128)(2,1)}, bf16[5376,128]{1,0:T(8,128)(2,1)S(1)}, u32[]{:S(2)}, u32[]{:S(2)}) collective-permute-start(bf16[5376,128]{1,0:T(8,128)(2,1)} %get-tuple-element.23), channel_id=1, source_target_pairs={{0,3},{1,0},{2,1},{3,2},{4,7},{5,4},{6,5},{7,6},{8,11},{9,8},{10,9... | collective-permute-start | bytes 4128776 | tf_op jit(solution)/shard_map/ppermute | solution.py:17
  18.3 1.8 %norm_and_route.1 = (bf16[16,3584]{1,0:T(8,128)(2,1)}, f32[16,896]{1,0:T(8,128)}, bf16[256,16]{1,0:T(8,128)(2,1)}, bf16[128,2,896]{2,1,0:T(2,128)(2,1)}) custom-call(bf16[4,16,3584]{2,1,0:T(8,128)(2,1)S(1)} %all-to-all-done.copies_ref, bf16[16,3584]{1,0:T(8,128)(2,1)S(1)} %copy-done.8, f32[3584]{0:T(1024)S(1)} %copy-done.10, s32[8,16]{1,0:T(8,128)S(1)} %bitcast.23), custom_call_target="tpu_custom_call" | custom-call | flops 7340032 | bytes 1146880 | tf_op jit(solution)/shard_map/norm_and_route/pallas_call | solution.py:265
  20.1 20.6 %all-to-all-start.1 = ((bf16[128,2,896]{2,1,0:T(2,128)(2,1)}), bf16[128,2,896]{2,1,0:T(2,128)(2,1)S(1)}, u32[]{:S(2)}, u32[]{:S(2)}) async-start(bf16[128,2,896]{2,1,0:T(2,128)(2,1)} %get-tuple-element.18), calls=%async_computation.1 | async-start | bytes 917504 | tf_op jit(solution)/shard_map/all_to_all | solution.py:469
  40.7 4.0 %collective-permute-done.after_ref = bf16[5376,128]{1,0:T(8,128)(2,1)S(1)} collective-permute-done((bf16[5376,128]{1,0:T(8,128)(2,1)}, bf16[5376,128]{1,0:T(8,128)(2,1)S(1)}, u32[]{:S(2)}, u32[]{:S(2)}) %collective-permute-start) | collective-permute-done | bytes 1376288 | tf_op jit(solution)/shard_map/ppermute | solution.py:17
  45.5 1.9 %collective-permute-start.2 = (bf16[1792,128]{1,0:T(8,128)(2,1)}, bf16[1792,128]{1,0:T(8,128)(2,1)S(1)}, u32[]{:S(2)}, u32[]{:S(2)}) collective-permute-start(bf16[1792,128]{1,0:T(8,128)(2,1)} %slice.16), channel_id=1, source_target_pairs={{0,1},{1,2},{2,3},{3,0},{4,5},{5,6},{6,7},{7,4},{8,9},{9,10},{10,1... | collective-permute-start | bytes 1376264 | tf_op jit(solution)/shard_map/ppermute | solution.py:17
  48.3 4.6 %collective-permute-start.3 = (bf16[1792,128]{1,0:T(8,128)(2,1)}, bf16[1792,128]{1,0:T(8,128)(2,1)}, u32[]{:S(2)}, u32[]{:S(2)}) collective-permute-start(bf16[1792,128]{1,0:T(8,128)(2,1)} %slice.17), channel_id=1, source_target_pairs={{0,3},{1,0},{2,1},{3,2},{4,7},{5,4},{6,5},{7,6},{8,11},{9,8},{10,9... | collective-permute-start | bytes 1376264 | tf_op jit(solution)/shard_map/ppermute | solution.py:17
  52.9 2.2 %own_blocks.1 = (bf16[896,256]{1,0:T(8,128)(2,1)}, bf16[256,896]{1,0:T(8,128)(2,1)}) custom-call(bf16[3584,256]{1,0:T(8,128)(2,1)} %bitcast.25, bf16[256,3584]{1,0:T(8,128)(2,1)} %bitcast.27, bf16[16,3584]{1,0:T(8,128)(2,1)} %get-tuple-element.19.earlier_ref), custom_call_target="tpu_custom_call" | custom-call | tf_op jit(solution)/shard_map/own_blocks/pallas_call | solution.py:156
  56.8 1.7 %collective-permute-done.3.high_ref = bf16[1792,128]{1,0:T(8,128)(2,1)} collective-permute-done((bf16[1792,128]{1,0:T(8,128)(2,1)}, bf16[1792,128]{1,0:T(8,128)(2,1)}, u32[]{:S(2)}, u32[]{:S(2)}) %collective-permute-start.3) | collective-permute-done | bytes 458784 | tf_op jit(solution)/shard_map/ppermute | solution.py:17
  60.6 1.7 %join_weights.1 = (bf16[896,1024]{1,0:T(8,128)(2,1)S(1)}, bf16[1024,896]{1,0:T(8,128)(2,1)S(1)}) custom-call(bf16[896,256]{1,0:T(8,128)(2,1)S(1)} %copy-done.5, bf16[256,896]{1,0:T(8,128)(2,1)S(1)} %copy-done.6, bf16[5376,128]{1,0:T(8,128)(2,1)S(1)} %collective-permute-done.after_ref, bf16[5376,128]{1,0:T(8,128)(2,1)S(1)} %collective-permute-done.1.before_ref, ...), custom_call_target="tpu_custom_call" | custom-call | bytes 7340032 | tf_op jit(solution)/shard_map/join_weights/pallas_call | solution.py:195
  64.8 6.3 %all-to-all-done.1.rows_ref = bf16[128,2,896]{2,1,0:T(2,128)(2,1)S(1)} async-done(((bf16[128,2,896]{2,1,0:T(2,128)(2,1)}), bf16[128,2,896]{2,1,0:T(2,128)(2,1)S(1)}, u32[]{:S(2)}, u32[]{:S(2)}) %all-to-all-start.1) | async-done | bytes 458784 | tf_op jit(solution)/shard_map/all_to_all | solution.py:469
  73.4 10.9 %all_to_all.25.shares_hbm = bf16[4,256,256]{2,1,0:T(8,128)(2,1)S(1)} all-to-all(bf16[4,256,256]{2,1,0:T(8,128)(2,1)S(1)} %expert_up.1), channel_id=1, replica_groups=mesh['dp'=128,'hg'=4] {'hg'}, dimensions={0} | all-to-all | bytes 1048576 | tf_op jit(solution)/shard_map/all_to_all | solution.py:25
  84.3 1.7 %expert_silu.1 = bf16[4,272,256]{2,1,0:T(8,128)(2,1)} custom-call(bf16[4,256,256]{2,1,0:T(8,128)(2,1)S(1)} %all_to_all.25.shares_hbm, bf16[16,256]{1,0:T(8,128)(2,1)S(1)} %fusion.9.extra_hbm), custom_call_target="tpu_custom_call" | custom-call | flops 524288 | bytes 1048576 | tf_op jit(solution)/shard_map/expert_silu/pallas_call | solution.py:391
  86.0 10.6 %all_to_all.26.active_ref = bf16[4,272,256]{2,1,0:T(8,128)(2,1)S(1)} all-to-all(bf16[4,272,256]{2,1,0:T(8,128)(2,1)} %expert_silu.1), channel_id=1, replica_groups=mesh['dp'=128,'hg'=4] {'hg'}, dimensions={0} | all-to-all | bytes 1114112 | tf_op jit(solution)/shard_map/all_to_all | solution.py:25
  98.2 21.3 %all-to-all-start.4 = ((bf16[128,2,896]{2,1,0:T(2,128)(2,1)}), bf16[128,2,896]{2,1,0:T(2,128)(2,1)S(1)}, u32[]{:S(2)}, u32[]{:S(2)}) async-start(bf16[128,2,896]{2,1,0:T(2,128)(2,1)} %expert_down.1), calls=%async_computation.4 | async-start | bytes 917504 | tf_op jit(solution)/shard_map/all_to_all | solution.py:485
  120.2 2.2 %collective-permute-start.4 = (bf16[1,128,576]{1,2,0:T(8,128)(2,1)S(1)}, bf16[1,128,576]{1,2,0:T(8,128)(2,1)S(1)}, u32[]{:S(2)}, u32[]{:S(2)}) collective-permute-start(bf16[1,128,576]{1,2,0:T(8,128)(2,1)S(1)} %copy-done.13), channel_id=1, source_target_pairs={{0,1},{1,2},{2,3},{3,0},{4,5},{5,6},{6,7},{7,4},{8,9},{9,10},{10,1... | collective-permute-start | bytes 442376 | tf_op jit(solution)/shard_map/ppermute | solution.py:17
  122.4 3.7 %collective-permute-start.5 = (bf16[1,128,576]{1,2,0:T(8,128)(2,1)S(1)}, bf16[1,128,576]{1,2,0:T(8,128)(2,1)S(1)}, u32[]{:S(2)}, u32[]{:S(2)}) collective-permute-start(bf16[1,128,576]{1,2,0:T(8,128)(2,1)S(1)} %copy-done.13), channel_id=1, source_target_pairs={{0,2},{1,3},{2,0},{3,1},{4,6},{5,7},{6,4},{7,5},{8,10},{9,11},{10,... | collective-permute-start | bytes 442376 | tf_op jit(solution)/shard_map/ppermute | solution.py:17
  126.1 2.7 %collective-permute-start.6 = (bf16[1,128,576]{1,2,0:T(8,128)(2,1)S(1)}, bf16[1,128,576]{1,2,0:T(8,128)(2,1)S(1)}, u32[]{:S(2)}, u32[]{:S(2)}) collective-permute-start(bf16[1,128,576]{1,2,0:T(8,128)(2,1)S(1)} %copy-done.13), channel_id=1, source_target_pairs={{0,3},{1,0},{2,1},{3,2},{4,7},{5,4},{6,5},{7,6},{8,11},{9,8},{10,9... | collective-permute-start | bytes 442376 | tf_op jit(solution)/shard_map/ppermute | solution.py:17
  129.5 1.8 %gates.1.gates_hbm = bf16[256,16]{1,0:T(8,128)(2,1)} custom-call(bf16[4,16,256]{2,1,0:T(8,128)(2,1)} %slice.19.parts_ref, bf16[256,16]{1,0:T(8,128)(2,1)} %get-tuple-element.31.route_ref), custom_call_target="tpu_custom_call" | custom-call | tf_op jit(solution)/shard_map/gates/pallas_call | solution.py:310
  131.4 2.5 %collective-permute-done.6 = bf16[1,128,576]{1,2,0:T(8,128)(2,1)S(1)} collective-permute-done((bf16[1,128,576]{1,2,0:T(8,128)(2,1)S(1)}, bf16[1,128,576]{1,2,0:T(8,128)(2,1)S(1)}, u32[]{:S(2)}, u32[]{:S(2)}) %collective-permute-start.6) | collective-permute-done | bytes 147488 | tf_op jit(solution)/shard_map/ppermute | solution.py:17
  135.3 14.7 %all-to-all-done.4.returned_ref = bf16[128,2,896]{2,1,0:T(2,128)(2,1)S(1)} async-done(((bf16[128,2,896]{2,1,0:T(2,128)(2,1)}), bf16[128,2,896]{2,1,0:T(2,128)(2,1)S(1)}, u32[]{:S(2)}, u32[]{:S(2)}) %all-to-all-start.4) | async-done | bytes 458784 | tf_op jit(solution)/shard_map/all_to_all | solution.py:485
  (51 shorter events, 16.2 us)
Async XLA Ops:
  0.6 54.4 %copy-start = (bf16[3584,32]{0,1:T(8,128)(2,1)S(1)}, bf16[3584,32]{0,1:T(8,128)(2,1)}, u32[]{:S(2)}) copy-start(bf16[3584,32]{0,1:T(8,128)(2,1)} %param.16) | copy-start | bytes 688132
  2.4 14.5 %all-to-all-start = ((bf16[4,16,3584]{2,1,0:T(8,128)(2,1)}), bf16[4,16,3584]{2,1,0:T(8,128)(2,1)S(1)}, u32[]{:S(2)}, u32[]{:S(2)}) async-start(bf16[4,16,3584]{2,1,0:T(8,128)(2,1)} %broadcast_in_dim.26.earlier_ref), calls=%async_computation | async-start | bytes 917504 | tf_op jit(solution)/shard_map/all_to_all | solution.py:25
  7.2 9.7 %copy-start.8 = (bf16[16,3584]{1,0:T(8,128)(2,1)S(1)}, bf16[16,3584]{1,0:T(8,128)(2,1)}, u32[]{:S(2)}) copy-start(bf16[16,3584]{1,0:T(8,128)(2,1)} %residual_hbm.1) | copy-start | bytes 344068
  10.4 34.4 %collective-permute-start = (bf16[5376,128]{1,0:T(8,128)(2,1)}, bf16[5376,128]{1,0:T(8,128)(2,1)S(1)}, u32[]{:S(2)}, u32[]{:S(2)}) collective-permute-start(bf16[5376,128]{1,0:T(8,128)(2,1)} %get-tuple-element.22), channel_id=1, source_target_pairs={{0,1},{1,2},{2,3},{3,0},{4,5},{5,6},{6,7},{7,4},{8,9},{9,10},{10,1... | collective-permute-start | bytes 4128776 | tf_op jit(solution)/shard_map/ppermute | solution.py:17
  13.8 33.7 %collective-permute-start.1 = (bf16[5376,128]{1,0:T(8,128)(2,1)}, bf16[5376,128]{1,0:T(8,128)(2,1)S(1)}, u32[]{:S(2)}, u32[]{:S(2)}) collective-permute-start(bf16[5376,128]{1,0:T(8,128)(2,1)} %get-tuple-element.23), channel_id=1, source_target_pairs={{0,3},{1,0},{2,1},{3,2},{4,7},{5,4},{6,5},{7,6},{8,11},{9,8},{10,9... | collective-permute-start | bytes 4128776 | tf_op jit(solution)/shard_map/ppermute | solution.py:17
  16.9 0.7 copy-start.10
  20.1 51.0 %all-to-all-start.1 = ((bf16[128,2,896]{2,1,0:T(2,128)(2,1)}), bf16[128,2,896]{2,1,0:T(2,128)(2,1)S(1)}, u32[]{:S(2)}, u32[]{:S(2)}) async-start(bf16[128,2,896]{2,1,0:T(2,128)(2,1)} %get-tuple-element.18), calls=%async_computation.1 | async-start | bytes 917504 | tf_op jit(solution)/shard_map/all_to_all | solution.py:469
  45.5 11.3 %collective-permute-start.2 = (bf16[1792,128]{1,0:T(8,128)(2,1)}, bf16[1792,128]{1,0:T(8,128)(2,1)S(1)}, u32[]{:S(2)}, u32[]{:S(2)}) collective-permute-start(bf16[1792,128]{1,0:T(8,128)(2,1)} %slice.16), channel_id=1, source_target_pairs={{0,1},{1,2},{2,3},{3,0},{4,5},{5,6},{6,7},{7,4},{8,9},{9,10},{10,1... | collective-permute-start | bytes 1376264 | tf_op jit(solution)/shard_map/ppermute | solution.py:17
  48.3 10.3 %collective-permute-start.3 = (bf16[1792,128]{1,0:T(8,128)(2,1)}, bf16[1792,128]{1,0:T(8,128)(2,1)}, u32[]{:S(2)}, u32[]{:S(2)}) collective-permute-start(bf16[1792,128]{1,0:T(8,128)(2,1)} %slice.17), channel_id=1, source_target_pairs={{0,3},{1,0},{2,1},{3,2},{4,7},{5,4},{6,5},{7,6},{8,11},{9,8},{10,9... | collective-permute-start | bytes 1376264 | tf_op jit(solution)/shard_map/ppermute | solution.py:17
  52.9 2.2 %copy-start.12 = (bf16[16,3584]{1,0:T(8,128)(2,1)S(1)}, bf16[16,3584]{1,0:T(8,128)(2,1)}, u32[]{:S(2)}) copy-start(bf16[16,3584]{1,0:T(8,128)(2,1)} %get-tuple-element.19.earlier_ref) | copy-start | bytes 344068
  58.6 1.0 copy-start.5
  59.6 1.0 copy-start.6
  62.4 1.3 copy-start.1
  63.6 1.2 copy-start.3
  71.2 1.5 copy-start.4
  73.4 23.2 %copy-start.2 = (bf16[1024,896]{1,0:T(8,128)(2,1)S(1)}, bf16[1024,896]{1,0:T(8,128)(2,1)}, u32[]{:S(2)}) copy-start(bf16[1024,896]{1,0:T(8,128)(2,1)} %copy-done.1) | copy-start | bytes 5505028
  96.6 23.5 %copy-start.13 = (bf16[1,128,576]{1,2,0:T(8,128)(2,1)S(1)}, bf16[1,128,576]{1,2,0:T(8,128)(2,1)}, u32[]{:S(2)}) copy-start(bf16[1,128,576]{1,2,0:T(8,128)(2,1)} %param.11) | copy-start | bytes 442372
  98.2 35.7 %copy-start.14 = (bf16[1,32,576]{2,1,0:T(8,128)(2,1)S(1)}, bf16[1,32,576]{2,1,0:T(8,128)(2,1)}, u32[]{:S(2)}) copy-start(bf16[1,32,576]{2,1,0:T(8,128)(2,1)} %param.10) | copy-start | bytes 110596
  98.2 51.8 %copy-start.9 = (f32[16,896]{1,0:T(8,128)S(1)}, f32[16,896]{1,0:T(8,128)}, u32[]{:S(2)}) copy-start(f32[16,896]{1,0:T(8,128)} %get-tuple-element.33.hidden_hbm) | copy-start | bytes 172036
  98.2 51.8 %all-to-all-start.4 = ((bf16[128,2,896]{2,1,0:T(2,128)(2,1)}), bf16[128,2,896]{2,1,0:T(2,128)(2,1)S(1)}, u32[]{:S(2)}, u32[]{:S(2)}) async-start(bf16[128,2,896]{2,1,0:T(2,128)(2,1)} %expert_down.1), calls=%async_computation.4 | async-start | bytes 917504 | tf_op jit(solution)/shard_map/all_to_all | solution.py:485
  120.2 11.1 %collective-permute-start.4 = (bf16[1,128,576]{1,2,0:T(8,128)(2,1)S(1)}, bf16[1,128,576]{1,2,0:T(8,128)(2,1)S(1)}, u32[]{:S(2)}, u32[]{:S(2)}) collective-permute-start(bf16[1,128,576]{1,2,0:T(8,128)(2,1)S(1)} %copy-done.13), channel_id=1, source_target_pairs={{0,1},{1,2},{2,3},{3,0},{4,5},{5,6},{6,7},{7,4},{8,9},{9,10},{10,1... | collective-permute-start | bytes 442376 | tf_op jit(solution)/shard_map/ppermute | solution.py:17
  122.4 8.9 %collective-permute-start.5 = (bf16[1,128,576]{1,2,0:T(8,128)(2,1)S(1)}, bf16[1,128,576]{1,2,0:T(8,128)(2,1)S(1)}, u32[]{:S(2)}, u32[]{:S(2)}) collective-permute-start(bf16[1,128,576]{1,2,0:T(8,128)(2,1)S(1)} %copy-done.13), channel_id=1, source_target_pairs={{0,2},{1,3},{2,0},{3,1},{4,6},{5,7},{6,4},{7,5},{8,10},{9,11},{10,... | collective-permute-start | bytes 442376 | tf_op jit(solution)/shard_map/ppermute | solution.py:17
  126.1 7.7 %collective-permute-start.6 = (bf16[1,128,576]{1,2,0:T(8,128)(2,1)S(1)}, bf16[1,128,576]{1,2,0:T(8,128)(2,1)S(1)}, u32[]{:S(2)}, u32[]{:S(2)}) collective-permute-start(bf16[1,128,576]{1,2,0:T(8,128)(2,1)S(1)} %copy-done.13), channel_id=1, source_target_pairs={{0,3},{1,0},{2,1},{3,2},{4,7},{5,4},{6,5},{7,6},{8,11},{9,8},{10,9... | collective-permute-start | bytes 442376 | tf_op jit(solution)/shard_map/ppermute | solution.py:17
  131.3 18.7 %copy-start.7 = (bf16[256,16]{1,0:T(8,128)(2,1)S(1)}, bf16[256,16]{1,0:T(8,128)(2,1)}, u32[]{:S(2)}) copy-start(bf16[256,16]{1,0:T(8,128)(2,1)} %gates.1.gates_hbm) | copy-start | bytes 24580
  (1 other events, 0.7 us)

commit v3 on v2

--- a/solution.py
+++ b/solution.py
@@ -11,6 +11,9 @@
 NORM_EPS = 1e-06
 VMEM_LIMIT = 16 << 20
 WHOLE_VMEM = 60 << 20
+JOIN_FLOPS = 9 * 10 ** 9
+DOWN_FLOPS = 4 * 10 ** 9
+ORDER = (0, 1, 3, 2)
 
 
 def shift(value, distance, size):
@@ -80,55 +83,60 @@
     part = features // size
     half = units // 2
     chunks = part // 128
+    first = chunks // 2
     block = 2 * part
+    length = 2 * block + first * units
     assert units == 256 and size == 4 and part % 128 == 0 and block == chunks * units
-    turns = (1, 3, 2)
-
-    def kernel(up_hbm, down_hbm, earlier_ref, next_hbm, back_hbm, up_ref, down_ref, next_ref, back_ref, sems):
+
+    def kernel(up_hbm, down_hbm, earlier_ref, next_hbm, back_hbm, up_ref, down_ref, far_ref, next_ref, back_ref, sems):
         ups = start_all(
-            [(up_hbm.at[pl.ds(place(d, size, part), part), :], up_ref.at[i]) for i, d in enumerate(turns)], sems
+            [(up_hbm.at[pl.ds(place(d, size, part), part), :], up_ref.at[i]) for i, d in enumerate((1, 2, 3))], sems
         )
         downs = start_all(
-            [(down_hbm.at[:, pl.ds(place(d, size, part), part)], down_ref.at[i]) for i, d in enumerate(turns)], sems, 3
-        )
-        outs = []
-        for i, (to_ref, to_hbm) in enumerate(((next_ref, next_hbm), (back_ref, back_hbm))):
+            [
+                (down_hbm.at[:, pl.ds(place(d, size, part), first * 128)], down_ref.at[i])
+                for i, d in enumerate((1, 3))
+            ]
+            + [(down_hbm.at[:, pl.ds(place(2, size, part), part)], far_ref)],
+            sems, 3,
+        )
+
+        def put_up(i, to_ref, at):
             ups[i].wait()
-            to_ref[:part, :] = up_ref[i, :, :half]
-            to_ref[part:block, :] = up_ref[i, :, half:]
+            to_ref[at:at + part, :] = up_ref[i, :, :half]
+            to_ref[at + part:at + block, :] = up_ref[i, :, half:]
+
+        def put_down(i, to_ref):
             downs[i].wait()
-            for k in range(chunks):
-                to_ref[block + k * units:block + (k + 1) * units, :] = down_ref[i, :, k * 128:(k + 1) * 128]
-            outs += start_all(
-                [(to_ref.at[:2 * block, :], to_hbm.at[:2 * block, :])], sems, 6 + 2 * i
-            )
-        ups[2].wait()
+            for k in range(first):
+                at = 2 * block + k * units
+                to_ref[at:at + units, :] = down_ref[i, :, k * 128:(k + 1) * 128]
+
+        put_up(0, next_ref, 0)
+        put_up(1, next_ref, block)
+        put_down(0, next_ref)
+        outs = start_all([(next_ref, next_hbm)], sems, 6)
+        put_up(2, back_ref, 0)
+        put_down(1, back_ref)
         downs[2].wait()
-        for i, (to_ref, to_hbm) in enumerate(((next_ref, next_hbm), (back_ref, back_hbm))):
-            first = 2 * block
-            to_ref[first:first + part, :] = up_ref[2, :, i * half:(i + 1) * half]
-            first += part
-            for k in range(chunks):
-                to_ref[first + k * half:first + (k + 1) * half, :] = down_ref[
-                    2, i * half:(i + 1) * half, k * 128:(k + 1) * 128
-                ]
-            outs += start_all(
-                [(to_ref.at[2 * block:, :], to_hbm.at[2 * block:, :])], sems, 7 + 2 * i
-            )
+        for k in range(chunks):
+            back_ref[block + k * units:block + (k + 1) * units, :] = far_ref[:, k * 128:(k + 1) * 128]
+        outs += start_all([(back_ref, back_hbm)], sems, 7)
         wait_all(outs)
 
-    sent = pltpu.HBM((3 * block, 128), up_weights.dtype)
-    return pl.pallas_call(
-        kernel,
-        out_shape=[sent, sent],
+    dtype = up_weights.dtype
+    return pl.pallas_call(
+        kernel,
+        out_shape=[pltpu.HBM((length, 128), dtype)] * 2,
         in_specs=[HBM, HBM, pl.BlockSpec(memory_space=pl.ANY)],
         out_specs=[HBM, HBM],
         scratch_shapes=[
-            pltpu.VMEM((3, part, units), up_weights.dtype),
-            pltpu.VMEM((3, units, part), up_weights.dtype),
-            pltpu.VMEM((3 * block, 128), up_weights.dtype),
-            pltpu.VMEM((3 * block, 128), up_weights.dtype),
-            pltpu.SemaphoreType.DMA((10,)),
+            pltpu.VMEM((3, part, units), dtype),
+            pltpu.VMEM((2, units, first * 128), dtype),
+            pltpu.VMEM((units, part), dtype),
+            pltpu.VMEM((length, 128), dtype),
+            pltpu.VMEM((length, 128), dtype),
+            pltpu.SemaphoreType.DMA((8,)),
         ],
         cost_estimate=pl.CostEstimate(
             flops=0, bytes_accessed=8 * features * units, transcendentals=0
@@ -138,72 +146,141 @@
     )(up_weights, down_weights, earlier)
 
 
-def own_blocks(up_weights, down_weights, earlier, size):
+def rest_blocks(down_weights, earlier, size):
+    units, features = down_weights.shape
+    part = features // size
+    skip = part // 256 * 128
+    width = part - skip
+
+    def kernel(down_hbm, earlier_ref, next_hbm, back_hbm, ref, sems):
+        fetched = start_all(
+            [
+                (down_hbm.at[:, pl.ds(pl.multiple_of(place(d, size, part) + skip, 128), width)], ref.at[i])
+                for i, d in enumerate((1, 3))
+            ],
+            sems,
+        )
+        outs = []
+        for i, out_hbm in enumerate((next_hbm, back_hbm)):
+            fetched[i].wait()
+            outs += start_all([(ref.at[i], out_hbm)], sems, 2 + i)
+        wait_all(outs)
+
+    return pl.pallas_call(
+        kernel,
+        out_shape=[pltpu.HBM((units, width), down_weights.dtype)] * 2,
+        in_specs=[HBM, pl.BlockSpec(memory_space=pl.ANY)],
+        out_specs=[HBM, HBM],
+        scratch_shapes=[pltpu.VMEM((2, units, width), down_weights.dtype), pltpu.SemaphoreType.DMA((4,))],
+        compiler_params=pltpu.CompilerParams(vmem_limit_bytes=WHOLE_VMEM),
+        name="rest_blocks",
+    )(down_weights, earlier)
+
+
+def join_up_near(up_weights, after, before, size):
     features, units = up_weights.shape
     part = features // size
-
-    def kernel(up_hbm, down_hbm, earlier_ref, own_up_hbm, own_down_hbm, up_ref, down_ref, sems):
-        wait_all(start_all(
-            [
-                (up_hbm.at[pl.ds(place(0, size, part), part), :], up_ref),
-                (down_hbm.at[:, pl.ds(place(0, size, part), part)], down_ref),
+    half = units // 2
+
+    def kernel(up_hbm, after_hbm, before_hbm, out_hbm, ref, sems):
+        fetched = start_all(
+            [(up_hbm.at[pl.ds(place(0, size, part), part), :], ref.at[:, :units])]
+            + [
+                (hbm.at[j * part:(j + 1) * part, :], ref.at[:, i * units + j * half:i * units + (j + 1) * half])
+                for i, hbm in ((1, after_hbm), (2, before_hbm))
+                for j in (0, 1)
             ],
             sems,
+        )
+        wait_all(fetched)
+        wait_all(start_all([(ref, out_hbm.at[:, :3 * units])], sems, 5))
+
+    dtype = up_weights.dtype
+    return pl.pallas_call(
+        kernel,
+        out_shape=pltpu.HBM((part, size * units), dtype),
+        in_specs=[HBM] * 3,
+        out_specs=HBM,
+        scratch_shapes=[pltpu.VMEM((part, 3 * units), dtype), pltpu.SemaphoreType.DMA((6,))],
+        cost_estimate=pl.CostEstimate(
+            flops=JOIN_FLOPS, bytes_accessed=12 * part * units, transcendentals=0
+        ),
+        compiler_params=pltpu.CompilerParams(vmem_limit_bytes=WHOLE_VMEM),
+        name="join_up_near",
+    )(up_weights, after, before)
+
+
+def join_up_far(joined, far):
+    part, width = joined.shape
+    half = far.shape[1]
+
+    def kernel(far_hbm, joined_hbm, out_hbm, ref, sems):
+        wait_all(start_all(
+            [(far_hbm.at[i * part:(i + 1) * part, :], ref.at[:, i * half:(i + 1) * half]) for i in (0, 1)], sems
         ))
-        wait_all(start_all([(up_ref, own_up_hbm), (down_ref, own_down_hbm)], sems, 2))
-
-    dtype = up_weights.dtype
-    return pl.pallas_call(
-        kernel,
-        out_shape=[pltpu.HBM((part, units), dtype), pltpu.HBM((units, part), dtype)],
-        in_specs=[HBM, HBM, pl.BlockSpec(memory_space=pl.ANY)],
-        out_specs=[HBM, HBM],
+        wait_all(start_all([(ref, out_hbm.at[:, width - 2 * half:])], sems, 2))
+
+    return pl.pallas_call(
+        kernel,
+        out_shape=pltpu.HBM(joined.shape, joined.dtype),
+        in_specs=[HBM] * 2,
+        out_specs=HBM,
+        scratch_shapes=[pltpu.VMEM((part, 2 * half), joined.dtype), pltpu.SemaphoreType.DMA((3,))],
+        input_output_aliases={1: 0},
+        compiler_params=pltpu.CompilerParams(vmem_limit_bytes=WHOLE_VMEM),
+        name="join_up_far",
+    )(far, joined)
+
+
+def join_down(down_weights, after, before, after_rest, before_rest, far, size):
+    units, features = down_weights.shape
+    part = features // size
+    chunks = part // 128
+    first = chunks // 2
+    block = 2 * part
+
+    def kernel(
+        down_hbm, after_hbm, before_hbm, after_rest_hbm, before_rest_hbm, far_hbm, out_hbm, near_ref, far_ref, ref, sems
+    ):
+        fetched = start_all(
+            [
+                (after_hbm.at[2 * block:, :], near_ref.at[0]),
+                (before_hbm.at[2 * block:, :], near_ref.at[1]),
+                (far_hbm, far_ref),
+                (down_hbm.at[:, pl.ds(place(0, size, part), part)], ref.at[:units, :]),
+                (after_rest_hbm, ref.at[units:2 * units, first * 128:]),
+                (before_rest_hbm, ref.at[2 * units:3 * units, first * 128:]),
+            ],
+            sems,
+        )
+        for i in (0, 1):
+            fetched[i].wait()
+            for k in range(first):
+                ref[(i + 1) * units:(i + 2) * units, k * 128:(k + 1) * 128] = near_ref[i, k * units:(k + 1) * units, :]
+        fetched[2].wait()
+        for k in range(chunks):
+            ref[3 * units:, k * 128:(k + 1) * 128] = far_ref[k * units:(k + 1) * units, :]
+        wait_all(fetched[3:])
+        wait_all(start_all([(ref, out_hbm)], sems, 6))
+
+    dtype = down_weights.dtype
+    return pl.pallas_call(
+        kernel,
+        out_shape=pltpu.HBM((size * units, part), dtype),
+        in_specs=[HBM] * 6,
+        out_specs=HBM,
         scratch_shapes=[
-            pltpu.VMEM((part, units), dtype),
-            pltpu.VMEM((units, part), dtype),
-            pltpu.SemaphoreType.DMA((4,)),
+            pltpu.VMEM((2, first * units, 128), dtype),
+            pltpu.VMEM((block, 128), dtype),
+            pltpu.VMEM((size * units, part), dtype),
+            pltpu.SemaphoreType.DMA((7,)),
         ],
+        cost_estimate=pl.CostEstimate(
+            flops=DOWN_FLOPS, bytes_accessed=16 * part * units, transcendentals=0
+        ),
         compiler_params=pltpu.CompilerParams(vmem_limit_bytes=WHOLE_VMEM),
-        name="own_blocks",
-    )(up_weights, down_weights, earlier)
-
-
-def join_weights(own_up, own_down, after, before, far_low, far_high):
-    part, units = own_up.shape
-    half = units // 2
-    chunks = part // 128
-    block = 2 * part
-
-    def kernel(own_up_ref, own_down_ref, after_ref, before_ref, low_ref, high_ref, up_ref, down_ref):
-        up_ref[:, :units] = own_up_ref[...]
-        up_ref[:, units:units + half] = after_ref[:part, :]
-        up_ref[:, units + half:2 * units] = after_ref[part:block, :]
-        up_ref[:, 2 * units:2 * units + half] = low_ref[:part, :]
-        up_ref[:, 2 * units + half:3 * units] = high_ref[:part, :]
-        up_ref[:, 3 * units:3 * units + half] = before_ref[:part, :]
-        up_ref[:, 3 * units + half:] = before_ref[part:block, :]
-        down_ref[:units, :] = own_down_ref[...]
-        for k in range(chunks):
-            lanes = slice(k * 128, (k + 1) * 128)
-            whole = slice(block + k * units, block + (k + 1) * units)
-            some = slice(part + k * half, part + (k + 1) * half)
-            down_ref[units:2 * units, lanes] = after_ref[whole, :]
-            down_ref[2 * units:2 * units + half, lanes] = low_ref[some, :]
-            down_ref[2 * units + half:3 * units, lanes] = high_ref[some, :]
-            down_ref[3 * units:, lanes] = before_ref[whole, :]
-
-    return pl.pallas_call(
-        kernel,
-        out_shape=[
-            jax.ShapeDtypeStruct((part, 4 * units), own_up.dtype),
-            jax.ShapeDtypeStruct((4 * units, part), own_up.dtype),
-        ],
-        cost_estimate=pl.CostEstimate(
-            flops=0, bytes_accessed=32 * part * units, transcendentals=0
-        ),
-        compiler_params=pltpu.CompilerParams(vmem_limit_bytes=VMEM_LIMIT),
-        name="join_weights",
-    )(own_up, own_down, after, before, far_low, far_high)
+        name="join_down",
+    )(down_weights, after, before, after_rest, before_rest, far)
 
 
 def norm_and_route(copies, residual, gain, choices, experts, capacity):
@@ -350,10 +427,9 @@
     def kernel(rows_ref, weights_ref, out_ref):
         me = lax.axis_index("hg")
         rows = rows_ref[...].reshape(slots, part)
-        for d in range(size):
-            owner = lax.rem(me + size - d, size)
-            out_ref[owner] = jnp.dot(
-                rows, weights_ref[:, d * units:(d + 1) * units],
+        for i, d in enumerate(ORDER):
+            out_ref[lax.rem(me + size - d, size)] = jnp.dot(
+                rows, weights_ref[:, i * units:(i + 1) * units],
                 preferred_element_type=jnp.float32,
             ).astype(jnp.bfloat16)
 
@@ -416,10 +492,10 @@
     def kernel(active_ref, weights_ref, out_ref):
         me = lax.axis_index("hg")
         total = jnp.zeros((slots, part), jnp.float32)
-        for d in range(size):
-            owner = lax.rem(me + size - d, size)
+        for i, d in enumerate(ORDER):
             total += jnp.dot(
-                active_ref[owner, :slots, :], weights_ref[d * units:(d + 1) * units, :],
+                active_ref[lax.rem(me + size - d, size), :slots, :],
+                weights_ref[i * units:(i + 1) * units, :],
                 preferred_element_type=jnp.float32,
             )
         out_ref[...] = total.astype(jnp.bfloat16).reshape(experts, capacity, part)
@@ -460,8 +536,11 @@
     copies = jnp.broadcast_to(partials[0][None], (size,) + partials.shape[1:])
     to_next, to_back = pack_weights(up_proj[0], down_proj[0], copies, size)
     after, before = shift(to_next, 1, size), shift(to_back, size - 1, size)
-    far = 4 * (feature_width // size)
-    far_low, far_high = shift(after[far:], 1, size), shift(before[far:], size - 1, size)
+    block = 2 * (feature_width // size)
+    far_up = shift(after[block:2 * block], 1, size)
+    far_down = shift(before[block:2 * block], size - 1, size)
+    next_rest, back_rest = rest_blocks(down_proj[0], after, size)
+    after_rest, before_rest = shift(next_rest, 1, size), shift(back_rest, size - 1, size)
 
     normed, hidden, route, outgoing = norm_and_route(
         exchange(copies), residual, norm_gain, expert_ids.T, experts, capacity
@@ -474,11 +553,13 @@
     extra = jnp.pad(
         jnp.concatenate([high, low], axis=1), ((0, 0), (0, unit_count - 2 * high.shape[1]))
     )
-    own_up, own_down = own_blocks(up_proj[0], down_proj[0], normed, size)
-    up_all, down_all = join_weights(own_up, own_down, after, before, far_low, far_high)
-    arrived, extra, up_all, down_all = lax.optimization_barrier((arrived, extra, up_all, down_all))
-
+    up_all = join_up_near(up_proj[0], after, before, size)
+    up_all = join_up_far(up_all, far_up)
+    arrived, extra, up_all = lax.optimization_barrier((arrived, extra, up_all))
     shares = exchange(expert_up(arrived, up_all))
+
+    down_all = join_down(down_proj[0], after, before, after_rest, before_rest, far_down, size)
+    shares, down_all = lax.optimization_barrier((shares, down_all))
     active = exchange(expert_silu(shares, extra))
     reduced = expert_down(active, down_all, experts, capacity)
     reduced, latent_cache = lax.optimization_barrier((reduced, latent_cache))

time: 152 us -> 142 us (0.934)
  blocking collectives: 21.5 us -> 10.6 us
  local copies, waits for them, and re-layouts: 11.5 us -> 5.66 us
  Pallas kernels: 15.6 us -> 21.3 us
    all_to_all x2 -> x1, blocking collectives: 21.5 us -> 10.6 us  [exchange(): return lax.all_to_all(value, 'hg', 0, 0, tiled=True)]
    all_to_all x1, starting transfers between devices: 21.3 us -> 12.2 us  [on_device(): lax.all_to_all(reduced, 'dp', split_axis=0, concat_axis=0, tiled=True)]
    ppermute x7 -> x9, waiting for transfers between devices: 9.7 us -> 2.48 us  [shift(): lax.ppermute(value, 'hg', [(i, (i + distance) % size) for i in range(size)])]
    ppermute x7 -> x9, starting transfers between devices: 21.6 us -> 26.9 us  [shift(): lax.ppermute(value, 'hg', [(i, (i + distance) % size) for i in range(size)])]
    pallas_call x3 -> x5, Pallas kernels: 7.08 us -> 11.9 us  [the longest x1 2.85 us: pack_weights(): pl.pallas_call(kernel, out_shape=[pltpu.HBM((length, 128), dtype)] * 2, i...]
    unnamed x33 -> x31, local copies, waits for them, and re-layouts: 7.53 us -> 3.19 us
    all_to_all x1, waiting for transfers between devices: 6.35 us -> 10.3 us  [on_device(): lax.all_to_all(outgoing, 'dp', split_axis=0, concat_axis=0, tiled=True)]
    all_to_all x1 -> x2, waiting for transfers between devices: 0.01 us -> 3.86 us  [exchange(): return lax.all_to_all(value, 'hg', 0, 0, tiled=True)]
  transfers between devices with their start and end apart: 10 -> 13, of which waited for: 6 -> 4; matrix products, arithmetic and copies ran while one was open for 3% -> 2% of each run, Pallas kernels for 7% -> 12%
where the time goes in v3:
time: 142 us; the launch traced here: 141 us
  starting transfers between devices  68 us (48%)
  waiting for transfers between devices  31.3 us (22%)
  Pallas kernels  21.3 us (15%)
  blocking collectives  10.6 us (7%)
  local copies, waits for them, and re-layouts  5.66 us (4%)
  matrix products  2.28 us (2%)
  between operations  1.65 us (1%)
    ppermute x9, starting transfers between devices, shift(): lax.ppermute(value, 'hg', [(i, (i + distance) % size) for i in range(size)])  26.9 us
    all_to_all x1, starting transfers between devices, on_device(): lax.all_to_all(outgoing, 'dp', split_axis=0, concat_axis=0, tiled=True)  20.6 us
    all_to_all x1, waiting for transfers between devices, on_device(): lax.all_to_all(reduced, 'dp', split_axis=0, concat_axis=0, tiled=True)  14.7 us
    all_to_all x1, starting transfers between devices, on_device(): lax.all_to_all(reduced, 'dp', split_axis=0, concat_axis=0, tiled=True)  12.2 us
    all_to_all x1, blocking collectives, exchange(): return lax.all_to_all(value, 'hg', 0, 0, tiled=True)  10.6 us
    all_to_all x1, waiting for transfers between devices, on_device(): lax.all_to_all(outgoing, 'dp', split_axis=0, concat_axis=0, tiled=True)  10.3 us
    all_to_all x2, starting transfers between devices, exchange(): return lax.all_to_all(value, 'hg', 0, 0, tiled=True)  8.31 us
    all_to_all x2, waiting for transfers between devices, exchange(): return lax.all_to_all(value, 'hg', 0, 0, tiled=True)  3.86 us
  transfers between devices with their start and end apart: 13, of which 4 were waited for; matrix products, arithmetic and copies ran while one was open for 2% of the time, Pallas kernels for 12%

profile of v3, /device:TPU:1, one launch (start us, length us, event | category | flops | bytes accessed | tf_op | source)
XLA Modules:
  0.0 141.1 jit_solution(3586971720618546105)
XLA Ops:
  2.4 4.8 %all-to-all-start = ((bf16[4,16,3584]{2,1,0:T(8,128)(2,1)}), bf16[4,16,3584]{2,1,0:T(8,128)(2,1)S(1)}, u32[]{:S(2)}, u32[]{:S(2)}) async-start(bf16[4,16,3584]{2,1,0:T(8,128)(2,1)} %broadcast_in_dim.26.earlier_ref), calls=%async_computation | async-start | bytes 917504 | tf_op jit(solution)/shard_map/all_to_all | solution.py:28
  7.2 2.9 %pack_weights.1 = (bf16[4352,128]{1,0:T(8,128)(2,1)}, bf16[4352,128]{1,0:T(8,128)(2,1)}) custom-call(bf16[3584,256]{1,0:T(8,128)(2,1)} %bitcast.27, bf16[256,3584]{1,0:T(8,128)(2,1)} %bitcast.24, bf16[4,16,3584]{2,1,0:T(8,128)(2,1)} %broadcast_in_dim.26.earlier_ref), custom_call_target="tpu_custom_call" | custom-call | bytes 7340032 | tf_op jit(solution)/shard_map/pack_weights/pallas_call | solution.py:128
  10.1 3.4 %collective-permute-start = (bf16[4352,128]{1,0:T(8,128)(2,1)}, bf16[4352,128]{1,0:T(8,128)(2,1)S(1)}, u32[]{:S(2)}, u32[]{:S(2)}) collective-permute-start(bf16[4352,128]{1,0:T(8,128)(2,1)} %get-tuple-element.19), channel_id=1, source_target_pairs={{0,1},{1,2},{2,3},{3,0},{4,5},{5,6},{6,7},{7,4},{8,9},{9,10},{10,1... | collective-permute-start | bytes 3342344 | tf_op jit(solution)/shard_map/ppermute | solution.py:20
  13.5 3.1 %collective-permute-start.2 = (bf16[4352,128]{1,0:T(8,128)(2,1)}, bf16[4352,128]{1,0:T(8,128)(2,1)S(1)}, u32[]{:S(2)}, u32[]{:S(2)}) collective-permute-start(bf16[4352,128]{1,0:T(8,128)(2,1)} %get-tuple-element.20), channel_id=1, source_target_pairs={{0,3},{1,0},{2,1},{3,2},{4,7},{5,4},{6,5},{7,6},{8,11},{9,8},{10,9... | collective-permute-start | bytes 3342344 | tf_op jit(solution)/shard_map/ppermute | solution.py:20
  16.7 1.8 %norm_and_route.1 = (bf16[16,3584]{1,0:T(8,128)(2,1)}, f32[16,896]{1,0:T(8,128)}, bf16[256,16]{1,0:T(8,128)(2,1)}, bf16[128,2,896]{2,1,0:T(2,128)(2,1)}) custom-call(bf16[4,16,3584]{2,1,0:T(8,128)(2,1)S(1)} %all-to-all-done.copies_ref, bf16[16,3584]{1,0:T(8,128)(2,1)S(1)} %copy-done.4, f32[3584]{0:T(1024)S(1)} %copy-done.6, s32[8,16]{1,0:T(8,128)S(1)} %bitcast.23), custom_call_target="tpu_custom_call" | custom-call | flops 7340032 | bytes 1146880 | tf_op jit(solution)/shard_map/norm_and_route/pallas_call | solution.py:342
  18.5 20.6 %all-to-all-start.1 = ((bf16[128,2,896]{2,1,0:T(2,128)(2,1)}), bf16[128,2,896]{2,1,0:T(2,128)(2,1)S(1)}, u32[]{:S(2)}, u32[]{:S(2)}) async-start(bf16[128,2,896]{2,1,0:T(2,128)(2,1)} %get-tuple-element.17), calls=%async_computation.1 | async-start | bytes 917504 | tf_op jit(solution)/shard_map/all_to_all | solution.py:548
  40.3 2.4 %collective-permute-start.1 = (bf16[1792,128]{1,0:T(8,128)(2,1)S(1)}, bf16[1792,128]{1,0:T(8,128)(2,1)S(1)}, u32[]{:S(2)}, u32[]{:S(2)}) collective-permute-start(bf16[1792,128]{1,0:T(8,128)(2,1)S(1)} %slice.16), channel_id=1, source_target_pairs={{0,1},{1,2},{2,3},{3,0},{4,5},{5,6},{6,7},{7,4},{8,9},{9,10},{10,1... | collective-permute-start | bytes 1376264 | tf_op jit(solution)/shard_map/ppermute | solution.py:20
  42.7 1.8 %rest_blocks.1 = (bf16[256,512]{1,0:T(8,128)(2,1)}, bf16[256,512]{1,0:T(8,128)(2,1)}) custom-call(bf16[256,3584]{1,0:T(8,128)(2,1)} %bitcast.25, bf16[4352,128]{1,0:T(8,128)(2,1)} %copy-done.8), custom_call_target="tpu_custom_call" | custom-call | tf_op jit(solution)/shard_map/rest_blocks/pallas_call | solution.py:169
  44.6 3.1 %collective-permute-start.3 = (bf16[256,512]{1,0:T(8,128)(2,1)}, bf16[256,512]{1,0:T(8,128)(2,1)}, u32[]{:S(2)}, u32[]{:S(2)}) collective-permute-start(bf16[256,512]{1,0:T(8,128)(2,1)} %get-tuple-element.23), channel_id=1, source_target_pairs={{0,1},{1,2},{2,3},{3,0},{4,5},{5,6},{6,7},{7,4},{8,9},{9,10},{10,1... | collective-permute-start | bytes 786440 | tf_op jit(solution)/shard_map/ppermute | solution.py:20
  47.7 3.4 %collective-permute-start.4 = (bf16[256,512]{1,0:T(8,128)(2,1)}, bf16[256,512]{1,0:T(8,128)(2,1)}, u32[]{:S(2)}, u32[]{:S(2)}) collective-permute-start(bf16[256,512]{1,0:T(8,128)(2,1)} %get-tuple-element.24), channel_id=1, source_target_pairs={{0,3},{1,0},{2,1},{3,2},{4,7},{5,4},{6,5},{7,6},{8,11},{9,8},{10,9... | collective-permute-start | bytes 786440 | tf_op jit(solution)/shard_map/ppermute | solution.py:20
  51.1 2.9 %collective-permute-start.5 = (bf16[1792,128]{1,0:T(8,128)(2,1)S(1)}, bf16[1792,128]{1,0:T(8,128)(2,1)S(1)}, u32[]{:S(2)}, u32[]{:S(2)}) collective-permute-start(bf16[1792,128]{1,0:T(8,128)(2,1)S(1)} %slice.17), channel_id=1, source_target_pairs={{0,3},{1,0},{2,1},{3,2},{4,7},{5,4},{6,5},{7,6},{8,11},{9,8},{10,9... | collective-permute-start | bytes 1376264 | tf_op jit(solution)/shard_map/ppermute | solution.py:20
  54.0 2.5 %join_up_near.1.joined_hbm = bf16[896,1024]{1,0:T(8,128)(2,1)} custom-call(bf16[3584,256]{1,0:T(8,128)(2,1)} %bitcast.28, bf16[4352,128]{1,0:T(8,128)(2,1)} %copy-done.8, bf16[4352,128]{1,0:T(8,128)(2,1)} %copy-done.10), custom_call_target="tpu_custom_call" | custom-call | flops 8999999488 | bytes 2752512 | tf_op jit(solution)/shard_map/join_up_near/pallas_call | solution.py:199
  57.3 1.9 %join_up_far.1.weights_ref = bf16[896,1024]{1,0:T(8,128)(2,1)} custom-call(bf16[1792,128]{1,0:T(8,128)(2,1)} %copy-done.9, bf16[896,1024]{1,0:T(8,128)(2,1)} %join_up_near.1.joined_hbm), custom_call_target="tpu_custom_call", output_to_operand_aliasing={{}: (1, {})} | custom-call | tf_op jit(solution)/shard_map/join_up_far/pallas_call | solution.py:223
  59.2 10.3 %all-to-all-done.1.rows_ref = bf16[128,2,896]{2,1,0:T(2,128)(2,1)S(1)} async-done(((bf16[128,2,896]{2,1,0:T(2,128)(2,1)}), bf16[128,2,896]{2,1,0:T(2,128)(2,1)S(1)}, u32[]{:S(2)}, u32[]{:S(2)}) %all-to-all-start.1) | async-done | bytes 458784 | tf_op jit(solution)/shard_map/all_to_all | solution.py:548
  72.6 3.5 %all-to-all-start.2 = ((bf16[4,256,256]{2,1,0:T(8,128)(2,1)}), bf16[4,256,256]{2,1,0:T(8,128)(2,1)S(1)}, u32[]{:S(2)}, u32[]{:S(2)}) async-start(bf16[4,256,256]{2,1,0:T(8,128)(2,1)} %expert_up.1), calls=%async_computation.2 | async-start | bytes 1048576 | tf_op jit(solution)/shard_map/all_to_all | solution.py:28
  76.9 2.8 %join_down.1.weights_ref = bf16[1024,896]{1,0:T(8,128)(2,1)} custom-call(bf16[256,3584]{1,0:T(8,128)(2,1)} %bitcast.26, bf16[4352,128]{1,0:T(8,128)(2,1)} %copy-done.8, bf16[4352,128]{1,0:T(8,128)(2,1)} %copy-done.10, bf16[256,512]{1,0:T(8,128)(2,1)} %collective-permute-done.3.after_rest_hbm, bf16[256,512]{1,0:T(8,128)(2,1)} %collective-permute-done.4.before_rest_hbm, ...), custom_call_target="tpu_custom_call" | custom-call | flops 4000000000 | bytes 3670016 | tf_op jit(solution)/shard_map/join_down/pallas_call | solution.py:267
  79.7 3.9 %all-to-all-done.2.shares_hbm = bf16[4,256,256]{2,1,0:T(8,128)(2,1)S(1)} async-done(((bf16[4,256,256]{2,1,0:T(8,128)(2,1)}), bf16[4,256,256]{2,1,0:T(8,128)(2,1)S(1)}, u32[]{:S(2)}, u32[]{:S(2)}) %all-to-all-start.2) | async-done | bytes 524320 | tf_op jit(solution)/shard_map/all_to_all | solution.py:28
  85.3 10.6 %all_to_all.25.active_ref = bf16[4,272,256]{2,1,0:T(8,128)(2,1)S(1)} all-to-all(bf16[4,272,256]{2,1,0:T(8,128)(2,1)} %expert_silu.1), channel_id=1, replica_groups=mesh['dp'=128,'hg'=4] {'hg'}, dimensions={0} | all-to-all | bytes 1114112 | tf_op jit(solution)/shard_map/all_to_all | solution.py:28
  97.4 12.2 %all-to-all-start.4 = ((bf16[128,2,896]{2,1,0:T(2,128)(2,1)}), bf16[128,2,896]{2,1,0:T(2,128)(2,1)S(1)}, u32[]{:S(2)}, u32[]{:S(2)}) async-start(bf16[128,2,896]{2,1,0:T(2,128)(2,1)} %expert_down.1), calls=%async_computation.4 | async-start | bytes 917504 | tf_op jit(solution)/shard_map/all_to_all | solution.py:566
  110.3 2.2 %collective-permute-start.6 = (bf16[1,128,576]{1,2,0:T(8,128)(2,1)S(1)}, bf16[1,128,576]{1,2,0:T(8,128)(2,1)S(1)}, u32[]{:S(2)}, u32[]{:S(2)}) collective-permute-start(bf16[1,128,576]{1,2,0:T(8,128)(2,1)S(1)} %copy-done.11), channel_id=1, source_target_pairs={{0,1},{1,2},{2,3},{3,0},{4,5},{5,6},{6,7},{7,4},{8,9},{9,10},{10,1... | collective-permute-start | bytes 442376 | tf_op jit(solution)/shard_map/ppermute | solution.py:20
  112.5 3.7 %collective-permute-start.7 = (bf16[1,128,576]{1,2,0:T(8,128)(2,1)S(1)}, bf16[1,128,576]{1,2,0:T(8,128)(2,1)S(1)}, u32[]{:S(2)}, u32[]{:S(2)}) collective-permute-start(bf16[1,128,576]{1,2,0:T(8,128)(2,1)S(1)} %copy-done.11), channel_id=1, source_target_pairs={{0,2},{1,3},{2,0},{3,1},{4,6},{5,7},{6,4},{7,5},{8,10},{9,11},{10,... | collective-permute-start | bytes 442376 | tf_op jit(solution)/shard_map/ppermute | solution.py:20
  116.3 2.7 %collective-permute-start.8 = (bf16[1,128,576]{1,2,0:T(8,128)(2,1)S(1)}, bf16[1,128,576]{1,2,0:T(8,128)(2,1)S(1)}, u32[]{:S(2)}, u32[]{:S(2)}) collective-permute-start(bf16[1,128,576]{1,2,0:T(8,128)(2,1)S(1)} %copy-done.11), channel_id=1, source_target_pairs={{0,3},{1,0},{2,1},{3,2},{4,7},{5,4},{6,5},{7,6},{8,11},{9,8},{10,9... | collective-permute-start | bytes 442376 | tf_op jit(solution)/shard_map/ppermute | solution.py:20
  121.5 2.5 %collective-permute-done.8 = bf16[1,128,576]{1,2,0:T(8,128)(2,1)S(1)} collective-permute-done((bf16[1,128,576]{1,2,0:T(8,128)(2,1)S(1)}, bf16[1,128,576]{1,2,0:T(8,128)(2,1)S(1)}, u32[]{:S(2)}, u32[]{:S(2)}) %collective-permute-start.8) | collective-permute-done | bytes 147488 | tf_op jit(solution)/shard_map/ppermute | solution.py:20
  125.4 14.7 %all-to-all-done.4.returned_ref = bf16[128,2,896]{2,1,0:T(2,128)(2,1)S(1)} async-done(((bf16[128,2,896]{2,1,0:T(2,128)(2,1)}), bf16[128,2,896]{2,1,0:T(2,128)(2,1)S(1)}, u32[]{:S(2)}, u32[]{:S(2)}) %all-to-all-start.4) | async-done | bytes 458784 | tf_op jit(solution)/shard_map/all_to_all | solution.py:566
  (56 shorter events, 15.8 us)
Async XLA Ops:
  0.6 38.5 %copy-start = (bf16[3584,32]{0,1:T(8,128)(2,1)S(1)}, bf16[3584,32]{0,1:T(8,128)(2,1)}, u32[]{:S(2)}) copy-start(bf16[3584,32]{0,1:T(8,128)(2,1)} %param.16) | copy-start | bytes 688132
  2.4 14.2 %all-to-all-start = ((bf16[4,16,3584]{2,1,0:T(8,128)(2,1)}), bf16[4,16,3584]{2,1,0:T(8,128)(2,1)S(1)}, u32[]{:S(2)}, u32[]{:S(2)}) async-start(bf16[4,16,3584]{2,1,0:T(8,128)(2,1)} %broadcast_in_dim.26.earlier_ref), calls=%async_computation | async-start | bytes 917504 | tf_op jit(solution)/shard_map/all_to_all | solution.py:28
  7.2 9.4 %copy-start.4 = (bf16[16,3584]{1,0:T(8,128)(2,1)S(1)}, bf16[16,3584]{1,0:T(8,128)(2,1)}, u32[]{:S(2)}) copy-start(bf16[16,3584]{1,0:T(8,128)(2,1)} %residual_hbm.1) | copy-start | bytes 344068
  7.2 9.4 %copy-start.6 = (f32[3584]{0:T(1024)S(1)}, f32[3584]{0:T(1024)}, u32[]{:S(2)}) copy-start(f32[3584]{0:T(1024)} %gain_hbm.1) | copy-start | bytes 43012
  7.2 9.4 %copy-start.7 = (s32[16,8]{0,1:T(8,128)S(1)}, s32[16,8]{0,1:T(8,128)}, u32[]{:S(2)}) copy-start(s32[16,8]{0,1:T(8,128)} %param.17) | copy-start | bytes 1540
  10.1 30.1 %collective-permute-start = (bf16[4352,128]{1,0:T(8,128)(2,1)}, bf16[4352,128]{1,0:T(8,128)(2,1)S(1)}, u32[]{:S(2)}, u32[]{:S(2)}) collective-permute-start(bf16[4352,128]{1,0:T(8,128)(2,1)} %get-tuple-element.19), channel_id=1, source_target_pairs={{0,1},{1,2},{2,3},{3,0},{4,5},{5,6},{6,7},{7,4},{8,9},{9,10},{10,1... | collective-permute-start | bytes 3342344 | tf_op jit(solution)/shard_map/ppermute | solution.py:20
  13.5 37.6 %collective-permute-start.2 = (bf16[4352,128]{1,0:T(8,128)(2,1)}, bf16[4352,128]{1,0:T(8,128)(2,1)S(1)}, u32[]{:S(2)}, u32[]{:S(2)}) collective-permute-start(bf16[4352,128]{1,0:T(8,128)(2,1)} %get-tuple-element.20), channel_id=1, source_target_pairs={{0,3},{1,0},{2,1},{3,2},{4,7},{5,4},{6,5},{7,6},{8,11},{9,8},{10,9... | collective-permute-start | bytes 3342344 | tf_op jit(solution)/shard_map/ppermute | solution.py:20
  18.5 51.0 %all-to-all-start.1 = ((bf16[128,2,896]{2,1,0:T(2,128)(2,1)}), bf16[128,2,896]{2,1,0:T(2,128)(2,1)S(1)}, u32[]{:S(2)}, u32[]{:S(2)}) async-start(bf16[128,2,896]{2,1,0:T(2,128)(2,1)} %get-tuple-element.17), calls=%async_computation.1 | async-start | bytes 917504 | tf_op jit(solution)/shard_map/all_to_all | solution.py:548
  40.2 2.5 %copy-start.8 = (bf16[4352,128]{1,0:T(8,128)(2,1)}, bf16[4352,128]{1,0:T(8,128)(2,1)S(1)}, u32[]{:S(2)}) copy-start(bf16[4352,128]{1,0:T(8,128)(2,1)S(1)} %collective-permute-done.after_hbm.earlier_ref) | copy-start | bytes 3342340
  40.3 16.2 %collective-permute-start.1 = (bf16[1792,128]{1,0:T(8,128)(2,1)S(1)}, bf16[1792,128]{1,0:T(8,128)(2,1)S(1)}, u32[]{:S(2)}, u32[]{:S(2)}) collective-permute-start(bf16[1792,128]{1,0:T(8,128)(2,1)S(1)} %slice.16), channel_id=1, source_target_pairs={{0,1},{1,2},{2,3},{3,0},{4,5},{5,6},{6,7},{7,4},{8,9},{9,10},{10,1... | collective-permute-start | bytes 1376264 | tf_op jit(solution)/shard_map/ppermute | solution.py:20
  44.6 31.5 %collective-permute-start.3 = (bf16[256,512]{1,0:T(8,128)(2,1)}, bf16[256,512]{1,0:T(8,128)(2,1)}, u32[]{:S(2)}, u32[]{:S(2)}) collective-permute-start(bf16[256,512]{1,0:T(8,128)(2,1)} %get-tuple-element.23), channel_id=1, source_target_pairs={{0,1},{1,2},{2,3},{3,0},{4,5},{5,6},{6,7},{7,4},{8,9},{9,10},{10,1... | collective-permute-start | bytes 786440 | tf_op jit(solution)/shard_map/ppermute | solution.py:20
  47.7 28.4 %collective-permute-start.4 = (bf16[256,512]{1,0:T(8,128)(2,1)}, bf16[256,512]{1,0:T(8,128)(2,1)}, u32[]{:S(2)}, u32[]{:S(2)}) collective-permute-start(bf16[256,512]{1,0:T(8,128)(2,1)} %get-tuple-element.24), channel_id=1, source_target_pairs={{0,3},{1,0},{2,1},{3,2},{4,7},{5,4},{6,5},{7,6},{8,11},{9,8},{10,9... | collective-permute-start | bytes 786440 | tf_op jit(solution)/shard_map/ppermute | solution.py:20
  51.1 2.9 %copy-start.10 = (bf16[4352,128]{1,0:T(8,128)(2,1)}, bf16[4352,128]{1,0:T(8,128)(2,1)S(1)}, u32[]{:S(2)}) copy-start(bf16[4352,128]{1,0:T(8,128)(2,1)S(1)} %collective-permute-done.2.before_hbm) | copy-start | bytes 3342340
  51.1 25.0 %collective-permute-start.5 = (bf16[1792,128]{1,0:T(8,128)(2,1)S(1)}, bf16[1792,128]{1,0:T(8,128)(2,1)S(1)}, u32[]{:S(2)}, u32[]{:S(2)}) collective-permute-start(bf16[1792,128]{1,0:T(8,128)(2,1)S(1)} %slice.17), channel_id=1, source_target_pairs={{0,3},{1,0},{2,1},{3,2},{4,7},{5,4},{6,5},{7,6},{8,11},{9,8},{10,9... | collective-permute-start | bytes 1376264 | tf_op jit(solution)/shard_map/ppermute | solution.py:20
  72.6 11.0 %all-to-all-start.2 = ((bf16[4,256,256]{2,1,0:T(8,128)(2,1)}), bf16[4,256,256]{2,1,0:T(8,128)(2,1)S(1)}, u32[]{:S(2)}, u32[]{:S(2)}) async-start(bf16[4,256,256]{2,1,0:T(8,128)(2,1)} %expert_up.1), calls=%async_computation.2 | async-start | bytes 1048576 | tf_op jit(solution)/shard_map/all_to_all | solution.py:28
  79.7 16.2 %copy-start.2 = (bf16[1024,896]{1,0:T(8,128)(2,1)S(1)}, bf16[1024,896]{1,0:T(8,128)(2,1)}, u32[]{:S(2)}) copy-start(bf16[1024,896]{1,0:T(8,128)(2,1)} %join_down.1.weights_ref) | copy-start | bytes 5505028
  95.9 14.4 %copy-start.11 = (bf16[1,128,576]{1,2,0:T(8,128)(2,1)S(1)}, bf16[1,128,576]{1,2,0:T(8,128)(2,1)}, u32[]{:S(2)}) copy-start(bf16[1,128,576]{1,2,0:T(8,128)(2,1)} %param.11) | copy-start | bytes 442372
  97.4 26.6 %copy-start.12 = (bf16[1,32,576]{2,1,0:T(8,128)(2,1)S(1)}, bf16[1,32,576]{2,1,0:T(8,128)(2,1)}, u32[]{:S(2)}) copy-start(bf16[1,32,576]{2,1,0:T(8,128)(2,1)} %param.10) | copy-start | bytes 110596
  97.4 42.7 %copy-start.5 = (f32[16,896]{1,0:T(8,128)S(1)}, f32[16,896]{1,0:T(8,128)}, u32[]{:S(2)}) copy-start(f32[16,896]{1,0:T(8,128)} %get-tuple-element.31.hidden_hbm) | copy-start | bytes 172036
  97.4 42.7 %all-to-all-start.4 = ((bf16[128,2,896]{2,1,0:T(2,128)(2,1)}), bf16[128,2,896]{2,1,0:T(2,128)(2,1)S(1)}, u32[]{:S(2)}, u32[]{:S(2)}) async-start(bf16[128,2,896]{2,1,0:T(2,128)(2,1)} %expert_down.1), calls=%async_computation.4 | async-start | bytes 917504 | tf_op jit(solution)/shard_map/all_to_all | solution.py:566
  110.3 11.1 %collective-permute-start.6 = (bf16[1,128,576]{1,2,0:T(8,128)(2,1)S(1)}, bf16[1,128,576]{1,2,0:T(8,128)(2,1)S(1)}, u32[]{:S(2)}, u32[]{:S(2)}) collective-permute-start(bf16[1,128,576]{1,2,0:T(8,128)(2,1)S(1)} %copy-done.11), channel_id=1, source_target_pairs={{0,1},{1,2},{2,3},{3,0},{4,5},{5,6},{6,7},{7,4},{8,9},{9,10},{10,1... | collective-permute-start | bytes 442376 | tf_op jit(solution)/shard_map/ppermute | solution.py:20
  112.5 8.9 %collective-permute-start.7 = (bf16[1,128,576]{1,2,0:T(8,128)(2,1)S(1)}, bf16[1,128,576]{1,2,0:T(8,128)(2,1)S(1)}, u32[]{:S(2)}, u32[]{:S(2)}) collective-permute-start(bf16[1,128,576]{1,2,0:T(8,128)(2,1)S(1)} %copy-done.11), channel_id=1, source_target_pairs={{0,2},{1,3},{2,0},{3,1},{4,6},{5,7},{6,4},{7,5},{8,10},{9,11},{10,... | collective-permute-start | bytes 442376 | tf_op jit(solution)/shard_map/ppermute | solution.py:20
  116.3 7.7 %collective-permute-start.8 = (bf16[1,128,576]{1,2,0:T(8,128)(2,1)S(1)}, bf16[1,128,576]{1,2,0:T(8,128)(2,1)S(1)}, u32[]{:S(2)}, u32[]{:S(2)}) collective-permute-start(bf16[1,128,576]{1,2,0:T(8,128)(2,1)S(1)} %copy-done.11), channel_id=1, source_target_pairs={{0,3},{1,0},{2,1},{3,2},{4,7},{5,4},{6,5},{7,6},{8,11},{9,8},{10,9... | collective-permute-start | bytes 442376 | tf_op jit(solution)/shard_map/ppermute | solution.py:20
  121.4 18.7 %copy-start.3 = (bf16[256,16]{1,0:T(8,128)(2,1)S(1)}, bf16[256,16]{1,0:T(8,128)(2,1)}, u32[]{:S(2)}) copy-start(bf16[256,16]{1,0:T(8,128)(2,1)} %gates.1.gates_hbm) | copy-start | bytes 24580
  (3 other events, 3.1 us)

commit v4 on v3

--- a/solution.py
+++ b/solution.py
@@ -193,12 +193,12 @@
             sems,
         )
         wait_all(fetched)
-        wait_all(start_all([(ref, out_hbm.at[:, :3 * units])], sems, 5))
+        wait_all(start_all([(ref, out_hbm)], sems, 5))
 
     dtype = up_weights.dtype
     return pl.pallas_call(
         kernel,
-        out_shape=pltpu.HBM((part, size * units), dtype),
+        out_shape=pltpu.HBM((part, 3 * units), dtype),
         in_specs=[HBM] * 3,
         out_specs=HBM,
         scratch_shapes=[pltpu.VMEM((part, 3 * units), dtype), pltpu.SemaphoreType.DMA((6,))],
@@ -214,20 +214,19 @@
     part, width = joined.shape
     half = far.shape[1]
 
-    def kernel(far_hbm, joined_hbm, out_hbm, ref, sems):
-        wait_all(start_all(
-            [(far_hbm.at[i * part:(i + 1) * part, :], ref.at[:, i * half:(i + 1) * half]) for i in (0, 1)], sems
-        ))
-        wait_all(start_all([(ref, out_hbm.at[:, width - 2 * half:])], sems, 2))
-
-    return pl.pallas_call(
-        kernel,
-        out_shape=pltpu.HBM(joined.shape, joined.dtype),
-        in_specs=[HBM] * 2,
-        out_specs=HBM,
-        scratch_shapes=[pltpu.VMEM((part, 2 * half), joined.dtype), pltpu.SemaphoreType.DMA((3,))],
-        input_output_aliases={1: 0},
-        compiler_params=pltpu.CompilerParams(vmem_limit_bytes=WHOLE_VMEM),
+    def kernel(far_ref, joined_hbm, out_ref, sems):
+        fetched = start_all([(joined_hbm, out_ref.at[:, :width])], sems)
+        out_ref[:, width:width + half] = far_ref[:part, :]
+        out_ref[:, width + half:] = far_ref[part:, :]
+        wait_all(fetched)
+
+    return pl.pallas_call(
+        kernel,
+        out_shape=jax.ShapeDtypeStruct((part, width + 2 * half), joined.dtype),
+        in_specs=[VMEM, HBM],
+        out_specs=VMEM,
+        scratch_shapes=[pltpu.SemaphoreType.DMA((1,))],
+        compiler_params=pltpu.CompilerParams(vmem_limit_bytes=VMEM_LIMIT),
         name="join_up_far",
     )(far, joined)
 
@@ -450,29 +449,23 @@
     size, slots, units = shares.shape
     more = extra.shape[0]
 
-    def kernel(shares_hbm, extra_hbm, out_hbm, shares_ref, active_ref, sems):
-        copies = start_all(
-            [(shares_hbm.at[x], shares_ref.at[x]) for x in range(size)]
-            + [(extra_hbm, active_ref.at[slots:, :])],
-            sems,
-        )
-        total = jnp.zeros((slots, units), jnp.float32)
-        for x in range(size):
-            copies[x].wait()
+    def kernel(shares_ref, extra_hbm, out_hbm, active_ref, sems):
+        copies = start_all([(extra_hbm, active_ref.at[slots:, :])], sems)
+        total = shares_ref[0].astype(jnp.float32)
+        for x in range(1, size):
             total += shares_ref[x].astype(jnp.float32)
         active_ref[:slots, :] = (total / (1.0 + jnp.exp(-total))).astype(jnp.bfloat16)
-        copies[size].wait()
-        wait_all(start_all([(active_ref, out_hbm.at[x]) for x in range(size)], sems, size + 1))
+        wait_all(copies)
+        wait_all(start_all([(active_ref, out_hbm.at[x]) for x in range(size)], sems, 1))
 
     return pl.pallas_call(
         kernel,
         out_shape=pltpu.HBM((size, slots + more, units), jnp.bfloat16),
-        in_specs=[pl.BlockSpec(memory_space=pl.ANY)] * 2,
+        in_specs=[VMEM, pl.BlockSpec(memory_space=pl.ANY)],
         out_specs=HBM,
         scratch_shapes=[
-            pltpu.VMEM((size, slots, units), jnp.bfloat16),
             pltpu.VMEM((slots + more, units), jnp.bfloat16),
-            pltpu.SemaphoreType.DMA((2 * size + 1,)),
+            pltpu.SemaphoreType.DMA((size + 1,)),
         ],
         cost_estimate=pl.CostEstimate(
             flops=8 * slots * units,
@@ -539,12 +532,12 @@
     block = 2 * (feature_width // size)
     far_up = shift(after[block:2 * block], 1, size)
     far_down = shift(before[block:2 * block], size - 1, size)
-    next_rest, back_rest = rest_blocks(down_proj[0], after, size)
-    after_rest, before_rest = shift(next_rest, 1, size), shift(back_rest, size - 1, size)
-
     normed, hidden, route, outgoing = norm_and_route(
         exchange(copies), residual, norm_gain, expert_ids.T, experts, capacity
     )
+    next_rest, back_rest = rest_blocks(down_proj[0], normed, size)
+    next_rest, back_rest, before = lax.optimization_barrier((next_rest, back_rest, before))
+    after_rest, before_rest = shift(next_rest, 1, size), shift(back_rest, size - 1, size)
     arrived = lax.all_to_all(outgoing, "dp", split_axis=0, concat_axis=0, tiled=True)
 
     local_logits = jnp.dot(normed, router, preferred_element_type=jnp.float32)
@@ -555,7 +548,7 @@
     )
     up_all = join_up_near(up_proj[0], after, before, size)
     up_all = join_up_far(up_all, far_up)
-    arrived, extra, up_all = lax.optimization_barrier((arrived, extra, up_all))
+    arrived, up_all = lax.optimization_barrier((arrived, up_all))
     shares = exchange(expert_up(arrived, up_all))
 
     down_all = join_down(down_proj[0], after, before, after_rest, before_rest, far_down, size)

time: 142 us -> 139 us (0.979)
  Pallas kernels: 21.3 us -> 18.9 us
    pallas_call x2, Pallas kernels: 4.41 us -> 2.82 us  [the longest x1 2.49 us: join_up_near(): pl.pallas_call(kernel, out_shape=pltpu.HBM((part, 3 * units), dtype), in_...]
    unnamed x31 -> x29, local copies, waits for them, and re-layouts: 3.19 us -> 2.26 us
  transfers between devices with their start and end apart: 13 -> 13, of which waited for: 4 -> 4; matrix products, arithmetic and copies ran while one was open for 2% -> 3% of each run, Pallas kernels for 12% -> 11%
where the time goes in v4:
time: 139 us; the launch traced here: 138 us
  starting transfers between devices  66.9 us (48%)
  waiting for transfers between devices  32.5 us (23%)
  Pallas kernels  18.9 us (14%)
  blocking collectives  10.6 us (8%)
  local copies, waits for them, and re-layouts  5.76 us (4%)
  between operations  1.64 us (1%)
    ppermute x9, starting transfers between devices, shift(): lax.ppermute(value, 'hg', [(i, (i + distance) % size) for i in range(size)])  26.7 us
    all_to_all x1, starting transfers between devices, on_device(): lax.all_to_all(outgoing, 'dp', split_axis=0, concat_axis=0, tiled=True)  20.7 us
    all_to_all x1, waiting for transfers between devices, on_device(): lax.all_to_all(reduced, 'dp', split_axis=0, concat_axis=0, tiled=True)  14 us
    all_to_all x1, waiting for transfers between devices, on_device(): lax.all_to_all(outgoing, 'dp', split_axis=0, concat_axis=0, tiled=True)  11.3 us
    all_to_all x1, starting transfers between devices, on_device(): lax.all_to_all(reduced, 'dp', split_axis=0, concat_axis=0, tiled=True)  11.2 us
    all_to_all x1, blocking collectives, exchange(): return lax.all_to_all(value, 'hg', 0, 0, tiled=True)  10.6 us
    all_to_all x2, starting transfers between devices, exchange(): return lax.all_to_all(value, 'hg', 0, 0, tiled=True)  8.31 us
    all_to_all x2, waiting for transfers between devices, exchange(): return lax.all_to_all(value, 'hg', 0, 0, tiled=True)  3.83 us
  transfers between devices with their start and end apart: 13, of which 4 were waited for; matrix products, arithmetic and copies ran while one was open for 3% of the time, Pallas kernels for 11%

profile of v4, /device:TPU:1, one launch (start us, length us, event | category | flops | bytes accessed | tf_op | source)
XLA Modules:
  0.0 138.0 jit_solution(11640987419338895327)
XLA Ops:
  2.4 4.8 %all-to-all-start = ((bf16[4,16,3584]{2,1,0:T(8,128)(2,1)}), bf16[4,16,3584]{2,1,0:T(8,128)(2,1)S(1)}, u32[]{:S(2)}, u32[]{:S(2)}) async-start(bf16[4,16,3584]{2,1,0:T(8,128)(2,1)} %broadcast_in_dim.26.earlier_ref), calls=%async_computation | async-start | bytes 917504 | tf_op jit(solution)/shard_map/all_to_all | solution.py:28
  7.2 2.9 %pack_weights.1 = (bf16[4352,128]{1,0:T(8,128)(2,1)}, bf16[4352,128]{1,0:T(8,128)(2,1)}) custom-call(bf16[3584,256]{1,0:T(8,128)(2,1)} %bitcast.27, bf16[256,3584]{1,0:T(8,128)(2,1)} %bitcast.24, bf16[4,16,3584]{2,1,0:T(8,128)(2,1)} %broadcast_in_dim.26.earlier_ref), custom_call_target="tpu_custom_call" | custom-call | bytes 7340032 | tf_op jit(solution)/shard_map/pack_weights/pallas_call | solution.py:128
  10.1 3.4 %collective-permute-start = (bf16[4352,128]{1,0:T(8,128)(2,1)}, bf16[4352,128]{1,0:T(8,128)(2,1)S(1)}, u32[]{:S(2)}, u32[]{:S(2)}) collective-permute-start(bf16[4352,128]{1,0:T(8,128)(2,1)} %get-tuple-element.20), channel_id=1, source_target_pairs={{0,1},{1,2},{2,3},{3,0},{4,5},{5,6},{6,7},{7,4},{8,9},{9,10},{10,1... | collective-permute-start | bytes 3342344 | tf_op jit(solution)/shard_map/ppermute | solution.py:20
  13.5 3.1 %collective-permute-start.2 = (bf16[4352,128]{1,0:T(8,128)(2,1)}, bf16[4352,128]{1,0:T(8,128)(2,1)}, u32[]{:S(2)}, u32[]{:S(2)}) collective-permute-start(bf16[4352,128]{1,0:T(8,128)(2,1)} %get-tuple-element.24), channel_id=1, source_target_pairs={{0,3},{1,0},{2,1},{3,2},{4,7},{5,4},{6,5},{7,6},{8,11},{9,8},{10,9... | collective-permute-start | bytes 3342344 | tf_op jit(solution)/shard_map/ppermute | solution.py:20
  16.7 1.8 %norm_and_route.1 = (bf16[16,3584]{1,0:T(8,128)(2,1)}, f32[16,896]{1,0:T(8,128)}, bf16[256,16]{1,0:T(8,128)(2,1)}, bf16[128,2,896]{2,1,0:T(2,128)(2,1)}) custom-call(bf16[4,16,3584]{2,1,0:T(8,128)(2,1)S(1)} %all-to-all-done.copies_ref, bf16[16,3584]{1,0:T(8,128)(2,1)S(1)} %copy-done.4, f32[3584]{0:T(1024)S(1)} %copy-done.6, s32[8,16]{1,0:T(8,128)S(1)} %bitcast.23), custom_call_target="tpu_custom_call" | custom-call | flops 7340032 | bytes 1146880 | tf_op jit(solution)/shard_map/norm_and_route/pallas_call | solution.py:341
  18.5 20.7 %all-to-all-start.1 = ((bf16[128,2,896]{2,1,0:T(2,128)(2,1)}), bf16[128,2,896]{2,1,0:T(2,128)(2,1)S(1)}, u32[]{:S(2)}, u32[]{:S(2)}) async-start(bf16[128,2,896]{2,1,0:T(2,128)(2,1)} %get-tuple-element.19), calls=%async_computation.1 | async-start | bytes 917504 | tf_op jit(solution)/shard_map/all_to_all | solution.py:541
  39.2 1.8 %rest_blocks.1 = (bf16[256,512]{1,0:T(8,128)(2,1)}, bf16[256,512]{1,0:T(8,128)(2,1)}) custom-call(bf16[256,3584]{1,0:T(8,128)(2,1)} %bitcast.25, bf16[16,3584]{1,0:T(8,128)(2,1)} %get-tuple-element.21.earlier_ref), custom_call_target="tpu_custom_call" | custom-call | tf_op jit(solution)/shard_map/rest_blocks/pallas_call | solution.py:169
  41.3 2.4 %collective-permute-start.1 = (bf16[1792,128]{1,0:T(8,128)(2,1)S(1)}, bf16[1792,128]{1,0:T(8,128)(2,1)S(1)}, u32[]{:S(2)}, u32[]{:S(2)}) collective-permute-start(bf16[1792,128]{1,0:T(8,128)(2,1)S(1)} %slice.16), channel_id=1, source_target_pairs={{0,1},{1,2},{2,3},{3,0},{4,5},{5,6},{6,7},{7,4},{8,9},{9,10},{10,1... | collective-permute-start | bytes 1376264 | tf_op jit(solution)/shard_map/ppermute | solution.py:20
  43.7 3.1 %collective-permute-start.3 = (bf16[256,512]{1,0:T(8,128)(2,1)}, bf16[256,512]{1,0:T(8,128)(2,1)}, u32[]{:S(2)}, u32[]{:S(2)}) collective-permute-start(bf16[256,512]{1,0:T(8,128)(2,1)} %get-tuple-element.28), channel_id=1, source_target_pairs={{0,1},{1,2},{2,3},{3,0},{4,5},{5,6},{6,7},{7,4},{8,9},{9,10},{10,1... | collective-permute-start | bytes 786440 | tf_op jit(solution)/shard_map/ppermute | solution.py:20
  46.8 3.4 %collective-permute-start.4 = (bf16[256,512]{1,0:T(8,128)(2,1)}, bf16[256,512]{1,0:T(8,128)(2,1)}, u32[]{:S(2)}, u32[]{:S(2)}) collective-permute-start(bf16[256,512]{1,0:T(8,128)(2,1)} %get-tuple-element.29), channel_id=1, source_target_pairs={{0,3},{1,0},{2,1},{3,2},{4,7},{5,4},{6,5},{7,6},{8,11},{9,8},{10,9... | collective-permute-start | bytes 786440 | tf_op jit(solution)/shard_map/ppermute | solution.py:20
  51.3 2.9 %collective-permute-start.5 = (bf16[1792,128]{1,0:T(8,128)(2,1)S(1)}, bf16[1792,128]{1,0:T(8,128)(2,1)S(1)}, u32[]{:S(2)}, u32[]{:S(2)}) collective-permute-start(bf16[1792,128]{1,0:T(8,128)(2,1)S(1)} %slice.17), channel_id=1, source_target_pairs={{0,3},{1,0},{2,1},{3,2},{4,7},{5,4},{6,5},{7,6},{8,11},{9,8},{10,9... | collective-permute-start | bytes 1376264 | tf_op jit(solution)/shard_map/ppermute | solution.py:20
  54.2 2.5 %join_up_near.1.joined_hbm = bf16[896,768]{1,0:T(8,128)(2,1)} custom-call(bf16[3584,256]{1,0:T(8,128)(2,1)} %bitcast.28, bf16[4352,128]{1,0:T(8,128)(2,1)} %copy-done.9, bf16[4352,128]{1,0:T(8,128)(2,1)} %collective-permute-done.2.before_hbm), custom_call_target="tpu_custom_call" | custom-call | flops 8999999488 | bytes 2752512 | tf_op jit(solution)/shard_map/join_up_near/pallas_call | solution.py:199
  58.3 11.3 %all-to-all-done.1.rows_ref = bf16[128,2,896]{2,1,0:T(2,128)(2,1)S(1)} async-done(((bf16[128,2,896]{2,1,0:T(2,128)(2,1)}), bf16[128,2,896]{2,1,0:T(2,128)(2,1)S(1)}, u32[]{:S(2)}, u32[]{:S(2)}) %all-to-all-start.1) | async-done | bytes 458784 | tf_op jit(solution)/shard_map/all_to_all | solution.py:541
  71.2 3.5 %all-to-all-start.2 = ((bf16[4,256,256]{2,1,0:T(8,128)(2,1)}), bf16[4,256,256]{2,1,0:T(8,128)(2,1)S(1)}, u32[]{:S(2)}, u32[]{:S(2)}) async-start(bf16[4,256,256]{2,1,0:T(8,128)(2,1)} %expert_up.1), calls=%async_computation.2 | async-start | bytes 1048576 | tf_op jit(solution)/shard_map/all_to_all | solution.py:28
  75.6 2.8 %join_down.1.weights_ref = bf16[1024,896]{1,0:T(8,128)(2,1)} custom-call(bf16[256,3584]{1,0:T(8,128)(2,1)} %bitcast.26, bf16[4352,128]{1,0:T(8,128)(2,1)} %copy-done.9, bf16[4352,128]{1,0:T(8,128)(2,1)} %collective-permute-done.2.before_hbm, bf16[256,512]{1,0:T(8,128)(2,1)} %collective-permute-done.3.after_rest_hbm, ...), custom_call_target="tpu_custom_call" | custom-call | flops 4000000000 | bytes 3670016 | tf_op jit(solution)/shard_map/join_down/pallas_call | solution.py:266
  78.4 3.8 %all-to-all-done.2.shares_ref = bf16[4,256,256]{2,1,0:T(8,128)(2,1)S(1)} async-done(((bf16[4,256,256]{2,1,0:T(8,128)(2,1)}), bf16[4,256,256]{2,1,0:T(8,128)(2,1)S(1)}, u32[]{:S(2)}, u32[]{:S(2)}) %all-to-all-start.2) | async-done | bytes 524320 | tf_op jit(solution)/shard_map/all_to_all | solution.py:28
  83.2 10.6 %all_to_all.25.active_ref = bf16[4,272,256]{2,1,0:T(8,128)(2,1)S(1)} all-to-all(bf16[4,272,256]{2,1,0:T(8,128)(2,1)} %expert_silu.1), channel_id=1, replica_groups=mesh['dp'=128,'hg'=4] {'hg'}, dimensions={0} | all-to-all | bytes 1114112 | tf_op jit(solution)/shard_map/all_to_all | solution.py:28
  95.3 11.2 %all-to-all-start.4 = ((bf16[128,2,896]{2,1,0:T(2,128)(2,1)}), bf16[128,2,896]{2,1,0:T(2,128)(2,1)S(1)}, u32[]{:S(2)}, u32[]{:S(2)}) async-start(bf16[128,2,896]{2,1,0:T(2,128)(2,1)} %expert_down.1), calls=%async_computation.4 | async-start | bytes 917504 | tf_op jit(solution)/shard_map/all_to_all | solution.py:559
  107.2 2.2 %collective-permute-start.6 = (bf16[1,128,576]{1,2,0:T(8,128)(2,1)S(1)}, bf16[1,128,576]{1,2,0:T(8,128)(2,1)S(1)}, u32[]{:S(2)}, u32[]{:S(2)}) collective-permute-start(bf16[1,128,576]{1,2,0:T(8,128)(2,1)S(1)} %copy-done.10), channel_id=1, source_target_pairs={{0,1},{1,2},{2,3},{3,0},{4,5},{5,6},{6,7},{7,4},{8,9},{9,10},{10,1... | collective-permute-start | bytes 442376 | tf_op jit(solution)/shard_map/ppermute | solution.py:20
  109.4 4.3 %collective-permute-start.8 = (bf16[1,128,576]{1,2,0:T(8,128)(2,1)S(1)}, bf16[1,128,576]{1,2,0:T(8,128)(2,1)S(1)}, u32[]{:S(2)}, u32[]{:S(2)}) collective-permute-start(bf16[1,128,576]{1,2,0:T(8,128)(2,1)S(1)} %copy-done.10), channel_id=1, source_target_pairs={{0,3},{1,0},{2,1},{3,2},{4,7},{5,4},{6,5},{7,6},{8,11},{9,8},{10,9... | collective-permute-start | bytes 442376 | tf_op jit(solution)/shard_map/ppermute | solution.py:20
  113.7 1.9 %collective-permute-start.7 = (bf16[1,128,576]{1,2,0:T(8,128)(2,1)S(1)}, bf16[1,128,576]{1,2,0:T(8,128)(2,1)S(1)}, u32[]{:S(2)}, u32[]{:S(2)}) collective-permute-start(bf16[1,128,576]{1,2,0:T(8,128)(2,1)S(1)} %copy-done.10), channel_id=1, source_target_pairs={{0,2},{1,3},{2,0},{3,1},{4,6},{5,7},{6,4},{7,5},{8,10},{9,11},{10,... | collective-permute-start | bytes 442376 | tf_op jit(solution)/shard_map/ppermute | solution.py:20
  116.3 1.8 %gates.1.gates_hbm = bf16[256,16]{1,0:T(8,128)(2,1)} custom-call(bf16[4,16,256]{2,1,0:T(8,128)(2,1)} %slice.19.parts_ref, bf16[256,16]{1,0:T(8,128)(2,1)} %get-tuple-element.33.route_ref), custom_call_target="tpu_custom_call" | custom-call | tf_op jit(solution)/shard_map/gates/pallas_call | solution.py:386
  118.1 3.3 %collective-permute-done.7 = bf16[1,128,576]{1,2,0:T(8,128)(2,1)S(1)} collective-permute-done((bf16[1,128,576]{1,2,0:T(8,128)(2,1)S(1)}, bf16[1,128,576]{1,2,0:T(8,128)(2,1)S(1)}, u32[]{:S(2)}, u32[]{:S(2)}) %collective-permute-start.7) | collective-permute-done | bytes 147488 | tf_op jit(solution)/shard_map/ppermute | solution.py:20
  122.9 14.0 %all-to-all-done.4.returned_ref = bf16[128,2,896]{2,1,0:T(2,128)(2,1)S(1)} async-done(((bf16[128,2,896]{2,1,0:T(2,128)(2,1)}), bf16[128,2,896]{2,1,0:T(2,128)(2,1)S(1)}, u32[]{:S(2)}, u32[]{:S(2)}) %all-to-all-start.4) | async-done | bytes 458784 | tf_op jit(solution)/shard_map/all_to_all | solution.py:559
  (54 shorter events, 12.8 us)
Async XLA Ops:
  0.6 40.4 %copy-start = (bf16[3584,32]{0,1:T(8,128)(2,1)S(1)}, bf16[3584,32]{0,1:T(8,128)(2,1)}, u32[]{:S(2)}) copy-start(bf16[3584,32]{0,1:T(8,128)(2,1)} %param.16) | copy-start | bytes 688132
  2.4 14.2 %all-to-all-start = ((bf16[4,16,3584]{2,1,0:T(8,128)(2,1)}), bf16[4,16,3584]{2,1,0:T(8,128)(2,1)S(1)}, u32[]{:S(2)}, u32[]{:S(2)}) async-start(bf16[4,16,3584]{2,1,0:T(8,128)(2,1)} %broadcast_in_dim.26.earlier_ref), calls=%async_computation | async-start | bytes 917504 | tf_op jit(solution)/shard_map/all_to_all | solution.py:28
  7.2 9.4 %copy-start.4 = (bf16[16,3584]{1,0:T(8,128)(2,1)S(1)}, bf16[16,3584]{1,0:T(8,128)(2,1)}, u32[]{:S(2)}) copy-start(bf16[16,3584]{1,0:T(8,128)(2,1)} %residual_hbm.1) | copy-start | bytes 344068
  7.2 9.4 %copy-start.6 = (f32[3584]{0:T(1024)S(1)}, f32[3584]{0:T(1024)}, u32[]{:S(2)}) copy-start(f32[3584]{0:T(1024)} %gain_hbm.1) | copy-start | bytes 43012
  7.2 9.4 %copy-start.7 = (s32[16,8]{0,1:T(8,128)S(1)}, s32[16,8]{0,1:T(8,128)}, u32[]{:S(2)}) copy-start(s32[16,8]{0,1:T(8,128)} %param.17) | copy-start | bytes 1540
  10.1 31.1 %collective-permute-start = (bf16[4352,128]{1,0:T(8,128)(2,1)}, bf16[4352,128]{1,0:T(8,128)(2,1)S(1)}, u32[]{:S(2)}, u32[]{:S(2)}) collective-permute-start(bf16[4352,128]{1,0:T(8,128)(2,1)} %get-tuple-element.20), channel_id=1, source_target_pairs={{0,1},{1,2},{2,3},{3,0},{4,5},{5,6},{6,7},{7,4},{8,9},{9,10},{10,1... | collective-permute-start | bytes 3342344 | tf_op jit(solution)/shard_map/ppermute | solution.py:20
  13.5 30.2 %collective-permute-start.2 = (bf16[4352,128]{1,0:T(8,128)(2,1)}, bf16[4352,128]{1,0:T(8,128)(2,1)}, u32[]{:S(2)}, u32[]{:S(2)}) collective-permute-start(bf16[4352,128]{1,0:T(8,128)(2,1)} %get-tuple-element.24), channel_id=1, source_target_pairs={{0,3},{1,0},{2,1},{3,2},{4,7},{5,4},{6,5},{7,6},{8,11},{9,8},{10,9... | collective-permute-start | bytes 3342344 | tf_op jit(solution)/shard_map/ppermute | solution.py:20
  18.5 22.5 %copy-start.8 = (bf16[16,3584]{1,0:T(8,128)(2,1)S(1)}, bf16[16,3584]{1,0:T(8,128)(2,1)}, u32[]{:S(2)}) copy-start(bf16[16,3584]{1,0:T(8,128)(2,1)} %get-tuple-element.21.earlier_ref) | copy-start | bytes 344068
  18.5 51.2 %all-to-all-start.1 = ((bf16[128,2,896]{2,1,0:T(2,128)(2,1)}), bf16[128,2,896]{2,1,0:T(2,128)(2,1)S(1)}, u32[]{:S(2)}, u32[]{:S(2)}) async-start(bf16[128,2,896]{2,1,0:T(2,128)(2,1)} %get-tuple-element.19), calls=%async_computation.1 | async-start | bytes 917504 | tf_op jit(solution)/shard_map/all_to_all | solution.py:541
  41.2 12.9 %copy-start.9 = (bf16[4352,128]{1,0:T(8,128)(2,1)}, bf16[4352,128]{1,0:T(8,128)(2,1)S(1)}, u32[]{:S(2)}) copy-start(bf16[4352,128]{1,0:T(8,128)(2,1)S(1)} %collective-permute-done.after_hbm) | copy-start | bytes 3342340
  41.3 15.4 %collective-permute-start.1 = (bf16[1792,128]{1,0:T(8,128)(2,1)S(1)}, bf16[1792,128]{1,0:T(8,128)(2,1)S(1)}, u32[]{:S(2)}, u32[]{:S(2)}) collective-permute-start(bf16[1792,128]{1,0:T(8,128)(2,1)S(1)} %slice.16), channel_id=1, source_target_pairs={{0,1},{1,2},{2,3},{3,0},{4,5},{5,6},{6,7},{7,4},{8,9},{9,10},{10,1... | collective-permute-start | bytes 1376264 | tf_op jit(solution)/shard_map/ppermute | solution.py:20
  43.7 31.0 %collective-permute-start.3 = (bf16[256,512]{1,0:T(8,128)(2,1)}, bf16[256,512]{1,0:T(8,128)(2,1)}, u32[]{:S(2)}, u32[]{:S(2)}) collective-permute-start(bf16[256,512]{1,0:T(8,128)(2,1)} %get-tuple-element.28), channel_id=1, source_target_pairs={{0,1},{1,2},{2,3},{3,0},{4,5},{5,6},{6,7},{7,4},{8,9},{9,10},{10,1... | collective-permute-start | bytes 786440 | tf_op jit(solution)/shard_map/ppermute | solution.py:20
  46.8 27.9 %collective-permute-start.4 = (bf16[256,512]{1,0:T(8,128)(2,1)}, bf16[256,512]{1,0:T(8,128)(2,1)}, u32[]{:S(2)}, u32[]{:S(2)}) collective-permute-start(bf16[256,512]{1,0:T(8,128)(2,1)} %get-tuple-element.29), channel_id=1, source_target_pairs={{0,3},{1,0},{2,1},{3,2},{4,7},{5,4},{6,5},{7,6},{8,11},{9,8},{10,9... | collective-permute-start | bytes 786440 | tf_op jit(solution)/shard_map/ppermute | solution.py:20
  51.3 23.5 %collective-permute-start.5 = (bf16[1792,128]{1,0:T(8,128)(2,1)S(1)}, bf16[1792,128]{1,0:T(8,128)(2,1)S(1)}, u32[]{:S(2)}, u32[]{:S(2)}) collective-permute-start(bf16[1792,128]{1,0:T(8,128)(2,1)S(1)} %slice.17), channel_id=1, source_target_pairs={{0,3},{1,0},{2,1},{3,2},{4,7},{5,4},{6,5},{7,6},{8,11},{9,8},{10,9... | collective-permute-start | bytes 1376264 | tf_op jit(solution)/shard_map/ppermute | solution.py:20
  71.2 11.0 %all-to-all-start.2 = ((bf16[4,256,256]{2,1,0:T(8,128)(2,1)}), bf16[4,256,256]{2,1,0:T(8,128)(2,1)S(1)}, u32[]{:S(2)}, u32[]{:S(2)}) async-start(bf16[4,256,256]{2,1,0:T(8,128)(2,1)} %expert_up.1), calls=%async_computation.2 | async-start | bytes 1048576 | tf_op jit(solution)/shard_map/all_to_all | solution.py:28
  78.4 15.4 %copy-start.1 = (bf16[1024,896]{1,0:T(8,128)(2,1)S(1)}, bf16[1024,896]{1,0:T(8,128)(2,1)}, u32[]{:S(2)}) copy-start(bf16[1024,896]{1,0:T(8,128)(2,1)} %join_down.1.weights_ref) | copy-start | bytes 5505028
  93.8 13.4 %copy-start.10 = (bf16[1,128,576]{1,2,0:T(8,128)(2,1)S(1)}, bf16[1,128,576]{1,2,0:T(8,128)(2,1)}, u32[]{:S(2)}) copy-start(bf16[1,128,576]{1,2,0:T(8,128)(2,1)} %param.11) | copy-start | bytes 442372
  95.3 26.2 %copy-start.11 = (bf16[1,32,576]{2,1,0:T(8,128)(2,1)S(1)}, bf16[1,32,576]{2,1,0:T(8,128)(2,1)}, u32[]{:S(2)}) copy-start(bf16[1,32,576]{2,1,0:T(8,128)(2,1)} %param.10) | copy-start | bytes 110596
  95.3 41.7 %all-to-all-start.4 = ((bf16[128,2,896]{2,1,0:T(2,128)(2,1)}), bf16[128,2,896]{2,1,0:T(2,128)(2,1)S(1)}, u32[]{:S(2)}, u32[]{:S(2)}) async-start(bf16[128,2,896]{2,1,0:T(2,128)(2,1)} %expert_down.1), calls=%async_computation.4 | async-start | bytes 917504 | tf_op jit(solution)/shard_map/all_to_all | solution.py:559
  107.2 10.9 %collective-permute-start.6 = (bf16[1,128,576]{1,2,0:T(8,128)(2,1)S(1)}, bf16[1,128,576]{1,2,0:T(8,128)(2,1)S(1)}, u32[]{:S(2)}, u32[]{:S(2)}) collective-permute-start(bf16[1,128,576]{1,2,0:T(8,128)(2,1)S(1)} %copy-done.10), channel_id=1, source_target_pairs={{0,1},{1,2},{2,3},{3,0},{4,5},{5,6},{6,7},{7,4},{8,9},{9,10},{10,1... | collective-permute-start | bytes 442376 | tf_op jit(solution)/shard_map/ppermute | solution.py:20
  109.4 12.0 %collective-permute-start.8 = (bf16[1,128,576]{1,2,0:T(8,128)(2,1)S(1)}, bf16[1,128,576]{1,2,0:T(8,128)(2,1)S(1)}, u32[]{:S(2)}, u32[]{:S(2)}) collective-permute-start(bf16[1,128,576]{1,2,0:T(8,128)(2,1)S(1)} %copy-done.10), channel_id=1, source_target_pairs={{0,3},{1,0},{2,1},{3,2},{4,7},{5,4},{6,5},{7,6},{8,11},{9,8},{10,9... | collective-permute-start | bytes 442376 | tf_op jit(solution)/shard_map/ppermute | solution.py:20
  113.7 7.7 %collective-permute-start.7 = (bf16[1,128,576]{1,2,0:T(8,128)(2,1)S(1)}, bf16[1,128,576]{1,2,0:T(8,128)(2,1)S(1)}, u32[]{:S(2)}, u32[]{:S(2)}) collective-permute-start(bf16[1,128,576]{1,2,0:T(8,128)(2,1)S(1)} %copy-done.10), channel_id=1, source_target_pairs={{0,2},{1,3},{2,0},{3,1},{4,6},{5,7},{6,4},{7,5},{8,10},{9,11},{10,... | collective-permute-start | bytes 442376 | tf_op jit(solution)/shard_map/ppermute | solution.py:20
  115.7 21.3 %copy-start.5 = (f32[16,896]{1,0:T(8,128)S(1)}, f32[16,896]{1,0:T(8,128)}, u32[]{:S(2)}) copy-start(f32[16,896]{1,0:T(8,128)} %get-tuple-element.35.hidden_hbm) | copy-start | bytes 172036
  118.1 18.9 %copy-start.3 = (bf16[256,16]{1,0:T(8,128)(2,1)S(1)}, bf16[256,16]{1,0:T(8,128)(2,1)}, u32[]{:S(2)}) copy-start(bf16[256,16]{1,0:T(8,128)(2,1)} %gates.1.gates_hbm) | copy-start | bytes 24580
  (2 other events, 2.1 us)

commit v5 on v4

--- a/solution.py
+++ b/solution.py
@@ -289,13 +289,9 @@
     top = choices.shape[0]
 
     def kernel(
-        copies_ref, residual_hbm, gain_hbm, choices_hbm, normed_hbm, hidden_hbm, route_hbm, out_hbm,
-        residual_ref, gain_ref, choices_ref, hidden_ref, normed_ref, route_ref, out_ref, sems,
+        copies_ref, residual_ref, gain_ref, choices_ref, normed_hbm, hidden_hbm, route_hbm, out_hbm,
+        hidden_ref, normed_ref, route_ref, out_ref, sems,
     ):
-        fetched = start_all(
-            [(choices_hbm, choices_ref), (residual_hbm, residual_ref), (gain_hbm, gain_ref)], sems, 4
-        )
-        fetched[0].wait()
         expert = lax.div(lax.broadcasted_iota(jnp.int32, (slots, rows), 0), capacity)
         slot = lax.broadcasted_iota(jnp.int32, (slots, rows), 0) - expert * capacity
         hits = jnp.zeros((slots, rows), jnp.float32)
@@ -311,7 +307,6 @@
         route = jnp.where(earlier == slot.astype(jnp.float32), hits, 0.0).astype(jnp.bfloat16)
         route_ref[...] = route
 
-        wait_all(fetched[1:])
         hidden = residual_ref[...].astype(jnp.float32)
         for x in range(size):
             hidden += copies_ref[x].astype(jnp.float32)
@@ -319,18 +314,13 @@
         scale = lax.rsqrt(jnp.mean(hidden * hidden, axis=1, keepdims=True) + NORM_EPS)
         normed_ref[...] = (hidden * scale * gain_ref[...][None, :]).astype(jnp.bfloat16)
         mine = pl.ds(place(0, size, part), part)
+        outs = start_all(
+            [(normed_ref, normed_hbm), (hidden_ref.at[:, mine], hidden_hbm), (route_ref, route_hbm)], sems
+        )
         out_ref[...] = jnp.dot(
             route, normed_ref[:, mine], preferred_element_type=jnp.float32
         ).astype(jnp.bfloat16).reshape(experts, capacity, part)
-        wait_all(start_all(
-            [
-                (out_ref, out_hbm),
-                (normed_ref, normed_hbm),
-                (hidden_ref.at[:, mine], hidden_hbm),
-                (route_ref, route_hbm),
-            ],
-            sems,
-        ))
+        wait_all(outs + start_all([(out_ref, out_hbm)], sems, 3))
 
     shapes = [
         ((rows, features), jnp.bfloat16),
@@ -341,17 +331,13 @@
     return pl.pallas_call(
         kernel,
         out_shape=[pltpu.HBM(*shape) for shape in shapes],
-        in_specs=[VMEM, HBM, HBM, HBM],
         out_specs=[HBM] * 4,
         scratch_shapes=[
-            pltpu.VMEM(residual.shape, residual.dtype),
-            pltpu.VMEM(gain.shape, gain.dtype),
-            pltpu.VMEM(choices.shape, choices.dtype),
             pltpu.VMEM((rows, features), jnp.float32),
             pltpu.VMEM((rows, features), jnp.bfloat16),
             pltpu.VMEM((slots, rows), jnp.bfloat16),
             pltpu.VMEM((experts, capacity, part), jnp.bfloat16),
-            pltpu.SemaphoreType.DMA((7,)),
+            pltpu.SemaphoreType.DMA((4,)),
         ],
         cost_estimate=pl.CostEstimate(
             flops=2 * slots * rows * part,
@@ -423,18 +409,26 @@
     slots = experts * capacity
     units = weights.shape[1] // size
 
-    def kernel(rows_ref, weights_ref, out_ref):
+    def kernel(rows_ref, weights_ref, out_hbm, out_ref, sems):
         me = lax.axis_index("hg")
         rows = rows_ref[...].reshape(slots, part)
+        outs = []
         for i, d in enumerate(ORDER):
-            out_ref[lax.rem(me + size - d, size)] = jnp.dot(
+            out_ref[i] = jnp.dot(
                 rows, weights_ref[:, i * units:(i + 1) * units],
                 preferred_element_type=jnp.float32,
             ).astype(jnp.bfloat16)
-
-    return pl.pallas_call(
-        kernel,
-        out_shape=jax.ShapeDtypeStruct((size, slots, units), jnp.bfloat16),
+            outs += start_all([(out_ref.at[i], out_hbm.at[lax.rem(me + size - d, size)])], sems, i)
+        wait_all(outs)
+
+    return pl.pallas_call(
+        kernel,
+        out_shape=pltpu.HBM((size, slots, units), jnp.bfloat16),
+        in_specs=[VMEM, VMEM],
+        out_specs=HBM,
+        scratch_shapes=[
+            pltpu.VMEM((size, slots, units), jnp.bfloat16), pltpu.SemaphoreType.DMA((size,))
+        ],
         cost_estimate=pl.CostEstimate(
             flops=2 * slots * size * part * units,
             bytes_accessed=2 * (slots * part + size * part * units + size * slots * units),
@@ -482,20 +476,33 @@
     part = weights.shape[1]
     slots = experts * capacity
 
-    def kernel(active_ref, weights_ref, out_ref):
+    cut = experts // 2
+
+    def kernel(active_ref, weights_ref, out_hbm, out_ref, sems):
         me = lax.axis_index("hg")
-        total = jnp.zeros((slots, part), jnp.float32)
-        for i, d in enumerate(ORDER):
-            total += jnp.dot(
-                active_ref[lax.rem(me + size - d, size), :slots, :],
-                weights_ref[i * units:(i + 1) * units, :],
-                preferred_element_type=jnp.float32,
-            )
-        out_ref[...] = total.astype(jnp.bfloat16).reshape(experts, capacity, part)
-
-    return pl.pallas_call(
-        kernel,
-        out_shape=jax.ShapeDtypeStruct((experts, capacity, part), jnp.bfloat16),
+        outs = []
+        for half in (0, 1):
+            rows = slice(half * cut * capacity, (half + 1) * cut * capacity)
+            total = jnp.zeros((cut * capacity, part), jnp.float32)
+            for i, d in enumerate(ORDER):
+                total += jnp.dot(
+                    active_ref[lax.rem(me + size - d, size), rows, :],
+                    weights_ref[i * units:(i + 1) * units, :],
+                    preferred_element_type=jnp.float32,
+                )
+            some = slice(half * cut, (half + 1) * cut)
+            out_ref[some] = total.astype(jnp.bfloat16).reshape(cut, capacity, part)
+            outs += start_all([(out_ref.at[some], out_hbm.at[some])], sems, half)
+        wait_all(outs)
+
+    return pl.pallas_call(
+        kernel,
+        out_shape=pltpu.HBM((experts, capacity, part), jnp.bfloat16),
+        in_specs=[VMEM, VMEM],
+        out_specs=HBM,
+        scratch_shapes=[
+            pltpu.VMEM((experts, capacity, part), jnp.bfloat16), pltpu.SemaphoreType.DMA((2,))
+        ],
         cost_estimate=pl.CostEstimate(
             flops=2 * slots * size * part * units,
             bytes_accessed=2 * (slots * size * units + size * part * units + slots * part),

time: 139 us -> 138 us (level)
  no operation moved by 1% of the time
where the time goes in v5:
time: 138 us; the launch traced here: 137 us
  starting transfers between devices  66.8 us (48%)
  waiting for transfers between devices  33.2 us (24%)
  Pallas kernels  18.3 us (13%)
  blocking collectives  10.6 us (8%)
  local copies, waits for them, and re-layouts  4.99 us (4%)
  between operations  1.67 us (1%)
    ppermute x9, starting transfers between devices, shift(): lax.ppermute(value, 'hg', [(i, (i + distance) % size) for i in range(size)])  26.7 us
    all_to_all x1, starting transfers between devices, on_device(): lax.all_to_all(outgoing, 'dp', split_axis=0, concat_axis=0, tiled=True)  20.7 us
    all_to_all x1, waiting for transfers between devices, on_device(): lax.all_to_all(reduced, 'dp', split_axis=0, concat_axis=0, tiled=True)  14 us
    all_to_all x1, waiting for transfers between devices, on_device(): lax.all_to_all(outgoing, 'dp', split_axis=0, concat_axis=0, tiled=True)  11.3 us
    all_to_all x1, starting transfers between devices, on_device(): lax.all_to_all(reduced, 'dp', split_axis=0, concat_axis=0, tiled=True)  11.1 us
    all_to_all x1, blocking collectives, exchange(): return lax.all_to_all(value, 'hg', 0, 0, tiled=True)  10.6 us
    all_to_all x2, starting transfers between devices, exchange(): return lax.all_to_all(value, 'hg', 0, 0, tiled=True)  8.32 us
    all_to_all x2, waiting for transfers between devices, exchange(): return lax.all_to_all(value, 'hg', 0, 0, tiled=True)  4.61 us
  transfers between devices with their start and end apart: 13, of which 4 were waited for; matrix products, arithmetic and copies ran while one was open for 3% of the time, Pallas kernels for 11%

profile of v5, /device:TPU:1, one launch (start us, length us, event | category | flops | bytes accessed | tf_op | source)
XLA Modules:
  0.0 137.3 jit_solution(17586627444326047603)
XLA Ops:
  0.6 1.8 %broadcast_in_dim.26.earlier_ref = bf16[4,16,3584]{2,1,0:T(8,128)(2,1)} broadcast(bf16[16,3584]{1,0:T(8,128)(2,1)} %bitcast.29), dimensions={1,2} | broadcast | bytes 573440 | tf_op jit(solution)/shard_map/broadcast_in_dim | solution.py:536
  2.4 4.8 %all-to-all-start = ((bf16[4,16,3584]{2,1,0:T(8,128)(2,1)}), bf16[4,16,3584]{2,1,0:T(8,128)(2,1)S(1)}, u32[]{:S(2)}, u32[]{:S(2)}) async-start(bf16[4,16,3584]{2,1,0:T(8,128)(2,1)} %broadcast_in_dim.26.earlier_ref), calls=%async_computation | async-start | bytes 917504 | tf_op jit(solution)/shard_map/all_to_all | solution.py:28
  7.2 2.8 %pack_weights.1 = (bf16[4352,128]{1,0:T(8,128)(2,1)}, bf16[4352,128]{1,0:T(8,128)(2,1)}) custom-call(bf16[3584,256]{1,0:T(8,128)(2,1)} %bitcast.27, bf16[256,3584]{1,0:T(8,128)(2,1)} %bitcast.24, bf16[4,16,3584]{2,1,0:T(8,128)(2,1)} %broadcast_in_dim.26.earlier_ref), custom_call_target="tpu_custom_call" | custom-call | bytes 7340032 | tf_op jit(solution)/shard_map/pack_weights/pallas_call | solution.py:128
  10.1 3.4 %collective-permute-start = (bf16[4352,128]{1,0:T(8,128)(2,1)}, bf16[4352,128]{1,0:T(8,128)(2,1)S(1)}, u32[]{:S(2)}, u32[]{:S(2)}) collective-permute-start(bf16[4352,128]{1,0:T(8,128)(2,1)} %get-tuple-element.20), channel_id=1, source_target_pairs={{0,1},{1,2},{2,3},{3,0},{4,5},{5,6},{6,7},{7,4},{8,9},{9,10},{10,1... | collective-permute-start | bytes 3342344 | tf_op jit(solution)/shard_map/ppermute | solution.py:20
  13.5 3.1 %collective-permute-start.2 = (bf16[4352,128]{1,0:T(8,128)(2,1)}, bf16[4352,128]{1,0:T(8,128)(2,1)S(1)}, u32[]{:S(2)}, u32[]{:S(2)}) collective-permute-start(bf16[4352,128]{1,0:T(8,128)(2,1)} %get-tuple-element.24), channel_id=1, source_target_pairs={{0,3},{1,0},{2,1},{3,2},{4,7},{5,4},{6,5},{7,6},{8,11},{9,8},{10,9... | collective-permute-start | bytes 3342344 | tf_op jit(solution)/shard_map/ppermute | solution.py:20
  18.0 20.7 %all-to-all-start.1 = ((bf16[128,2,896]{2,1,0:T(2,128)(2,1)}), bf16[128,2,896]{2,1,0:T(2,128)(2,1)S(1)}, u32[]{:S(2)}, u32[]{:S(2)}) async-start(bf16[128,2,896]{2,1,0:T(2,128)(2,1)} %get-tuple-element.19), calls=%async_computation.1 | async-start | bytes 917504 | tf_op jit(solution)/shard_map/all_to_all | solution.py:548
  38.7 1.8 %rest_blocks.1 = (bf16[256,512]{1,0:T(8,128)(2,1)}, bf16[256,512]{1,0:T(8,128)(2,1)}) custom-call(bf16[256,3584]{1,0:T(8,128)(2,1)} %bitcast.25, bf16[16,3584]{1,0:T(8,128)(2,1)} %get-tuple-element.21.earlier_ref), custom_call_target="tpu_custom_call" | custom-call | tf_op jit(solution)/shard_map/rest_blocks/pallas_call | solution.py:169
  40.8 2.4 %collective-permute-start.1 = (bf16[1792,128]{1,0:T(8,128)(2,1)S(1)}, bf16[1792,128]{1,0:T(8,128)(2,1)S(1)}, u32[]{:S(2)}, u32[]{:S(2)}) collective-permute-start(bf16[1792,128]{1,0:T(8,128)(2,1)S(1)} %slice.16), channel_id=1, source_target_pairs={{0,1},{1,2},{2,3},{3,0},{4,5},{5,6},{6,7},{7,4},{8,9},{9,10},{10,1... | collective-permute-start | bytes 1376264 | tf_op jit(solution)/shard_map/ppermute | solution.py:20
  43.3 3.1 %collective-permute-start.3 = (bf16[256,512]{1,0:T(8,128)(2,1)}, bf16[256,512]{1,0:T(8,128)(2,1)}, u32[]{:S(2)}, u32[]{:S(2)}) collective-permute-start(bf16[256,512]{1,0:T(8,128)(2,1)} %get-tuple-element.28), channel_id=1, source_target_pairs={{0,1},{1,2},{2,3},{3,0},{4,5},{5,6},{6,7},{7,4},{8,9},{9,10},{10,1... | collective-permute-start | bytes 786440 | tf_op jit(solution)/shard_map/ppermute | solution.py:20
  46.4 3.4 %collective-permute-start.4 = (bf16[256,512]{1,0:T(8,128)(2,1)}, bf16[256,512]{1,0:T(8,128)(2,1)}, u32[]{:S(2)}, u32[]{:S(2)}) collective-permute-start(bf16[256,512]{1,0:T(8,128)(2,1)} %get-tuple-element.29), channel_id=1, source_target_pairs={{0,3},{1,0},{2,1},{3,2},{4,7},{5,4},{6,5},{7,6},{8,11},{9,8},{10,9... | collective-permute-start | bytes 786440 | tf_op jit(solution)/shard_map/ppermute | solution.py:20
  50.8 2.9 %collective-permute-start.5 = (bf16[1792,128]{1,0:T(8,128)(2,1)S(1)}, bf16[1792,128]{1,0:T(8,128)(2,1)}, u32[]{:S(2)}, u32[]{:S(2)}) collective-permute-start(bf16[1792,128]{1,0:T(8,128)(2,1)S(1)} %slice.17), channel_id=1, source_target_pairs={{0,3},{1,0},{2,1},{3,2},{4,7},{5,4},{6,5},{7,6},{8,11},{9,8},{10,9... | collective-permute-start | bytes 1376264 | tf_op jit(solution)/shard_map/ppermute | solution.py:20
  53.7 2.5 %join_up_near.1.joined_hbm = bf16[896,768]{1,0:T(8,128)(2,1)} custom-call(bf16[3584,256]{1,0:T(8,128)(2,1)} %bitcast.28, bf16[4352,128]{1,0:T(8,128)(2,1)} %copy-done.9, bf16[4352,128]{1,0:T(8,128)(2,1)} %copy-done.10), custom_call_target="tpu_custom_call" | custom-call | flops 8999999488 | bytes 2752512 | tf_op jit(solution)/shard_map/join_up_near/pallas_call | solution.py:199
  57.9 11.3 %all-to-all-done.1.rows_ref = bf16[128,2,896]{2,1,0:T(2,128)(2,1)S(1)} async-done(((bf16[128,2,896]{2,1,0:T(2,128)(2,1)}), bf16[128,2,896]{2,1,0:T(2,128)(2,1)S(1)}, u32[]{:S(2)}, u32[]{:S(2)}) %all-to-all-start.1) | async-done | bytes 458784 | tf_op jit(solution)/shard_map/all_to_all | solution.py:548
  70.6 3.5 %all-to-all-start.2 = ((bf16[4,256,256]{2,1,0:T(8,128)(2,1)}), bf16[4,256,256]{2,1,0:T(8,128)(2,1)S(1)}, u32[]{:S(2)}, u32[]{:S(2)}) async-start(bf16[4,256,256]{2,1,0:T(8,128)(2,1)} %expert_up.1), calls=%async_computation.2 | async-start | bytes 1048576 | tf_op jit(solution)/shard_map/all_to_all | solution.py:28
  74.2 2.8 %join_down.1.weights_ref = bf16[1024,896]{1,0:T(8,128)(2,1)} custom-call(bf16[256,3584]{1,0:T(8,128)(2,1)} %bitcast.26, bf16[4352,128]{1,0:T(8,128)(2,1)} %copy-done.9, bf16[4352,128]{1,0:T(8,128)(2,1)} %copy-done.10, bf16[256,512]{1,0:T(8,128)(2,1)} %collective-permute-done.3.after_rest_hbm, bf16[256,512]{1,0:T(8,128)(2,1)} %collective-permute-done.4.before_rest_hbm, ...), custom_call_target="tpu_custom_call" | custom-call | flops 4000000000 | bytes 3670016 | tf_op jit(solution)/shard_map/join_down/pallas_call | solution.py:266
  77.1 4.6 %all-to-all-done.2.shares_ref = bf16[4,256,256]{2,1,0:T(8,128)(2,1)S(1)} async-done(((bf16[4,256,256]{2,1,0:T(8,128)(2,1)}), bf16[4,256,256]{2,1,0:T(8,128)(2,1)S(1)}, u32[]{:S(2)}, u32[]{:S(2)}) %all-to-all-start.2) | async-done | bytes 524320 | tf_op jit(solution)/shard_map/all_to_all | solution.py:28
  82.7 10.6 %all_to_all.25.active_ref = bf16[4,272,256]{2,1,0:T(8,128)(2,1)S(1)} all-to-all(bf16[4,272,256]{2,1,0:T(8,128)(2,1)} %expert_silu.1), channel_id=1, replica_groups=mesh['dp'=128,'hg'=4] {'hg'}, dimensions={0} | all-to-all | bytes 1114112 | tf_op jit(solution)/shard_map/all_to_all | solution.py:28
  94.7 11.1 %all-to-all-start.4 = ((bf16[128,2,896]{2,1,0:T(2,128)(2,1)}), bf16[128,2,896]{2,1,0:T(2,128)(2,1)S(1)}, u32[]{:S(2)}, u32[]{:S(2)}) async-start(bf16[128,2,896]{2,1,0:T(2,128)(2,1)} %expert_down.1), calls=%async_computation.4 | async-start | bytes 917504 | tf_op jit(solution)/shard_map/all_to_all | solution.py:566
  106.5 2.2 %collective-permute-start.6 = (bf16[1,128,576]{1,2,0:T(8,128)(2,1)S(1)}, bf16[1,128,576]{1,2,0:T(8,128)(2,1)S(1)}, u32[]{:S(2)}, u32[]{:S(2)}) collective-permute-start(bf16[1,128,576]{1,2,0:T(8,128)(2,1)S(1)} %copy-done.11), channel_id=1, source_target_pairs={{0,1},{1,2},{2,3},{3,0},{4,5},{5,6},{6,7},{7,4},{8,9},{9,10},{10,1... | collective-permute-start | bytes 442376 | tf_op jit(solution)/shard_map/ppermute | solution.py:20
  108.7 4.3 %collective-permute-start.8 = (bf16[1,128,576]{1,2,0:T(8,128)(2,1)S(1)}, bf16[1,128,576]{1,2,0:T(8,128)(2,1)S(1)}, u32[]{:S(2)}, u32[]{:S(2)}) collective-permute-start(bf16[1,128,576]{1,2,0:T(8,128)(2,1)S(1)} %copy-done.11), channel_id=1, source_target_pairs={{0,3},{1,0},{2,1},{3,2},{4,7},{5,4},{6,5},{7,6},{8,11},{9,8},{10,9... | collective-permute-start | bytes 442376 | tf_op jit(solution)/shard_map/ppermute | solution.py:20
  113.0 1.9 %collective-permute-start.7 = (bf16[1,128,576]{1,2,0:T(8,128)(2,1)S(1)}, bf16[1,128,576]{1,2,0:T(8,128)(2,1)S(1)}, u32[]{:S(2)}, u32[]{:S(2)}) collective-permute-start(bf16[1,128,576]{1,2,0:T(8,128)(2,1)S(1)} %copy-done.11), channel_id=1, source_target_pairs={{0,2},{1,3},{2,0},{3,1},{4,6},{5,7},{6,4},{7,5},{8,10},{9,11},{10,... | collective-permute-start | bytes 442376 | tf_op jit(solution)/shard_map/ppermute | solution.py:20
  115.6 1.8 %gates.1.gates_hbm = bf16[256,16]{1,0:T(8,128)(2,1)} custom-call(bf16[4,16,256]{2,1,0:T(8,128)(2,1)} %slice.19.parts_ref, bf16[256,16]{1,0:T(8,128)(2,1)} %get-tuple-element.33.route_ref), custom_call_target="tpu_custom_call" | custom-call | tf_op jit(solution)/shard_map/gates/pallas_call | solution.py:372
  117.5 3.3 %collective-permute-done.7 = bf16[1,128,576]{1,2,0:T(8,128)(2,1)S(1)} collective-permute-done((bf16[1,128,576]{1,2,0:T(8,128)(2,1)S(1)}, bf16[1,128,576]{1,2,0:T(8,128)(2,1)S(1)}, u32[]{:S(2)}, u32[]{:S(2)}) %collective-permute-start.7) | collective-permute-done | bytes 147488 | tf_op jit(solution)/shard_map/ppermute | solution.py:20
  122.2 14.0 %all-to-all-done.4.returned_ref = bf16[128,2,896]{2,1,0:T(2,128)(2,1)S(1)} async-done(((bf16[128,2,896]{2,1,0:T(2,128)(2,1)}), bf16[128,2,896]{2,1,0:T(2,128)(2,1)S(1)}, u32[]{:S(2)}, u32[]{:S(2)}) %all-to-all-start.4) | async-done | bytes 458784 | tf_op jit(solution)/shard_map/all_to_all | solution.py:566
  (54 shorter events, 11.5 us)
Async XLA Ops:
  0.6 39.9 %copy-start = (bf16[3584,32]{0,1:T(8,128)(2,1)S(1)}, bf16[3584,32]{0,1:T(8,128)(2,1)}, u32[]{:S(2)}) copy-start(bf16[3584,32]{0,1:T(8,128)(2,1)} %param.16) | copy-start | bytes 688132
  2.4 14.2 %all-to-all-start = ((bf16[4,16,3584]{2,1,0:T(8,128)(2,1)}), bf16[4,16,3584]{2,1,0:T(8,128)(2,1)S(1)}, u32[]{:S(2)}, u32[]{:S(2)}) async-start(bf16[4,16,3584]{2,1,0:T(8,128)(2,1)} %broadcast_in_dim.26.earlier_ref), calls=%async_computation | async-start | bytes 917504 | tf_op jit(solution)/shard_map/all_to_all | solution.py:28
  7.2 9.4 %copy-start.4 = (bf16[16,3584]{1,0:T(8,128)(2,1)S(1)}, bf16[16,3584]{1,0:T(8,128)(2,1)}, u32[]{:S(2)}) copy-start(bf16[16,3584]{1,0:T(8,128)(2,1)} %residual_ref.1) | copy-start | bytes 344068
  7.2 9.4 %copy-start.6 = (f32[3584]{0:T(1024)S(1)}, f32[3584]{0:T(1024)}, u32[]{:S(2)}) copy-start(f32[3584]{0:T(1024)} %gain_ref.1) | copy-start | bytes 43012
  7.2 9.4 %copy-start.7 = (s32[16,8]{0,1:T(8,128)S(1)}, s32[16,8]{0,1:T(8,128)}, u32[]{:S(2)}) copy-start(s32[16,8]{0,1:T(8,128)} %param.17) | copy-start | bytes 1540
  10.1 30.7 %collective-permute-start = (bf16[4352,128]{1,0:T(8,128)(2,1)}, bf16[4352,128]{1,0:T(8,128)(2,1)S(1)}, u32[]{:S(2)}, u32[]{:S(2)}) collective-permute-start(bf16[4352,128]{1,0:T(8,128)(2,1)} %get-tuple-element.20), channel_id=1, source_target_pairs={{0,1},{1,2},{2,3},{3,0},{4,5},{5,6},{6,7},{7,4},{8,9},{9,10},{10,1... | collective-permute-start | bytes 3342344 | tf_op jit(solution)/shard_map/ppermute | solution.py:20
  13.5 29.8 %collective-permute-start.2 = (bf16[4352,128]{1,0:T(8,128)(2,1)}, bf16[4352,128]{1,0:T(8,128)(2,1)S(1)}, u32[]{:S(2)}, u32[]{:S(2)}) collective-permute-start(bf16[4352,128]{1,0:T(8,128)(2,1)} %get-tuple-element.24), channel_id=1, source_target_pairs={{0,3},{1,0},{2,1},{3,2},{4,7},{5,4},{6,5},{7,6},{8,11},{9,8},{10,9... | collective-permute-start | bytes 3342344 | tf_op jit(solution)/shard_map/ppermute | solution.py:20
  18.0 22.6 %copy-start.8 = (bf16[16,3584]{1,0:T(8,128)(2,1)S(1)}, bf16[16,3584]{1,0:T(8,128)(2,1)}, u32[]{:S(2)}) copy-start(bf16[16,3584]{1,0:T(8,128)(2,1)} %get-tuple-element.21.earlier_ref) | copy-start | bytes 344068
  18.0 51.2 %all-to-all-start.1 = ((bf16[128,2,896]{2,1,0:T(2,128)(2,1)}), bf16[128,2,896]{2,1,0:T(2,128)(2,1)S(1)}, u32[]{:S(2)}, u32[]{:S(2)}) async-start(bf16[128,2,896]{2,1,0:T(2,128)(2,1)} %get-tuple-element.19), calls=%async_computation.1 | async-start | bytes 917504 | tf_op jit(solution)/shard_map/all_to_all | solution.py:548
  40.8 13.0 %copy-start.9 = (bf16[4352,128]{1,0:T(8,128)(2,1)}, bf16[4352,128]{1,0:T(8,128)(2,1)S(1)}, u32[]{:S(2)}) copy-start(bf16[4352,128]{1,0:T(8,128)(2,1)S(1)} %collective-permute-done.after_hbm) | copy-start | bytes 3342340
  40.8 15.4 %collective-permute-start.1 = (bf16[1792,128]{1,0:T(8,128)(2,1)S(1)}, bf16[1792,128]{1,0:T(8,128)(2,1)S(1)}, u32[]{:S(2)}, u32[]{:S(2)}) collective-permute-start(bf16[1792,128]{1,0:T(8,128)(2,1)S(1)} %slice.16), channel_id=1, source_target_pairs={{0,1},{1,2},{2,3},{3,0},{4,5},{5,6},{6,7},{7,4},{8,9},{9,10},{10,1... | collective-permute-start | bytes 1376264 | tf_op jit(solution)/shard_map/ppermute | solution.py:20
  43.3 30.9 %collective-permute-start.3 = (bf16[256,512]{1,0:T(8,128)(2,1)}, bf16[256,512]{1,0:T(8,128)(2,1)}, u32[]{:S(2)}, u32[]{:S(2)}) collective-permute-start(bf16[256,512]{1,0:T(8,128)(2,1)} %get-tuple-element.28), channel_id=1, source_target_pairs={{0,1},{1,2},{2,3},{3,0},{4,5},{5,6},{6,7},{7,4},{8,9},{9,10},{10,1... | collective-permute-start | bytes 786440 | tf_op jit(solution)/shard_map/ppermute | solution.py:20
  46.4 27.8 %collective-permute-start.4 = (bf16[256,512]{1,0:T(8,128)(2,1)}, bf16[256,512]{1,0:T(8,128)(2,1)}, u32[]{:S(2)}, u32[]{:S(2)}) collective-permute-start(bf16[256,512]{1,0:T(8,128)(2,1)} %get-tuple-element.29), channel_id=1, source_target_pairs={{0,3},{1,0},{2,1},{3,2},{4,7},{5,4},{6,5},{7,6},{8,11},{9,8},{10,9... | collective-permute-start | bytes 786440 | tf_op jit(solution)/shard_map/ppermute | solution.py:20
  50.8 23.4 %collective-permute-start.5 = (bf16[1792,128]{1,0:T(8,128)(2,1)S(1)}, bf16[1792,128]{1,0:T(8,128)(2,1)}, u32[]{:S(2)}, u32[]{:S(2)}) collective-permute-start(bf16[1792,128]{1,0:T(8,128)(2,1)S(1)} %slice.17), channel_id=1, source_target_pairs={{0,3},{1,0},{2,1},{3,2},{4,7},{5,4},{6,5},{7,6},{8,11},{9,8},{10,9... | collective-permute-start | bytes 1376264 | tf_op jit(solution)/shard_map/ppermute | solution.py:20
  70.6 11.0 %all-to-all-start.2 = ((bf16[4,256,256]{2,1,0:T(8,128)(2,1)}), bf16[4,256,256]{2,1,0:T(8,128)(2,1)S(1)}, u32[]{:S(2)}, u32[]{:S(2)}) async-start(bf16[4,256,256]{2,1,0:T(8,128)(2,1)} %expert_up.1), calls=%async_computation.2 | async-start | bytes 1048576 | tf_op jit(solution)/shard_map/all_to_all | solution.py:28
  77.1 16.2 %copy-start.1 = (bf16[1024,896]{1,0:T(8,128)(2,1)S(1)}, bf16[1024,896]{1,0:T(8,128)(2,1)}, u32[]{:S(2)}) copy-start(bf16[1024,896]{1,0:T(8,128)(2,1)} %join_down.1.weights_ref) | copy-start | bytes 5505028
  93.2 13.2 %copy-start.11 = (bf16[1,128,576]{1,2,0:T(8,128)(2,1)S(1)}, bf16[1,128,576]{1,2,0:T(8,128)(2,1)}, u32[]{:S(2)}) copy-start(bf16[1,128,576]{1,2,0:T(8,128)(2,1)} %param.11) | copy-start | bytes 442372
  94.7 26.1 %copy-start.12 = (bf16[1,32,576]{2,1,0:T(8,128)(2,1)S(1)}, bf16[1,32,576]{2,1,0:T(8,128)(2,1)}, u32[]{:S(2)}) copy-start(bf16[1,32,576]{2,1,0:T(8,128)(2,1)} %param.10) | copy-start | bytes 110596
  94.7 41.6 %all-to-all-start.4 = ((bf16[128,2,896]{2,1,0:T(2,128)(2,1)}), bf16[128,2,896]{2,1,0:T(2,128)(2,1)S(1)}, u32[]{:S(2)}, u32[]{:S(2)}) async-start(bf16[128,2,896]{2,1,0:T(2,128)(2,1)} %expert_down.1), calls=%async_computation.4 | async-start | bytes 917504 | tf_op jit(solution)/shard_map/all_to_all | solution.py:566
  106.5 10.9 %collective-permute-start.6 = (bf16[1,128,576]{1,2,0:T(8,128)(2,1)S(1)}, bf16[1,128,576]{1,2,0:T(8,128)(2,1)S(1)}, u32[]{:S(2)}, u32[]{:S(2)}) collective-permute-start(bf16[1,128,576]{1,2,0:T(8,128)(2,1)S(1)} %copy-done.11), channel_id=1, source_target_pairs={{0,1},{1,2},{2,3},{3,0},{4,5},{5,6},{6,7},{7,4},{8,9},{9,10},{10,1... | collective-permute-start | bytes 442376 | tf_op jit(solution)/shard_map/ppermute | solution.py:20
  108.7 12.0 %collective-permute-start.8 = (bf16[1,128,576]{1,2,0:T(8,128)(2,1)S(1)}, bf16[1,128,576]{1,2,0:T(8,128)(2,1)S(1)}, u32[]{:S(2)}, u32[]{:S(2)}) collective-permute-start(bf16[1,128,576]{1,2,0:T(8,128)(2,1)S(1)} %copy-done.11), channel_id=1, source_target_pairs={{0,3},{1,0},{2,1},{3,2},{4,7},{5,4},{6,5},{7,6},{8,11},{9,8},{10,9... | collective-permute-start | bytes 442376 | tf_op jit(solution)/shard_map/ppermute | solution.py:20
  113.0 7.7 %collective-permute-start.7 = (bf16[1,128,576]{1,2,0:T(8,128)(2,1)S(1)}, bf16[1,128,576]{1,2,0:T(8,128)(2,1)S(1)}, u32[]{:S(2)}, u32[]{:S(2)}) collective-permute-start(bf16[1,128,576]{1,2,0:T(8,128)(2,1)S(1)} %copy-done.11), channel_id=1, source_target_pairs={{0,2},{1,3},{2,0},{3,1},{4,6},{5,7},{6,4},{7,5},{8,10},{9,11},{10,... | collective-permute-start | bytes 442376 | tf_op jit(solution)/shard_map/ppermute | solution.py:20
  115.0 21.3 %copy-start.5 = (f32[16,896]{1,0:T(8,128)S(1)}, f32[16,896]{1,0:T(8,128)}, u32[]{:S(2)}) copy-start(f32[16,896]{1,0:T(8,128)} %get-tuple-element.35.hidden_hbm) | copy-start | bytes 172036
  117.4 18.9 %copy-start.3 = (bf16[256,16]{1,0:T(8,128)(2,1)S(1)}, bf16[256,16]{1,0:T(8,128)(2,1)}, u32[]{:S(2)}) copy-start(bf16[256,16]{1,0:T(8,128)(2,1)} %gates.1.gates_hbm) | copy-start | bytes 24580
  (2 other events, 4.5 us)

commit v6 on v5

--- a/solution.py
+++ b/solution.py
@@ -11,7 +11,7 @@
 NORM_EPS = 1e-06
 VMEM_LIMIT = 16 << 20
 WHOLE_VMEM = 60 << 20
-JOIN_FLOPS = 9 * 10 ** 9
+JOIN_FLOPS = 10 * 10 ** 9
 DOWN_FLOPS = 4 * 10 ** 9
 ORDER = (0, 1, 3, 2)
 
@@ -83,45 +83,51 @@
     part = features // size
     half = units // 2
     chunks = part // 128
-    first = chunks // 2
+    first = chunks // 3
     block = 2 * part
     length = 2 * block + first * units
     assert units == 256 and size == 4 and part % 128 == 0 and block == chunks * units
 
     def kernel(up_hbm, down_hbm, earlier_ref, next_hbm, back_hbm, up_ref, down_ref, far_ref, next_ref, back_ref, sems):
-        ups = start_all(
-            [(up_hbm.at[pl.ds(place(d, size, part), part), :], up_ref.at[i]) for i, d in enumerate((1, 2, 3))], sems
-        )
-        downs = start_all(
-            [
-                (down_hbm.at[:, pl.ds(place(d, size, part), first * 128)], down_ref.at[i])
-                for i, d in enumerate((1, 3))
-            ]
-            + [(down_hbm.at[:, pl.ds(place(2, size, part), part)], far_ref)],
-            sems, 3,
-        )
-
-        def put_up(i, to_ref, at):
-            ups[i].wait()
-            to_ref[at:at + part, :] = up_ref[i, :, :half]
-            to_ref[at + part:at + block, :] = up_ref[i, :, half:]
-
-        def put_down(i, to_ref):
-            downs[i].wait()
-            for k in range(first):
-                at = 2 * block + k * units
-                to_ref[at:at + units, :] = down_ref[i, :, k * 128:(k + 1) * 128]
-
-        put_up(0, next_ref, 0)
-        put_up(1, next_ref, block)
-        put_down(0, next_ref)
-        outs = start_all([(next_ref, next_hbm)], sems, 6)
-        put_up(2, back_ref, 0)
-        put_down(1, back_ref)
-        downs[2].wait()
+        def up_block(i, d):
+            return up_hbm.at[pl.ds(place(d, size, part), part), :], up_ref.at[i]
+
+        def down_part(i, d):
+            return down_hbm.at[:, pl.ds(place(d, size, part), first * 128)], down_ref.at[i]
+
+        far = down_hbm.at[:, pl.ds(place(2, size, part), part)]
+        fetched = start_all(
+            [up_block(0, 1), up_block(1, 2), down_part(0, 1), up_block(2, 3), (far, far_ref), down_part(1, 3)], sems
+        )
+        outs = []
+
+        def send(to_ref, to_hbm, at, length):
+            piece = slice(at, at + length)
+            outs.extend(start_all([(to_ref.at[piece, :], to_hbm.at[piece, :])], sems, 6 + len(outs)))
+
+        for i, to_ref, to_hbm, at in (
+            (0, next_ref, next_hbm, 0), (1, next_ref, next_hbm, block), (3, back_ref, back_hbm, 0)
+        ):
+            fetched[i].wait()
+            block_ref = up_ref.at[min(i, 2)]
+            to_ref[at:at + part, :] = block_ref[:, :half]
+            to_ref[at + part:at + block, :] = block_ref[:, half:]
+            send(to_ref, to_hbm, at, block)
+            if i == 1:
+                fetched[2].wait()
+                for k in range(first):
+                    to = 2 * block + k * units
+                    next_ref[to:to + units, :] = down_ref[0, :, k * 128:(k + 1) * 128]
+                send(next_ref, next_hbm, 2 * block, first * units)
+        fetched[4].wait()
         for k in range(chunks):
             back_ref[block + k * units:block + (k + 1) * units, :] = far_ref[:, k * 128:(k + 1) * 128]
-        outs += start_all([(back_ref, back_hbm)], sems, 7)
+        send(back_ref, back_hbm, block, block)
+        fetched[5].wait()
+        for k in range(first):
+            to = 2 * block + k * units
+            back_ref[to:to + units, :] = down_ref[1, :, k * 128:(k + 1) * 128]
+        send(back_ref, back_hbm, 2 * block, first * units)
         wait_all(outs)
 
     dtype = up_weights.dtype
@@ -136,7 +142,7 @@
             pltpu.VMEM((units, part), dtype),
             pltpu.VMEM((length, 128), dtype),
             pltpu.VMEM((length, 128), dtype),
-            pltpu.SemaphoreType.DMA((8,)),
+            pltpu.SemaphoreType.DMA((12,)),
         ],
         cost_estimate=pl.CostEstimate(
             flops=0, bytes_accessed=8 * features * units, transcendentals=0
@@ -149,7 +155,7 @@
 def rest_blocks(down_weights, earlier, size):
     units, features = down_weights.shape
     part = features // size
-    skip = part // 256 * 128
+    skip = part // 384 * 128
     width = part - skip
 
     def kernel(down_hbm, earlier_ref, next_hbm, back_hbm, ref, sems):
@@ -235,7 +241,7 @@
     units, features = down_weights.shape
     part = features // size
     chunks = part // 128
-    first = chunks // 2
+    first = chunks // 3
     block = 2 * part
 
     def kernel(

time: 138 us -> 138 us (level)
  no operation moved by 1% of the time
where the time goes in v6:
time: 138 us; the launch traced here: 137 us
  starting transfers between devices  67.2 us (49%)
  waiting for transfers between devices  33.2 us (24%)
  Pallas kernels  18.1 us (13%)
  blocking collectives  10.6 us (8%)
  local copies, waits for them, and re-layouts  4.98 us (4%)
  between operations  1.67 us (1%)
    ppermute x9, starting transfers between devices, shift(): lax.ppermute(value, 'hg', [(i, (i + distance) % size) for i in range(size)])  26.7 us
    all_to_all x1, starting transfers between devices, on_device(): lax.all_to_all(outgoing, 'dp', split_axis=0, concat_axis=0, tiled=True)  20.7 us
    all_to_all x1, waiting for transfers between devices, on_device(): lax.all_to_all(reduced, 'dp', split_axis=0, concat_axis=0, tiled=True)  14 us
    all_to_all x1, starting transfers between devices, on_device(): lax.all_to_all(reduced, 'dp', split_axis=0, concat_axis=0, tiled=True)  11.5 us
    all_to_all x1, waiting for transfers between devices, on_device(): lax.all_to_all(outgoing, 'dp', split_axis=0, concat_axis=0, tiled=True)  11.2 us
    all_to_all x1, blocking collectives, exchange(): return lax.all_to_all(value, 'hg', 0, 0, tiled=True)  10.6 us
    all_to_all x2, starting transfers between devices, exchange(): return lax.all_to_all(value, 'hg', 0, 0, tiled=True)  8.32 us
    all_to_all x2, waiting for transfers between devices, exchange(): return lax.all_to_all(value, 'hg', 0, 0, tiled=True)  4.66 us
  transfers between devices with their start and end apart: 13, of which 4 were waited for; matrix products, arithmetic and copies ran while one was open for 3% of the time, Pallas kernels for 11%

profile of v6, /device:TPU:1, one launch (start us, length us, event | category | flops | bytes accessed | tf_op | source)
XLA Modules:
  0.0 137.5 jit_solution(9834317468469330809)
XLA Ops:
  0.6 1.7 %broadcast_in_dim.26.earlier_ref = bf16[4,16,3584]{2,1,0:T(8,128)(2,1)} broadcast(bf16[16,3584]{1,0:T(8,128)(2,1)} %bitcast.29), dimensions={1,2} | broadcast | bytes 573440 | tf_op jit(solution)/shard_map/broadcast_in_dim | solution.py:542
  2.4 4.8 %all-to-all-start = ((bf16[4,16,3584]{2,1,0:T(8,128)(2,1)}), bf16[4,16,3584]{2,1,0:T(8,128)(2,1)S(1)}, u32[]{:S(2)}, u32[]{:S(2)}) async-start(bf16[4,16,3584]{2,1,0:T(8,128)(2,1)} %broadcast_in_dim.26.earlier_ref), calls=%async_computation | async-start | bytes 917504 | tf_op jit(solution)/shard_map/all_to_all | solution.py:28
  7.2 2.6 %pack_weights.1 = (bf16[4096,128]{1,0:T(8,128)(2,1)}, bf16[4096,128]{1,0:T(8,128)(2,1)}) custom-call(bf16[3584,256]{1,0:T(8,128)(2,1)} %bitcast.27, bf16[256,3584]{1,0:T(8,128)(2,1)} %bitcast.24, bf16[4,16,3584]{2,1,0:T(8,128)(2,1)} %broadcast_in_dim.26.earlier_ref), custom_call_target="tpu_custom_call" | custom-call | bytes 7340032 | tf_op jit(solution)/shard_map/pack_weights/pallas_call | solution.py:134
  9.8 3.4 %collective-permute-start = (bf16[4096,128]{1,0:T(8,128)(2,1)}, bf16[4096,128]{1,0:T(8,128)(2,1)S(1)}, u32[]{:S(2)}, u32[]{:S(2)}) collective-permute-start(bf16[4096,128]{1,0:T(8,128)(2,1)} %get-tuple-element.20), channel_id=1, source_target_pairs={{0,1},{1,2},{2,3},{3,0},{4,5},{5,6},{6,7},{7,4},{8,9},{9,10},{10,1... | collective-permute-start | bytes 3145736 | tf_op jit(solution)/shard_map/ppermute | solution.py:20
  13.2 3.1 %collective-permute-start.2 = (bf16[4096,128]{1,0:T(8,128)(2,1)}, bf16[4096,128]{1,0:T(8,128)(2,1)S(1)}, u32[]{:S(2)}, u32[]{:S(2)}) collective-permute-start(bf16[4096,128]{1,0:T(8,128)(2,1)} %get-tuple-element.24), channel_id=1, source_target_pairs={{0,3},{1,0},{2,1},{3,2},{4,7},{5,4},{6,5},{7,6},{8,11},{9,8},{10,9... | collective-permute-start | bytes 3145736 | tf_op jit(solution)/shard_map/ppermute | solution.py:20
  17.7 20.7 %all-to-all-start.1 = ((bf16[128,2,896]{2,1,0:T(2,128)(2,1)}), bf16[128,2,896]{2,1,0:T(2,128)(2,1)S(1)}, u32[]{:S(2)}, u32[]{:S(2)}) async-start(bf16[128,2,896]{2,1,0:T(2,128)(2,1)} %get-tuple-element.19), calls=%async_computation.1 | async-start | bytes 917504 | tf_op jit(solution)/shard_map/all_to_all | solution.py:554
  38.5 1.9 %rest_blocks.1 = (bf16[256,640]{1,0:T(8,128)(2,1)}, bf16[256,640]{1,0:T(8,128)(2,1)}) custom-call(bf16[256,3584]{1,0:T(8,128)(2,1)} %bitcast.25, bf16[16,3584]{1,0:T(8,128)(2,1)} %get-tuple-element.21.earlier_ref), custom_call_target="tpu_custom_call" | custom-call | tf_op jit(solution)/shard_map/rest_blocks/pallas_call | solution.py:175
  40.6 2.4 %collective-permute-start.1 = (bf16[1792,128]{1,0:T(8,128)(2,1)S(1)}, bf16[1792,128]{1,0:T(8,128)(2,1)S(1)}, u32[]{:S(2)}, u32[]{:S(2)}) collective-permute-start(bf16[1792,128]{1,0:T(8,128)(2,1)S(1)} %slice.16), channel_id=1, source_target_pairs={{0,1},{1,2},{2,3},{3,0},{4,5},{5,6},{6,7},{7,4},{8,9},{9,10},{10,1... | collective-permute-start | bytes 1376264 | tf_op jit(solution)/shard_map/ppermute | solution.py:20
  43.1 3.1 %collective-permute-start.3 = (bf16[256,640]{1,0:T(8,128)(2,1)}, bf16[256,640]{1,0:T(8,128)(2,1)}, u32[]{:S(2)}, u32[]{:S(2)}) collective-permute-start(bf16[256,640]{1,0:T(8,128)(2,1)} %get-tuple-element.28), channel_id=1, source_target_pairs={{0,1},{1,2},{2,3},{3,0},{4,5},{5,6},{6,7},{7,4},{8,9},{9,10},{10,1... | collective-permute-start | bytes 983048 | tf_op jit(solution)/shard_map/ppermute | solution.py:20
  46.2 3.4 %collective-permute-start.4 = (bf16[256,640]{1,0:T(8,128)(2,1)}, bf16[256,640]{1,0:T(8,128)(2,1)}, u32[]{:S(2)}, u32[]{:S(2)}) collective-permute-start(bf16[256,640]{1,0:T(8,128)(2,1)} %get-tuple-element.29), channel_id=1, source_target_pairs={{0,3},{1,0},{2,1},{3,2},{4,7},{5,4},{6,5},{7,6},{8,11},{9,8},{10,9... | collective-permute-start | bytes 983048 | tf_op jit(solution)/shard_map/ppermute | solution.py:20
  50.6 2.9 %collective-permute-start.5 = (bf16[1792,128]{1,0:T(8,128)(2,1)S(1)}, bf16[1792,128]{1,0:T(8,128)(2,1)}, u32[]{:S(2)}, u32[]{:S(2)}) collective-permute-start(bf16[1792,128]{1,0:T(8,128)(2,1)S(1)} %slice.17), channel_id=1, source_target_pairs={{0,3},{1,0},{2,1},{3,2},{4,7},{5,4},{6,5},{7,6},{8,11},{9,8},{10,9... | collective-permute-start | bytes 1376264 | tf_op jit(solution)/shard_map/ppermute | solution.py:20
  53.5 2.5 %join_up_near.1.joined_hbm = bf16[896,768]{1,0:T(8,128)(2,1)} custom-call(bf16[3584,256]{1,0:T(8,128)(2,1)} %bitcast.28, bf16[4096,128]{1,0:T(8,128)(2,1)} %copy-done.9, bf16[4096,128]{1,0:T(8,128)(2,1)} %copy-done.10), custom_call_target="tpu_custom_call" | custom-call | flops 10000000000 | bytes 2752512 | tf_op jit(solution)/shard_map/join_up_near/pallas_call | solution.py:205
  57.7 11.2 %all-to-all-done.1.rows_ref = bf16[128,2,896]{2,1,0:T(2,128)(2,1)S(1)} async-done(((bf16[128,2,896]{2,1,0:T(2,128)(2,1)}), bf16[128,2,896]{2,1,0:T(2,128)(2,1)S(1)}, u32[]{:S(2)}, u32[]{:S(2)}) %all-to-all-start.1) | async-done | bytes 458784 | tf_op jit(solution)/shard_map/all_to_all | solution.py:554
  70.4 3.5 %all-to-all-start.2 = ((bf16[4,256,256]{2,1,0:T(8,128)(2,1)}), bf16[4,256,256]{2,1,0:T(8,128)(2,1)S(1)}, u32[]{:S(2)}, u32[]{:S(2)}) async-start(bf16[4,256,256]{2,1,0:T(8,128)(2,1)} %expert_up.1), calls=%async_computation.2 | async-start | bytes 1048576 | tf_op jit(solution)/shard_map/all_to_all | solution.py:28
  74.0 2.8 %join_down.1.weights_ref = bf16[1024,896]{1,0:T(8,128)(2,1)} custom-call(bf16[256,3584]{1,0:T(8,128)(2,1)} %bitcast.26, bf16[4096,128]{1,0:T(8,128)(2,1)} %copy-done.9, bf16[4096,128]{1,0:T(8,128)(2,1)} %copy-done.10, bf16[256,640]{1,0:T(8,128)(2,1)} %collective-permute-done.3.after_rest_hbm, bf16[256,640]{1,0:T(8,128)(2,1)} %collective-permute-done.4.before_rest_hbm, ...), custom_call_target="tpu_custom_call" | custom-call | flops 4000000000 | bytes 3670016 | tf_op jit(solution)/shard_map/join_down/pallas_call | solution.py:272
  76.8 4.7 %all-to-all-done.2.shares_ref = bf16[4,256,256]{2,1,0:T(8,128)(2,1)S(1)} async-done(((bf16[4,256,256]{2,1,0:T(8,128)(2,1)}), bf16[4,256,256]{2,1,0:T(8,128)(2,1)S(1)}, u32[]{:S(2)}, u32[]{:S(2)}) %all-to-all-start.2) | async-done | bytes 524320 | tf_op jit(solution)/shard_map/all_to_all | solution.py:28
  82.4 10.6 %all_to_all.25.active_ref = bf16[4,272,256]{2,1,0:T(8,128)(2,1)S(1)} all-to-all(bf16[4,272,256]{2,1,0:T(8,128)(2,1)} %expert_silu.1), channel_id=1, replica_groups=mesh['dp'=128,'hg'=4] {'hg'}, dimensions={0} | all-to-all | bytes 1114112 | tf_op jit(solution)/shard_map/all_to_all | solution.py:28
  94.5 11.5 %all-to-all-start.4 = ((bf16[128,2,896]{2,1,0:T(2,128)(2,1)}), bf16[128,2,896]{2,1,0:T(2,128)(2,1)S(1)}, u32[]{:S(2)}, u32[]{:S(2)}) async-start(bf16[128,2,896]{2,1,0:T(2,128)(2,1)} %expert_down.1), calls=%async_computation.4 | async-start | bytes 917504 | tf_op jit(solution)/shard_map/all_to_all | solution.py:572
  106.7 2.2 %collective-permute-start.6 = (bf16[1,128,576]{1,2,0:T(8,128)(2,1)S(1)}, bf16[1,128,576]{1,2,0:T(8,128)(2,1)S(1)}, u32[]{:S(2)}, u32[]{:S(2)}) collective-permute-start(bf16[1,128,576]{1,2,0:T(8,128)(2,1)S(1)} %copy-done.11), channel_id=1, source_target_pairs={{0,1},{1,2},{2,3},{3,0},{4,5},{5,6},{6,7},{7,4},{8,9},{9,10},{10,1... | collective-permute-start | bytes 442376 | tf_op jit(solution)/shard_map/ppermute | solution.py:20
  108.9 4.3 %collective-permute-start.8 = (bf16[1,128,576]{1,2,0:T(8,128)(2,1)S(1)}, bf16[1,128,576]{1,2,0:T(8,128)(2,1)S(1)}, u32[]{:S(2)}, u32[]{:S(2)}) collective-permute-start(bf16[1,128,576]{1,2,0:T(8,128)(2,1)S(1)} %copy-done.11), channel_id=1, source_target_pairs={{0,3},{1,0},{2,1},{3,2},{4,7},{5,4},{6,5},{7,6},{8,11},{9,8},{10,9... | collective-permute-start | bytes 442376 | tf_op jit(solution)/shard_map/ppermute | solution.py:20
  113.2 1.9 %collective-permute-start.7 = (bf16[1,128,576]{1,2,0:T(8,128)(2,1)S(1)}, bf16[1,128,576]{1,2,0:T(8,128)(2,1)S(1)}, u32[]{:S(2)}, u32[]{:S(2)}) collective-permute-start(bf16[1,128,576]{1,2,0:T(8,128)(2,1)S(1)} %copy-done.11), channel_id=1, source_target_pairs={{0,2},{1,3},{2,0},{3,1},{4,6},{5,7},{6,4},{7,5},{8,10},{9,11},{10,... | collective-permute-start | bytes 442376 | tf_op jit(solution)/shard_map/ppermute | solution.py:20
  115.8 1.8 %gates.1.gates_hbm = bf16[256,16]{1,0:T(8,128)(2,1)} custom-call(bf16[4,16,256]{2,1,0:T(8,128)(2,1)} %slice.19.parts_ref, bf16[256,16]{1,0:T(8,128)(2,1)} %get-tuple-element.33.route_ref), custom_call_target="tpu_custom_call" | custom-call | tf_op jit(solution)/shard_map/gates/pallas_call | solution.py:378
  117.6 3.3 %collective-permute-done.7 = bf16[1,128,576]{1,2,0:T(8,128)(2,1)S(1)} collective-permute-done((bf16[1,128,576]{1,2,0:T(8,128)(2,1)S(1)}, bf16[1,128,576]{1,2,0:T(8,128)(2,1)S(1)}, u32[]{:S(2)}, u32[]{:S(2)}) %collective-permute-start.7) | collective-permute-done | bytes 147488 | tf_op jit(solution)/shard_map/ppermute | solution.py:20
  122.4 14.0 %all-to-all-done.4.returned_ref = bf16[128,2,896]{2,1,0:T(2,128)(2,1)S(1)} async-done(((bf16[128,2,896]{2,1,0:T(2,128)(2,1)}), bf16[128,2,896]{2,1,0:T(2,128)(2,1)S(1)}, u32[]{:S(2)}, u32[]{:S(2)}) %all-to-all-start.4) | async-done | bytes 458784 | tf_op jit(solution)/shard_map/all_to_all | solution.py:572
  (54 shorter events, 11.5 us)
Async XLA Ops:
  0.6 39.7 %copy-start = (bf16[3584,32]{0,1:T(8,128)(2,1)S(1)}, bf16[3584,32]{0,1:T(8,128)(2,1)}, u32[]{:S(2)}) copy-start(bf16[3584,32]{0,1:T(8,128)(2,1)} %param.16) | copy-start | bytes 688132
  2.4 13.9 %all-to-all-start = ((bf16[4,16,3584]{2,1,0:T(8,128)(2,1)}), bf16[4,16,3584]{2,1,0:T(8,128)(2,1)S(1)}, u32[]{:S(2)}, u32[]{:S(2)}) async-start(bf16[4,16,3584]{2,1,0:T(8,128)(2,1)} %broadcast_in_dim.26.earlier_ref), calls=%async_computation | async-start | bytes 917504 | tf_op jit(solution)/shard_map/all_to_all | solution.py:28
  7.2 9.1 %copy-start.4 = (bf16[16,3584]{1,0:T(8,128)(2,1)S(1)}, bf16[16,3584]{1,0:T(8,128)(2,1)}, u32[]{:S(2)}) copy-start(bf16[16,3584]{1,0:T(8,128)(2,1)} %residual_ref.1) | copy-start | bytes 344068
  7.2 9.1 %copy-start.6 = (f32[3584]{0:T(1024)S(1)}, f32[3584]{0:T(1024)}, u32[]{:S(2)}) copy-start(f32[3584]{0:T(1024)} %gain_ref.1) | copy-start | bytes 43012
  7.2 9.1 %copy-start.7 = (s32[16,8]{0,1:T(8,128)S(1)}, s32[16,8]{0,1:T(8,128)}, u32[]{:S(2)}) copy-start(s32[16,8]{0,1:T(8,128)} %param.17) | copy-start | bytes 1540
  9.8 30.7 %collective-permute-start = (bf16[4096,128]{1,0:T(8,128)(2,1)}, bf16[4096,128]{1,0:T(8,128)(2,1)S(1)}, u32[]{:S(2)}, u32[]{:S(2)}) collective-permute-start(bf16[4096,128]{1,0:T(8,128)(2,1)} %get-tuple-element.20), channel_id=1, source_target_pairs={{0,1},{1,2},{2,3},{3,0},{4,5},{5,6},{6,7},{7,4},{8,9},{9,10},{10,1... | collective-permute-start | bytes 3145736 | tf_op jit(solution)/shard_map/ppermute | solution.py:20
  13.2 29.9 %collective-permute-start.2 = (bf16[4096,128]{1,0:T(8,128)(2,1)}, bf16[4096,128]{1,0:T(8,128)(2,1)S(1)}, u32[]{:S(2)}, u32[]{:S(2)}) collective-permute-start(bf16[4096,128]{1,0:T(8,128)(2,1)} %get-tuple-element.24), channel_id=1, source_target_pairs={{0,3},{1,0},{2,1},{3,2},{4,7},{5,4},{6,5},{7,6},{8,11},{9,8},{10,9... | collective-permute-start | bytes 3145736 | tf_op jit(solution)/shard_map/ppermute | solution.py:20
  17.7 22.7 %copy-start.8 = (bf16[16,3584]{1,0:T(8,128)(2,1)S(1)}, bf16[16,3584]{1,0:T(8,128)(2,1)}, u32[]{:S(2)}) copy-start(bf16[16,3584]{1,0:T(8,128)(2,1)} %get-tuple-element.21.earlier_ref) | copy-start | bytes 344068
  17.7 51.2 %all-to-all-start.1 = ((bf16[128,2,896]{2,1,0:T(2,128)(2,1)}), bf16[128,2,896]{2,1,0:T(2,128)(2,1)S(1)}, u32[]{:S(2)}, u32[]{:S(2)}) async-start(bf16[128,2,896]{2,1,0:T(2,128)(2,1)} %get-tuple-element.19), calls=%async_computation.1 | async-start | bytes 917504 | tf_op jit(solution)/shard_map/all_to_all | solution.py:554
  40.6 13.0 %copy-start.9 = (bf16[4096,128]{1,0:T(8,128)(2,1)}, bf16[4096,128]{1,0:T(8,128)(2,1)S(1)}, u32[]{:S(2)}) copy-start(bf16[4096,128]{1,0:T(8,128)(2,1)S(1)} %collective-permute-done.after_hbm) | copy-start | bytes 3145732
  40.6 15.4 %collective-permute-start.1 = (bf16[1792,128]{1,0:T(8,128)(2,1)S(1)}, bf16[1792,128]{1,0:T(8,128)(2,1)S(1)}, u32[]{:S(2)}, u32[]{:S(2)}) collective-permute-start(bf16[1792,128]{1,0:T(8,128)(2,1)S(1)} %slice.16), channel_id=1, source_target_pairs={{0,1},{1,2},{2,3},{3,0},{4,5},{5,6},{6,7},{7,4},{8,9},{9,10},{10,1... | collective-permute-start | bytes 1376264 | tf_op jit(solution)/shard_map/ppermute | solution.py:20
  43.1 30.9 %collective-permute-start.3 = (bf16[256,640]{1,0:T(8,128)(2,1)}, bf16[256,640]{1,0:T(8,128)(2,1)}, u32[]{:S(2)}, u32[]{:S(2)}) collective-permute-start(bf16[256,640]{1,0:T(8,128)(2,1)} %get-tuple-element.28), channel_id=1, source_target_pairs={{0,1},{1,2},{2,3},{3,0},{4,5},{5,6},{6,7},{7,4},{8,9},{9,10},{10,1... | collective-permute-start | bytes 983048 | tf_op jit(solution)/shard_map/ppermute | solution.py:20
  46.2 27.8 %collective-permute-start.4 = (bf16[256,640]{1,0:T(8,128)(2,1)}, bf16[256,640]{1,0:T(8,128)(2,1)}, u32[]{:S(2)}, u32[]{:S(2)}) collective-permute-start(bf16[256,640]{1,0:T(8,128)(2,1)} %get-tuple-element.29), channel_id=1, source_target_pairs={{0,3},{1,0},{2,1},{3,2},{4,7},{5,4},{6,5},{7,6},{8,11},{9,8},{10,9... | collective-permute-start | bytes 983048 | tf_op jit(solution)/shard_map/ppermute | solution.py:20
  50.6 23.3 %collective-permute-start.5 = (bf16[1792,128]{1,0:T(8,128)(2,1)S(1)}, bf16[1792,128]{1,0:T(8,128)(2,1)}, u32[]{:S(2)}, u32[]{:S(2)}) collective-permute-start(bf16[1792,128]{1,0:T(8,128)(2,1)S(1)} %slice.17), channel_id=1, source_target_pairs={{0,3},{1,0},{2,1},{3,2},{4,7},{5,4},{6,5},{7,6},{8,11},{9,8},{10,9... | collective-permute-start | bytes 1376264 | tf_op jit(solution)/shard_map/ppermute | solution.py:20
  70.4 11.1 %all-to-all-start.2 = ((bf16[4,256,256]{2,1,0:T(8,128)(2,1)}), bf16[4,256,256]{2,1,0:T(8,128)(2,1)S(1)}, u32[]{:S(2)}, u32[]{:S(2)}) async-start(bf16[4,256,256]{2,1,0:T(8,128)(2,1)} %expert_up.1), calls=%async_computation.2 | async-start | bytes 1048576 | tf_op jit(solution)/shard_map/all_to_all | solution.py:28
  76.8 16.2 %copy-start.1 = (bf16[1024,896]{1,0:T(8,128)(2,1)S(1)}, bf16[1024,896]{1,0:T(8,128)(2,1)}, u32[]{:S(2)}) copy-start(bf16[1024,896]{1,0:T(8,128)(2,1)} %join_down.1.weights_ref) | copy-start | bytes 5505028
  93.0 13.7 %copy-start.11 = (bf16[1,128,576]{1,2,0:T(8,128)(2,1)S(1)}, bf16[1,128,576]{1,2,0:T(8,128)(2,1)}, u32[]{:S(2)}) copy-start(bf16[1,128,576]{1,2,0:T(8,128)(2,1)} %param.11) | copy-start | bytes 442372
  94.5 26.5 %copy-start.12 = (bf16[1,32,576]{2,1,0:T(8,128)(2,1)S(1)}, bf16[1,32,576]{2,1,0:T(8,128)(2,1)}, u32[]{:S(2)}) copy-start(bf16[1,32,576]{2,1,0:T(8,128)(2,1)} %param.10) | copy-start | bytes 110596
  94.5 42.0 %copy-start.5 = (f32[16,896]{1,0:T(8,128)S(1)}, f32[16,896]{1,0:T(8,128)}, u32[]{:S(2)}) copy-start(f32[16,896]{1,0:T(8,128)} %get-tuple-element.35.hidden_hbm) | copy-start | bytes 172036
  94.5 42.0 %all-to-all-start.4 = ((bf16[128,2,896]{2,1,0:T(2,128)(2,1)}), bf16[128,2,896]{2,1,0:T(2,128)(2,1)S(1)}, u32[]{:S(2)}, u32[]{:S(2)}) async-start(bf16[128,2,896]{2,1,0:T(2,128)(2,1)} %expert_down.1), calls=%async_computation.4 | async-start | bytes 917504 | tf_op jit(solution)/shard_map/all_to_all | solution.py:572
  106.7 10.9 %collective-permute-start.6 = (bf16[1,128,576]{1,2,0:T(8,128)(2,1)S(1)}, bf16[1,128,576]{1,2,0:T(8,128)(2,1)S(1)}, u32[]{:S(2)}, u32[]{:S(2)}) collective-permute-start(bf16[1,128,576]{1,2,0:T(8,128)(2,1)S(1)} %copy-done.11), channel_id=1, source_target_pairs={{0,1},{1,2},{2,3},{3,0},{4,5},{5,6},{6,7},{7,4},{8,9},{9,10},{10,1... | collective-permute-start | bytes 442376 | tf_op jit(solution)/shard_map/ppermute | solution.py:20
  108.9 12.0 %collective-permute-start.8 = (bf16[1,128,576]{1,2,0:T(8,128)(2,1)S(1)}, bf16[1,128,576]{1,2,0:T(8,128)(2,1)S(1)}, u32[]{:S(2)}, u32[]{:S(2)}) collective-permute-start(bf16[1,128,576]{1,2,0:T(8,128)(2,1)S(1)} %copy-done.11), channel_id=1, source_target_pairs={{0,3},{1,0},{2,1},{3,2},{4,7},{5,4},{6,5},{7,6},{8,11},{9,8},{10,9... | collective-permute-start | bytes 442376 | tf_op jit(solution)/shard_map/ppermute | solution.py:20
  113.2 7.7 %collective-permute-start.7 = (bf16[1,128,576]{1,2,0:T(8,128)(2,1)S(1)}, bf16[1,128,576]{1,2,0:T(8,128)(2,1)S(1)}, u32[]{:S(2)}, u32[]{:S(2)}) collective-permute-start(bf16[1,128,576]{1,2,0:T(8,128)(2,1)S(1)} %copy-done.11), channel_id=1, source_target_pairs={{0,2},{1,3},{2,0},{3,1},{4,6},{5,7},{6,4},{7,5},{8,10},{9,11},{10,... | collective-permute-start | bytes 442376 | tf_op jit(solution)/shard_map/ppermute | solution.py:20
  117.6 18.9 %copy-start.3 = (bf16[256,16]{1,0:T(8,128)(2,1)S(1)}, bf16[256,16]{1,0:T(8,128)(2,1)}, u32[]{:S(2)}) copy-start(bf16[256,16]{1,0:T(8,128)(2,1)} %gates.1.gates_hbm) | copy-start | bytes 24580
  (2 other events, 4.5 us)

commit v7 on v6

--- a/solution.py
+++ b/solution.py
@@ -11,7 +11,7 @@
 NORM_EPS = 1e-06
 VMEM_LIMIT = 16 << 20
 WHOLE_VMEM = 60 << 20
-JOIN_FLOPS = 10 * 10 ** 9
+JOIN_FLOPS = 8 * 10 ** 9
 DOWN_FLOPS = 4 * 10 ** 9
 ORDER = (0, 1, 3, 2)
 
@@ -549,7 +549,8 @@
         exchange(copies), residual, norm_gain, expert_ids.T, experts, capacity
     )
     next_rest, back_rest = rest_blocks(down_proj[0], normed, size)
-    next_rest, back_rest, before = lax.optimization_barrier((next_rest, back_rest, before))
+    up_all = join_up_near(up_proj[0], after, before, size)
+    next_rest, back_rest, up_all = lax.optimization_barrier((next_rest, back_rest, up_all))
     after_rest, before_rest = shift(next_rest, 1, size), shift(back_rest, size - 1, size)
     arrived = lax.all_to_all(outgoing, "dp", split_axis=0, concat_axis=0, tiled=True)
 
@@ -559,7 +560,6 @@
     extra = jnp.pad(
         jnp.concatenate([high, low], axis=1), ((0, 0), (0, unit_count - 2 * high.shape[1]))
     )
-    up_all = join_up_near(up_proj[0], after, before, size)
     up_all = join_up_far(up_all, far_up)
     arrived, up_all = lax.optimization_barrier((arrived, up_all))
     shares = exchange(expert_up(arrived, up_all))

time: 138 us -> 138 us (level)
  waiting for transfers between devices: 33.2 us -> 30.9 us
    ppermute x9, starting transfers between devices: 26.7 us -> 28.2 us  [shift(): lax.ppermute(value, 'hg', [(i, (i + distance) % size) for i in range(size)])]
where the time goes in v7:
time: 138 us; the launch traced here: 137 us
  starting transfers between devices  68.5 us (50%)
  waiting for transfers between devices  30.9 us (22%)
  Pallas kernels  18.1 us (13%)
  blocking collectives  10.6 us (8%)
  local copies, waits for them, and re-layouts  5.74 us (4%)
  between operations  1.66 us (1%)
    ppermute x9, starting transfers between devices, shift(): lax.ppermute(value, 'hg', [(i, (i + distance) % size) for i in range(size)])  28.2 us
    all_to_all x1, starting transfers between devices, on_device(): lax.all_to_all(outgoing, 'dp', split_axis=0, concat_axis=0, tiled=True)  20.6 us
    all_to_all x1, waiting for transfers between devices, on_device(): lax.all_to_all(reduced, 'dp', split_axis=0, concat_axis=0, tiled=True)  14.7 us
    all_to_all x1, starting transfers between devices, on_device(): lax.all_to_all(reduced, 'dp', split_axis=0, concat_axis=0, tiled=True)  11.4 us
    all_to_all x1, blocking collectives, exchange(): return lax.all_to_all(value, 'hg', 0, 0, tiled=True)  10.6 us
    all_to_all x1, waiting for transfers between devices, on_device(): lax.all_to_all(outgoing, 'dp', split_axis=0, concat_axis=0, tiled=True)  9.9 us
    all_to_all x2, starting transfers between devices, exchange(): return lax.all_to_all(value, 'hg', 0, 0, tiled=True)  8.32 us
    all_to_all x2, waiting for transfers between devices, exchange(): return lax.all_to_all(value, 'hg', 0, 0, tiled=True)  3.91 us
  transfers between devices with their start and end apart: 13, of which 4 were waited for; matrix products, arithmetic and copies ran while one was open for 3% of the time, Pallas kernels for 11%

profile of v7, /device:TPU:1, one launch (start us, length us, event | category | flops | bytes accessed | tf_op | source)
XLA Modules:
  0.0 137.2 jit_solution(13926241399369338614)
XLA Ops:
  0.6 1.7 %broadcast_in_dim.26.earlier_ref = bf16[4,16,3584]{2,1,0:T(8,128)(2,1)} broadcast(bf16[16,3584]{1,0:T(8,128)(2,1)} %bitcast.29), dimensions={1,2} | broadcast | bytes 573440 | tf_op jit(solution)/shard_map/broadcast_in_dim | solution.py:542
  2.4 4.8 %all-to-all-start = ((bf16[4,16,3584]{2,1,0:T(8,128)(2,1)}), bf16[4,16,3584]{2,1,0:T(8,128)(2,1)S(1)}, u32[]{:S(2)}, u32[]{:S(2)}) async-start(bf16[4,16,3584]{2,1,0:T(8,128)(2,1)} %broadcast_in_dim.26.earlier_ref), calls=%async_computation | async-start | bytes 917504 | tf_op jit(solution)/shard_map/all_to_all | solution.py:28
  7.2 2.6 %pack_weights.1 = (bf16[4096,128]{1,0:T(8,128)(2,1)}, bf16[4096,128]{1,0:T(8,128)(2,1)}) custom-call(bf16[3584,256]{1,0:T(8,128)(2,1)} %bitcast.27, bf16[256,3584]{1,0:T(8,128)(2,1)} %bitcast.24, bf16[4,16,3584]{2,1,0:T(8,128)(2,1)} %broadcast_in_dim.26.earlier_ref), custom_call_target="tpu_custom_call" | custom-call | bytes 7340032 | tf_op jit(solution)/shard_map/pack_weights/pallas_call | solution.py:134
  9.8 3.4 %collective-permute-start = (bf16[4096,128]{1,0:T(8,128)(2,1)}, bf16[4096,128]{1,0:T(8,128)(2,1)S(1)}, u32[]{:S(2)}, u32[]{:S(2)}) collective-permute-start(bf16[4096,128]{1,0:T(8,128)(2,1)} %get-tuple-element.20), channel_id=1, source_target_pairs={{0,1},{1,2},{2,3},{3,0},{4,5},{5,6},{6,7},{7,4},{8,9},{9,10},{10,1... | collective-permute-start | bytes 3145736 | tf_op jit(solution)/shard_map/ppermute | solution.py:20
  13.2 3.1 %collective-permute-start.2 = (bf16[4096,128]{1,0:T(8,128)(2,1)}, bf16[4096,128]{1,0:T(8,128)(2,1)}, u32[]{:S(2)}, u32[]{:S(2)}) collective-permute-start(bf16[4096,128]{1,0:T(8,128)(2,1)} %get-tuple-element.24), channel_id=1, source_target_pairs={{0,3},{1,0},{2,1},{3,2},{4,7},{5,4},{6,5},{7,6},{8,11},{9,8},{10,9... | collective-permute-start | bytes 3145736 | tf_op jit(solution)/shard_map/ppermute | solution.py:20
  17.7 20.6 %all-to-all-start.1 = ((bf16[128,2,896]{2,1,0:T(2,128)(2,1)}), bf16[128,2,896]{2,1,0:T(2,128)(2,1)S(1)}, u32[]{:S(2)}, u32[]{:S(2)}) async-start(bf16[128,2,896]{2,1,0:T(2,128)(2,1)} %get-tuple-element.19), calls=%async_computation.1 | async-start | bytes 917504 | tf_op jit(solution)/shard_map/all_to_all | solution.py:555
  38.3 1.9 %rest_blocks.1 = (bf16[256,640]{1,0:T(8,128)(2,1)}, bf16[256,640]{1,0:T(8,128)(2,1)}) custom-call(bf16[256,3584]{1,0:T(8,128)(2,1)} %bitcast.25, bf16[16,3584]{1,0:T(8,128)(2,1)} %get-tuple-element.21.earlier_ref), custom_call_target="tpu_custom_call" | custom-call | tf_op jit(solution)/shard_map/rest_blocks/pallas_call | solution.py:175
  40.2 2.4 %collective-permute-start.1 = (bf16[1792,128]{1,0:T(8,128)(2,1)S(1)}, bf16[1792,128]{1,0:T(8,128)(2,1)S(1)}, u32[]{:S(2)}, u32[]{:S(2)}) collective-permute-start(bf16[1792,128]{1,0:T(8,128)(2,1)S(1)} %slice.16), channel_id=1, source_target_pairs={{0,1},{1,2},{2,3},{3,0},{4,5},{5,6},{6,7},{7,4},{8,9},{9,10},{10,1... | collective-permute-start | bytes 1376264 | tf_op jit(solution)/shard_map/ppermute | solution.py:20
  43.8 4.2 %collective-permute-start.5 = (bf16[1792,128]{1,0:T(8,128)(2,1)S(1)}, bf16[1792,128]{1,0:T(8,128)(2,1)S(1)}, u32[]{:S(2)}, u32[]{:S(2)}) collective-permute-start(bf16[1792,128]{1,0:T(8,128)(2,1)S(1)} %slice.17), channel_id=1, source_target_pairs={{0,3},{1,0},{2,1},{3,2},{4,7},{5,4},{6,5},{7,6},{8,11},{9,8},{10,9... | collective-permute-start | bytes 1376264 | tf_op jit(solution)/shard_map/ppermute | solution.py:20
  48.0 2.5 %join_up_near.1.joined_hbm = bf16[896,768]{1,0:T(8,128)(2,1)} custom-call(bf16[3584,256]{1,0:T(8,128)(2,1)} %bitcast.28, bf16[4096,128]{1,0:T(8,128)(2,1)} %copy-done.9, bf16[4096,128]{1,0:T(8,128)(2,1)} %collective-permute-done.2.before_hbm), custom_call_target="tpu_custom_call" | custom-call | flops 8000000000 | bytes 2752512 | tf_op jit(solution)/shard_map/join_up_near/pallas_call | solution.py:205
  50.5 1.9 %collective-permute-start.3 = (bf16[256,640]{1,0:T(8,128)(2,1)}, bf16[256,640]{1,0:T(8,128)(2,1)}, u32[]{:S(2)}, u32[]{:S(2)}) collective-permute-start(bf16[256,640]{1,0:T(8,128)(2,1)} %get-tuple-element.28), channel_id=1, source_target_pairs={{0,1},{1,2},{2,3},{3,0},{4,5},{5,6},{6,7},{7,4},{8,9},{9,10},{10,1... | collective-permute-start | bytes 983048 | tf_op jit(solution)/shard_map/ppermute | solution.py:20
  52.4 4.6 %collective-permute-start.4 = (bf16[256,640]{1,0:T(8,128)(2,1)}, bf16[256,640]{1,0:T(8,128)(2,1)}, u32[]{:S(2)}, u32[]{:S(2)}) collective-permute-start(bf16[256,640]{1,0:T(8,128)(2,1)} %get-tuple-element.29), channel_id=1, source_target_pairs={{0,3},{1,0},{2,1},{3,2},{4,7},{5,4},{6,5},{7,6},{8,11},{9,8},{10,9... | collective-permute-start | bytes 983048 | tf_op jit(solution)/shard_map/ppermute | solution.py:20
  58.9 9.9 %all-to-all-done.1.rows_ref = bf16[128,2,896]{2,1,0:T(2,128)(2,1)S(1)} async-done(((bf16[128,2,896]{2,1,0:T(2,128)(2,1)}), bf16[128,2,896]{2,1,0:T(2,128)(2,1)S(1)}, u32[]{:S(2)}, u32[]{:S(2)}) %all-to-all-start.1) | async-done | bytes 458784 | tf_op jit(solution)/shard_map/all_to_all | solution.py:555
  70.3 3.5 %all-to-all-start.2 = ((bf16[4,256,256]{2,1,0:T(8,128)(2,1)}), bf16[4,256,256]{2,1,0:T(8,128)(2,1)S(1)}, u32[]{:S(2)}, u32[]{:S(2)}) async-start(bf16[4,256,256]{2,1,0:T(8,128)(2,1)} %expert_up.1), calls=%async_computation.2 | async-start | bytes 1048576 | tf_op jit(solution)/shard_map/all_to_all | solution.py:28
  74.6 2.8 %join_down.1.weights_ref = bf16[1024,896]{1,0:T(8,128)(2,1)} custom-call(bf16[256,3584]{1,0:T(8,128)(2,1)} %bitcast.26, bf16[4096,128]{1,0:T(8,128)(2,1)} %copy-done.9, bf16[4096,128]{1,0:T(8,128)(2,1)} %collective-permute-done.2.before_hbm, bf16[256,640]{1,0:T(8,128)(2,1)} %collective-permute-done.3.after_rest_hbm, ...), custom_call_target="tpu_custom_call" | custom-call | flops 4000000000 | bytes 3670016 | tf_op jit(solution)/shard_map/join_down/pallas_call | solution.py:272
  77.4 3.9 %all-to-all-done.2.shares_ref = bf16[4,256,256]{2,1,0:T(8,128)(2,1)S(1)} async-done(((bf16[4,256,256]{2,1,0:T(8,128)(2,1)}), bf16[4,256,256]{2,1,0:T(8,128)(2,1)S(1)}, u32[]{:S(2)}, u32[]{:S(2)}) %all-to-all-start.2) | async-done | bytes 524320 | tf_op jit(solution)/shard_map/all_to_all | solution.py:28
  82.3 10.6 %all_to_all.25.active_ref = bf16[4,272,256]{2,1,0:T(8,128)(2,1)S(1)} all-to-all(bf16[4,272,256]{2,1,0:T(8,128)(2,1)} %expert_silu.1), channel_id=1, replica_groups=mesh['dp'=128,'hg'=4] {'hg'}, dimensions={0} | all-to-all | bytes 1114112 | tf_op jit(solution)/shard_map/all_to_all | solution.py:28
  94.4 11.4 %all-to-all-start.4 = ((bf16[128,2,896]{2,1,0:T(2,128)(2,1)}), bf16[128,2,896]{2,1,0:T(2,128)(2,1)S(1)}, u32[]{:S(2)}, u32[]{:S(2)}) async-start(bf16[128,2,896]{2,1,0:T(2,128)(2,1)} %expert_down.1), calls=%async_computation.4 | async-start | bytes 917504 | tf_op jit(solution)/shard_map/all_to_all | solution.py:572
  106.4 2.2 %collective-permute-start.6 = (bf16[1,128,576]{1,2,0:T(8,128)(2,1)S(1)}, bf16[1,128,576]{1,2,0:T(8,128)(2,1)S(1)}, u32[]{:S(2)}, u32[]{:S(2)}) collective-permute-start(bf16[1,128,576]{1,2,0:T(8,128)(2,1)S(1)} %copy-done.10), channel_id=1, source_target_pairs={{0,1},{1,2},{2,3},{3,0},{4,5},{5,6},{6,7},{7,4},{8,9},{9,10},{10,1... | collective-permute-start | bytes 442376 | tf_op jit(solution)/shard_map/ppermute | solution.py:20
  108.6 3.7 %collective-permute-start.7 = (bf16[1,128,576]{1,2,0:T(8,128)(2,1)S(1)}, bf16[1,128,576]{1,2,0:T(8,128)(2,1)S(1)}, u32[]{:S(2)}, u32[]{:S(2)}) collective-permute-start(bf16[1,128,576]{1,2,0:T(8,128)(2,1)S(1)} %copy-done.10), channel_id=1, source_target_pairs={{0,2},{1,3},{2,0},{3,1},{4,6},{5,7},{6,4},{7,5},{8,10},{9,11},{10,... | collective-permute-start | bytes 442376 | tf_op jit(solution)/shard_map/ppermute | solution.py:20
  112.4 2.7 %collective-permute-start.8 = (bf16[1,128,576]{1,2,0:T(8,128)(2,1)S(1)}, bf16[1,128,576]{1,2,0:T(8,128)(2,1)S(1)}, u32[]{:S(2)}, u32[]{:S(2)}) collective-permute-start(bf16[1,128,576]{1,2,0:T(8,128)(2,1)S(1)} %copy-done.10), channel_id=1, source_target_pairs={{0,3},{1,0},{2,1},{3,2},{4,7},{5,4},{6,5},{7,6},{8,11},{9,8},{10,9... | collective-permute-start | bytes 442376 | tf_op jit(solution)/shard_map/ppermute | solution.py:20
  115.7 1.8 %gates.1.gates_hbm = bf16[256,16]{1,0:T(8,128)(2,1)} custom-call(bf16[4,16,256]{2,1,0:T(8,128)(2,1)} %slice.19.parts_ref, bf16[256,16]{1,0:T(8,128)(2,1)} %get-tuple-element.33.route_ref), custom_call_target="tpu_custom_call" | custom-call | tf_op jit(solution)/shard_map/gates/pallas_call | solution.py:378
  117.6 2.5 %collective-permute-done.8 = bf16[1,128,576]{1,2,0:T(8,128)(2,1)S(1)} collective-permute-done((bf16[1,128,576]{1,2,0:T(8,128)(2,1)S(1)}, bf16[1,128,576]{1,2,0:T(8,128)(2,1)S(1)}, u32[]{:S(2)}, u32[]{:S(2)}) %collective-permute-start.8) | collective-permute-done | bytes 147488 | tf_op jit(solution)/shard_map/ppermute | solution.py:20
  121.5 14.7 %all-to-all-done.4.returned_ref = bf16[128,2,896]{2,1,0:T(2,128)(2,1)S(1)} async-done(((bf16[128,2,896]{2,1,0:T(2,128)(2,1)}), bf16[128,2,896]{2,1,0:T(2,128)(2,1)S(1)}, u32[]{:S(2)}, u32[]{:S(2)}) %all-to-all-start.4) | async-done | bytes 458784 | tf_op jit(solution)/shard_map/all_to_all | solution.py:572
  (54 shorter events, 12.3 us)
Async XLA Ops:
  0.6 56.3 %copy-start = (bf16[3584,32]{0,1:T(8,128)(2,1)S(1)}, bf16[3584,32]{0,1:T(8,128)(2,1)}, u32[]{:S(2)}) copy-start(bf16[3584,32]{0,1:T(8,128)(2,1)} %param.16) | copy-start | bytes 688132
  2.4 13.9 %all-to-all-start = ((bf16[4,16,3584]{2,1,0:T(8,128)(2,1)}), bf16[4,16,3584]{2,1,0:T(8,128)(2,1)S(1)}, u32[]{:S(2)}, u32[]{:S(2)}) async-start(bf16[4,16,3584]{2,1,0:T(8,128)(2,1)} %broadcast_in_dim.26.earlier_ref), calls=%async_computation | async-start | bytes 917504 | tf_op jit(solution)/shard_map/all_to_all | solution.py:28
  7.2 9.1 %copy-start.4 = (bf16[16,3584]{1,0:T(8,128)(2,1)S(1)}, bf16[16,3584]{1,0:T(8,128)(2,1)}, u32[]{:S(2)}) copy-start(bf16[16,3584]{1,0:T(8,128)(2,1)} %residual_ref.1) | copy-start | bytes 344068
  7.2 9.1 %copy-start.6 = (f32[3584]{0:T(1024)S(1)}, f32[3584]{0:T(1024)}, u32[]{:S(2)}) copy-start(f32[3584]{0:T(1024)} %gain_ref.1) | copy-start | bytes 43012
  7.2 9.1 %copy-start.7 = (s32[16,8]{0,1:T(8,128)S(1)}, s32[16,8]{0,1:T(8,128)}, u32[]{:S(2)}) copy-start(s32[16,8]{0,1:T(8,128)} %param.17) | copy-start | bytes 1540
  9.8 30.4 %collective-permute-start = (bf16[4096,128]{1,0:T(8,128)(2,1)}, bf16[4096,128]{1,0:T(8,128)(2,1)S(1)}, u32[]{:S(2)}, u32[]{:S(2)}) collective-permute-start(bf16[4096,128]{1,0:T(8,128)(2,1)} %get-tuple-element.20), channel_id=1, source_target_pairs={{0,1},{1,2},{2,3},{3,0},{4,5},{5,6},{6,7},{7,4},{8,9},{9,10},{10,1... | collective-permute-start | bytes 3145736 | tf_op jit(solution)/shard_map/ppermute | solution.py:20
  13.2 29.5 %collective-permute-start.2 = (bf16[4096,128]{1,0:T(8,128)(2,1)}, bf16[4096,128]{1,0:T(8,128)(2,1)}, u32[]{:S(2)}, u32[]{:S(2)}) collective-permute-start(bf16[4096,128]{1,0:T(8,128)(2,1)} %get-tuple-element.24), channel_id=1, source_target_pairs={{0,3},{1,0},{2,1},{3,2},{4,7},{5,4},{6,5},{7,6},{8,11},{9,8},{10,9... | collective-permute-start | bytes 3145736 | tf_op jit(solution)/shard_map/ppermute | solution.py:20
  17.7 51.0 %all-to-all-start.1 = ((bf16[128,2,896]{2,1,0:T(2,128)(2,1)}), bf16[128,2,896]{2,1,0:T(2,128)(2,1)S(1)}, u32[]{:S(2)}, u32[]{:S(2)}) async-start(bf16[128,2,896]{2,1,0:T(2,128)(2,1)} %get-tuple-element.19), calls=%async_computation.1 | async-start | bytes 917504 | tf_op jit(solution)/shard_map/all_to_all | solution.py:555
  40.2 7.8 %copy-start.9 = (bf16[4096,128]{1,0:T(8,128)(2,1)}, bf16[4096,128]{1,0:T(8,128)(2,1)S(1)}, u32[]{:S(2)}) copy-start(bf16[4096,128]{1,0:T(8,128)(2,1)S(1)} %collective-permute-done.after_hbm) | copy-start | bytes 3145732
  40.2 16.9 %collective-permute-start.1 = (bf16[1792,128]{1,0:T(8,128)(2,1)S(1)}, bf16[1792,128]{1,0:T(8,128)(2,1)S(1)}, u32[]{:S(2)}, u32[]{:S(2)}) collective-permute-start(bf16[1792,128]{1,0:T(8,128)(2,1)S(1)} %slice.16), channel_id=1, source_target_pairs={{0,1},{1,2},{2,3},{3,0},{4,5},{5,6},{6,7},{7,4},{8,9},{9,10},{10,1... | collective-permute-start | bytes 1376264 | tf_op jit(solution)/shard_map/ppermute | solution.py:20
  43.7 13.2 %copy-start.8 = (bf16[16,3584]{1,0:T(8,128)(2,1)S(1)}, bf16[16,3584]{1,0:T(8,128)(2,1)}, u32[]{:S(2)}) copy-start(bf16[16,3584]{1,0:T(8,128)(2,1)} %get-tuple-element.21.earlier_ref) | copy-start | bytes 344068
  43.8 30.1 %collective-permute-start.5 = (bf16[1792,128]{1,0:T(8,128)(2,1)S(1)}, bf16[1792,128]{1,0:T(8,128)(2,1)S(1)}, u32[]{:S(2)}, u32[]{:S(2)}) collective-permute-start(bf16[1792,128]{1,0:T(8,128)(2,1)S(1)} %slice.17), channel_id=1, source_target_pairs={{0,3},{1,0},{2,1},{3,2},{4,7},{5,4},{6,5},{7,6},{8,11},{9,8},{10,9... | collective-permute-start | bytes 1376264 | tf_op jit(solution)/shard_map/ppermute | solution.py:20
  50.5 23.4 %collective-permute-start.3 = (bf16[256,640]{1,0:T(8,128)(2,1)}, bf16[256,640]{1,0:T(8,128)(2,1)}, u32[]{:S(2)}, u32[]{:S(2)}) collective-permute-start(bf16[256,640]{1,0:T(8,128)(2,1)} %get-tuple-element.28), channel_id=1, source_target_pairs={{0,1},{1,2},{2,3},{3,0},{4,5},{5,6},{6,7},{7,4},{8,9},{9,10},{10,1... | collective-permute-start | bytes 983048 | tf_op jit(solution)/shard_map/ppermute | solution.py:20
  52.4 21.4 %collective-permute-start.4 = (bf16[256,640]{1,0:T(8,128)(2,1)}, bf16[256,640]{1,0:T(8,128)(2,1)}, u32[]{:S(2)}, u32[]{:S(2)}) collective-permute-start(bf16[256,640]{1,0:T(8,128)(2,1)} %get-tuple-element.29), channel_id=1, source_target_pairs={{0,3},{1,0},{2,1},{3,2},{4,7},{5,4},{6,5},{7,6},{8,11},{9,8},{10,9... | collective-permute-start | bytes 983048 | tf_op jit(solution)/shard_map/ppermute | solution.py:20
  70.3 11.1 %all-to-all-start.2 = ((bf16[4,256,256]{2,1,0:T(8,128)(2,1)}), bf16[4,256,256]{2,1,0:T(8,128)(2,1)S(1)}, u32[]{:S(2)}, u32[]{:S(2)}) async-start(bf16[4,256,256]{2,1,0:T(8,128)(2,1)} %expert_up.1), calls=%async_computation.2 | async-start | bytes 1048576 | tf_op jit(solution)/shard_map/all_to_all | solution.py:28
  77.4 15.5 %copy-start.1 = (bf16[1024,896]{1,0:T(8,128)(2,1)S(1)}, bf16[1024,896]{1,0:T(8,128)(2,1)}, u32[]{:S(2)}) copy-start(bf16[1024,896]{1,0:T(8,128)(2,1)} %join_down.1.weights_ref) | copy-start | bytes 5505028
  92.9 13.5 %copy-start.10 = (bf16[1,128,576]{1,2,0:T(8,128)(2,1)S(1)}, bf16[1,128,576]{1,2,0:T(8,128)(2,1)}, u32[]{:S(2)}) copy-start(bf16[1,128,576]{1,2,0:T(8,128)(2,1)} %param.11) | copy-start | bytes 442372
  94.3 25.7 %copy-start.11 = (bf16[1,32,576]{2,1,0:T(8,128)(2,1)S(1)}, bf16[1,32,576]{2,1,0:T(8,128)(2,1)}, u32[]{:S(2)}) copy-start(bf16[1,32,576]{2,1,0:T(8,128)(2,1)} %param.10) | copy-start | bytes 110596
  94.4 41.8 %copy-start.5 = (f32[16,896]{1,0:T(8,128)S(1)}, f32[16,896]{1,0:T(8,128)}, u32[]{:S(2)}) copy-start(f32[16,896]{1,0:T(8,128)} %get-tuple-element.35.hidden_hbm) | copy-start | bytes 172036
  94.4 41.8 %all-to-all-start.4 = ((bf16[128,2,896]{2,1,0:T(2,128)(2,1)}), bf16[128,2,896]{2,1,0:T(2,128)(2,1)S(1)}, u32[]{:S(2)}, u32[]{:S(2)}) async-start(bf16[128,2,896]{2,1,0:T(2,128)(2,1)} %expert_down.1), calls=%async_computation.4 | async-start | bytes 917504 | tf_op jit(solution)/shard_map/all_to_all | solution.py:572
  106.4 11.1 %collective-permute-start.6 = (bf16[1,128,576]{1,2,0:T(8,128)(2,1)S(1)}, bf16[1,128,576]{1,2,0:T(8,128)(2,1)S(1)}, u32[]{:S(2)}, u32[]{:S(2)}) collective-permute-start(bf16[1,128,576]{1,2,0:T(8,128)(2,1)S(1)} %copy-done.10), channel_id=1, source_target_pairs={{0,1},{1,2},{2,3},{3,0},{4,5},{5,6},{6,7},{7,4},{8,9},{9,10},{10,1... | collective-permute-start | bytes 442376 | tf_op jit(solution)/shard_map/ppermute | solution.py:20
  108.6 8.9 %collective-permute-start.7 = (bf16[1,128,576]{1,2,0:T(8,128)(2,1)S(1)}, bf16[1,128,576]{1,2,0:T(8,128)(2,1)S(1)}, u32[]{:S(2)}, u32[]{:S(2)}) collective-permute-start(bf16[1,128,576]{1,2,0:T(8,128)(2,1)S(1)} %copy-done.10), channel_id=1, source_target_pairs={{0,2},{1,3},{2,0},{3,1},{4,6},{5,7},{6,4},{7,5},{8,10},{9,11},{10,... | collective-permute-start | bytes 442376 | tf_op jit(solution)/shard_map/ppermute | solution.py:20
  112.4 7.7 %collective-permute-start.8 = (bf16[1,128,576]{1,2,0:T(8,128)(2,1)S(1)}, bf16[1,128,576]{1,2,0:T(8,128)(2,1)S(1)}, u32[]{:S(2)}, u32[]{:S(2)}) collective-permute-start(bf16[1,128,576]{1,2,0:T(8,128)(2,1)S(1)} %copy-done.10), channel_id=1, source_target_pairs={{0,3},{1,0},{2,1},{3,2},{4,7},{5,4},{6,5},{7,6},{8,11},{9,8},{10,9... | collective-permute-start | bytes 442376 | tf_op jit(solution)/shard_map/ppermute | solution.py:20
  117.5 18.7 %copy-start.3 = (bf16[256,16]{1,0:T(8,128)(2,1)S(1)}, bf16[256,16]{1,0:T(8,128)(2,1)}, u32[]{:S(2)}) copy-start(bf16[256,16]{1,0:T(8,128)(2,1)} %gates.1.gates_hbm) | copy-start | bytes 24580
  (2 other events, 2.1 us)
